TPU v7x, 128 devices: a whole 4x4x4 slice. The times are simulated.
128 devices in a mesh: frames: 32 (over z, y, x_hi), rows: 4 (over x_lo, core).
Axes of the slice: x: 4 (x_hi: 2, x_lo: 2; x = x_hi * 2 + x_lo), y: 4, z: 4, core: 2. Of those that a mesh axis runs over, the one named last changes fastest.
Arguments:
- inputs: bfloat16 [256, 16, 64, 256], P('frames', 'rows'), may hold values from -40 to 40
- kernel_one: bfloat16 [3, 3, 3, 256, 256], replicated, may hold values from -0.078125 to 0.078125
- gain_one: float32 [256], replicated, may hold values from 0.1 to 1.9
- offset_one: float32 [256], replicated, may hold values from -3 to 3
- kernel_two: bfloat16 [3, 3, 3, 256, 256], replicated, may hold values from -0.078125 to 0.078125
- gain_two: float32 [256], replicated, may hold values from 0.1 to 1.9
- offset_two: float32 [256], replicated, may hold values from -3 to 3
- bias_two: float32 [256], replicated, may hold values from -3 to 3
Outputs:
- low_band: bfloat16 [128, 8, 32, 256], P('frames', None, 'rows')
- high_bands: bfloat16 [7, 128, 8, 32, 256], P(None, 'frames', 'rows')
All inputs are finite; a program needn't handle non-finite values.
Results may differ from a plain program's by a relative error of at most 0.009.
Values may be sent and summed in bfloat16 or wider, within the bound.
No kernel may reach another device: no remote copies, remote signals or barrier semaphores. Data moves between devices by JAX's collectives and lax.ppermute only.
A program may use at most 192 MiB of HBM per device.

v0:
```python
import jax
import jax.numpy as jnp
from jax import lax
from jax.sharding import PartitionSpec as P

GROUPS = 32


EPS = 1e-06


def shifted(block, axis, distance):
    devices = range(lax.axis_size(axis))
    route = [(i - distance, i) for i in devices if i - distance in devices]
    return lax.ppermute(block, axis, route)


def padded_2(block, sides, width):
    for axis, dim in sides:
        count = lax.axis_size(axis)
        forward = [(i, i + 1) for i in range(count - 1)]
        backward = [(target, source) for source, target in forward]
        low = lax.ppermute(
            lax.slice_in_dim(block, block.shape[dim] - width, None, axis=dim), axis, forward
        )
        high = lax.ppermute(lax.slice_in_dim(block, 0, width, axis=dim), axis, backward)
        block = jnp.concatenate([low, block, high], axis=dim)
    return block


def split_groups(values):
    shape = values.shape
    return values.reshape(shape[:-1] + (GROUPS, shape[-1] // GROUPS))


def norm_stats(values):
    grouped = split_groups(values)
    count_total = float(
        values.shape[0]
        * values.shape[1]
        * values.shape[2]
        * (values.shape[3] // GROUPS)
        * lax.axis_size("frames")
        * lax.axis_size("rows")
    )
    total = lax.psum(jnp.sum(grouped, axis=(0, 1, 2, 4)), ("frames", "rows"))
    mean = total / count_total
    centred = grouped - mean[:, None]
    spread = lax.psum(jnp.sum(centred * centred, axis=(0, 1, 2, 4)), ("frames", "rows"))
    var = spread / count_total
    return (mean, var)


def apply_norm(values, mean, var, gain, offset):
    grouped = split_groups(values)
    normed = ((grouped - mean[:, None]) / jnp.sqrt(var[:, None] + EPS)).reshape(values.shape)
    return jax.nn.silu(normed * gain + offset).astype(jnp.bfloat16)


def conv_valid(padded, kernel):
    frames_out = padded.shape[0] - 2
    rows_out = padded.shape[1] - 2
    columns = padded.shape[2]
    chans = padded.shape[3]
    sided = jnp.pad(padded, ((0, 0), (0, 0), (1, 1), (0, 0)))
    widened = jnp.concatenate(
        [sided[:, :, 0:columns], sided[:, :, 1 : columns + 1], sided[:, :, 2 : columns + 2]], axis=3
    )
    kernel_rows = kernel.reshape(3, 3, 3 * chans, kernel.shape[-1])
    total = jnp.zeros((frames_out * rows_out * columns, kernel.shape[-1]), jnp.float32)
    for lag_time in range(3):
        for lag_row in range(3):
            window = widened[
                lag_time : lag_time + frames_out, lag_row : lag_row + rows_out
            ].reshape(-1, 3 * chans)
            total = total + jnp.dot(
                window, kernel_rows[lag_time, lag_row], preferred_element_type=jnp.float32
            )
    return total.reshape(frames_out, rows_out, columns, -1)


def extend_input(active):
    earlier = shifted(active[-2:], "frames", 1)
    joined = jnp.concatenate([earlier, active], axis=0)
    return padded_2(joined, (("rows", 1),), 1)


def haar_split(field):
    frames_dev, rows_dev, columns, chans = field.shape
    blocks = field.reshape(frames_dev // 2, 2, rows_dev // 2, 2, columns // 2, 2, chans)
    factor = 1.0 / jnp.sqrt(jnp.float32(2.0))
    pieces = [blocks]
    for axis in (1, 2, 3):
        following = []
        for piece in pieces:
            first = jnp.take(piece, 0, axis=axis)
            second = jnp.take(piece, 1, axis=axis)
            following.append((first + second) * factor)
            following.append((first - second) * factor)
        pieces = following
    return (pieces[0], jnp.stack(pieces[1:], 0))


def body(inputs, kernel_one, gain_one, offset_one, kernel_two, gain_two, offset_two, bias_two):
    source = inputs.astype(jnp.float32)
    mean_one, var_one = norm_stats(source)
    act_one = apply_norm(source, mean_one, var_one, gain_one, offset_one)
    hidden = conv_valid(extend_input(act_one), kernel_one).astype(jnp.bfloat16)
    hidden_wide = hidden.astype(jnp.float32)
    mean_two, var_two = norm_stats(hidden_wide)
    act_two = apply_norm(hidden_wide, mean_two, var_two, gain_two, offset_two)
    branch = conv_valid(extend_input(act_two), kernel_two)
    summed = source + branch + bias_two
    low, high = haar_split(summed)
    low_tiles = lax.all_to_all(
        low.astype(jnp.bfloat16), "rows", split_axis=2, concat_axis=1, tiled=True
    )
    return (low_tiles, high.astype(jnp.bfloat16))


def solution(mesh):
    in_specs = (P("frames", "rows", None, None), P(), P(), P(), P(), P(), P(), P())
    out_specs = (P("frames", None, "rows", None), P(None, "frames", "rows", None, None))
    return jax.shard_map(body, mesh=mesh, in_specs=in_specs, out_specs=out_specs, check_vma=False)
```

profile of v0, /device:TPU:1, one launch (start us, length us, event | category | flops | bytes accessed | tf_op | source)
XLA Modules:
  0.0 379.3 jit_solution(13177914496804773397)
XLA Ops:
  0.6 1.5 convert_reduce_fusion
  2.4 68.7 %psum.28 = f32[32]{0:T(128)S(1)} all-reduce(f32[32]{0:T(128)S(1)} %reduce_sum.51), channel_id=1, replica_groups=mesh['frames'=32,'rows'=4] {'frames','rows'}, use_global_device_ids=true, to_apply=%region_2.0 | all-reduce | flops 32 | bytes 256 | tf_op jit(solution)/shard_map/psum | solution.py:46
  71.2 1.6 fusion.29
  73.0 62.6 %psum.29 = f32[32]{0:T(128)S(1)} all-reduce(f32[32]{0:T(128)S(1)} %reduce_sum.54), channel_id=1, replica_groups=mesh['frames'=32,'rows'=4] {'frames','rows'}, use_global_device_ids=true, to_apply=%region_5.6 | all-reduce | flops 32 | bytes 256 | tf_op jit(solution)/shard_map/psum | solution.py:49
  135.8 2.0 multiply_convert_fusion.1
  137.8 3.8 %collective-permute-start = (bf16[2,4,64,256]{3,2,1,0:T(8,128)(2,1)S(1)}, bf16[2,4,64,256]{3,2,1,0:T(8,128)(2,1)S(1)}, u32[]{:S(2)}, u32[]{:S(2)}) collective-permute-start(bf16[2,4,64,256]{3,2,1,0:T(8,128)(2,1)S(1)} %slice.304), channel_id=1, source_target_pairs={{0,4},{4,8},{8,12},{12,16},{16,20},{20,24},{24,28},{28,32},{32,36}... | collective-permute-start | bytes 786440 | tf_op jit(solution)/shard_map/ppermute | solution.py:15
  141.6 5.0 %collective-permute-done = bf16[2,4,64,256]{3,2,1,0:T(8,128)(2,1)S(1)} collective-permute-done((bf16[2,4,64,256]{3,2,1,0:T(8,128)(2,1)S(1)}, bf16[2,4,64,256]{3,2,1,0:T(8,128)(2,1)S(1)}, u32[]{:S(2)}, u32[]{:S(2)}) %collective-permute-start) | collective-permute-done | bytes 262176 | tf_op jit(solution)/shard_map/ppermute | solution.py:15
  146.7 4.0 %collective-permute-start.1 = (bf16[10,1,64,256]{3,2,1,0:T(8,128)(2,1)S(1)}, bf16[10,1,64,256]{3,2,1,0:T(8,128)(2,1)S(1)}, u32[]{:S(2)}, u32[]{:S(2)}) collective-permute-start(bf16[10,1,64,256]{3,2,1,0:T(8,128)(2,1)S(1)} %get-tuple-element.100), channel_id=1, source_target_pairs={{0,1},{1,2},{2,3},{4,5},{5,6},{6,7},{8,9},{9,10},{10,11},{12,13},{... | collective-permute-start | bytes 983048 | tf_op jit(solution)/shard_map/ppermute | solution.py:23
  150.7 2.1 collective-permute-start.2
  152.8 1.9 collective-permute-done.1
  154.7 4.4 %collective-permute-done.2 = bf16[10,1,64,256]{3,2,1,0:T(8,128)(2,1)S(1)} collective-permute-done((bf16[10,1,64,256]{3,2,1,0:T(8,128)(2,1)S(1)}, bf16[10,1,64,256]{3,2,1,0:T(8,128)(2,1)S(1)}, u32[]{:S(2)}, u32[]{:S(2)}) %collective-permute-start.2) | collective-permute-done | bytes 327712 | tf_op jit(solution)/shard_map/ppermute | solution.py:26
  159.1 1.1 fusion.26
  160.2 1.3 fusion.72
  161.6 0.5 pad_maximum_fusion
  162.1 7.4 %fusion.70 = (bf16[8,4,64,768]{3,2,1,0:T(8,128)(2,1)}, bf16[8,4,64,768]{3,2,1,0:T(8,128)(2,1)}, bf16[8,4,64,768]{3,2,1,0:T(8,128)(2,1)}, bf16[8,4,64,768]{3,2,1,...) fusion(bf16[10,6,64,768]{3,2,1,0:T(8,128)(2,1)S(1)} %pad_maximu, ...), kind=kLoop, calls=%fused_computation.136 | loop fusion | bytes 56623104 | tf_op jit(solution)/shard_map/slice | solution.py:73
  169.5 3.1 fusion.47
  172.6 0.9 copy-done.11
  173.5 1.0 fusion.48
  174.5 0.9 copy-done.4
  175.4 1.0 fusion.49
  176.4 0.9 copy-done.2
  177.3 1.0 fusion.50
  178.3 0.9 copy-done
  179.2 1.0 fusion.51
  180.2 1.0 fusion.52
  181.2 1.0 fusion.53
  182.2 1.0 fusion.54
  183.2 0.9 copy-done.9
  184.1 2.9 fusion.74
  187.1 67.5 %psum.30 = f32[32]{0:T(128)S(1)} all-reduce(f32[32]{0:T(128)S(1)} %reduce_sum.72), channel_id=1, replica_groups=mesh['frames'=32,'rows'=4] {'frames','rows'}, use_global_device_ids=true, to_apply=%region_8.9 | all-reduce | flops 32 | bytes 256 | tf_op jit(solution)/shard_map/psum | solution.py:46
  254.8 0.3 multiply_reduce_fusion
  255.3 62.5 %psum.31 = f32[32]{0:T(128)S(1)} all-reduce(f32[32]{0:T(128)S(1)} %reduce_sum.75), channel_id=1, replica_groups=mesh['frames'=32,'rows'=4] {'frames','rows'}, use_global_device_ids=true, to_apply=%region_11.12 | all-reduce | flops 32 | bytes 256 | tf_op jit(solution)/shard_map/psum | solution.py:49
  318.1 0.7 multiply_convert_fusion
  318.8 3.1 collective-permute-start.3
  321.9 4.9 %collective-permute-done.3 = bf16[2,4,64,256]{3,2,1,0:T(8,128)(2,1)S(1)} collective-permute-done((bf16[2,4,64,256]{3,2,1,0:T(8,128)(2,1)S(1)}, bf16[2,4,64,256]{3,2,1,0:T(8,128)(2,1)S(1)}, u32[]{:S(2)}, u32[]{:S(2)}) %collective-permute-start.3) | collective-permute-done | bytes 262176 | tf_op jit(solution)/shard_map/ppermute | solution.py:15
  326.9 4.9 %collective-permute-start.4 = (bf16[10,1,64,256]{3,2,1,0:T(8,128)(2,1)S(1)}, bf16[10,1,64,256]{3,2,1,0:T(8,128)(2,1)S(1)}, u32[]{:S(2)}, u32[]{:S(2)}) collective-permute-start(bf16[10,1,64,256]{3,2,1,0:T(8,128)(2,1)S(1)} %get-tuple-element.98), channel_id=1, source_target_pairs={{0,1},{1,2},{2,3},{4,5},{5,6},{6,7},{8,9},{9,10},{10,11},{12,13},{... | collective-permute-start | bytes 983048 | tf_op jit(solution)/shard_map/ppermute | solution.py:23
  331.7 1.9 collective-permute-start.5
  333.7 2.1 collective-permute-done.4
  335.7 4.4 %collective-permute-done.5 = bf16[10,1,64,256]{3,2,1,0:T(8,128)(2,1)S(1)} collective-permute-done((bf16[10,1,64,256]{3,2,1,0:T(8,128)(2,1)S(1)}, bf16[10,1,64,256]{3,2,1,0:T(8,128)(2,1)S(1)}, u32[]{:S(2)}, u32[]{:S(2)}) %collective-permute-start.5) | collective-permute-done | bytes 327712 | tf_op jit(solution)/shard_map/ppermute | solution.py:26
  340.1 1.1 select_maximum_fusion
  341.3 1.3 fusion.71
  342.6 0.5 pad_maximum_fusion.1
  343.2 7.4 %fusion.69 = (bf16[8,4,64,768]{3,2,1,0:T(8,128)(2,1)}, bf16[8,4,64,768]{3,2,1,0:T(8,128)(2,1)}, bf16[8,4,64,768]{3,2,1,0:T(8,128)(2,1)}, bf16[8,4,64,768]{3,2,1,...) fusion(bf16[10,6,64,768]{3,2,1,0:T(8,128)(2,1)S(1)} %pad_maximu, ...), kind=kLoop, calls=%fused_computation.135 | loop fusion | bytes 56623104 | tf_op jit(solution)/shard_map/slice | solution.py:73
  350.6 3.1 fusion.39
  353.7 0.9 copy-done.12
  354.6 1.0 fusion.40
  355.6 0.9 copy-done.5
  356.5 1.0 fusion.41
  357.5 0.9 copy-done.3
  358.4 1.0 fusion.42
  359.3 0.9 copy-done.1
  360.2 1.0 fusion.43
  361.2 1.0 fusion.44
  362.2 1.0 fusion.45
  363.2 1.0 fusion.46
  364.2 0.9 copy-done.10
  365.1 1.5 fusion.8
  366.6 1.7 fusion.32
  368.3 2.5 reshape.134
  370.8 0.7 fusion.73
  372.4 0.8 copy.34
  373.2 3.3 all-to-all-start
  376.9 1.7 all-to-all-done
  378.6 0.7 copy.35
  (62 shorter events, 2.8 us)
Async XLA Ops:
  137.8 8.8 %collective-permute-start = (bf16[2,4,64,256]{3,2,1,0:T(8,128)(2,1)S(1)}, bf16[2,4,64,256]{3,2,1,0:T(8,128)(2,1)S(1)}, u32[]{:S(2)}, u32[]{:S(2)}) collective-permute-start(bf16[2,4,64,256]{3,2,1,0:T(8,128)(2,1)S(1)} %slice.304), channel_id=1, source_target_pairs={{0,4},{4,8},{8,12},{12,16},{16,20},{20,24},{24,28},{28,32},{32,36}... | collective-permute-start | bytes 786440 | tf_op jit(solution)/shard_map/ppermute | solution.py:15
  146.7 8.0 %collective-permute-start.1 = (bf16[10,1,64,256]{3,2,1,0:T(8,128)(2,1)S(1)}, bf16[10,1,64,256]{3,2,1,0:T(8,128)(2,1)S(1)}, u32[]{:S(2)}, u32[]{:S(2)}) collective-permute-start(bf16[10,1,64,256]{3,2,1,0:T(8,128)(2,1)S(1)} %get-tuple-element.100), channel_id=1, source_target_pairs={{0,1},{1,2},{2,3},{4,5},{5,6},{6,7},{8,9},{9,10},{10,11},{12,13},{... | collective-permute-start | bytes 983048 | tf_op jit(solution)/shard_map/ppermute | solution.py:23
  150.7 8.4 %collective-permute-start.2 = (bf16[10,1,64,256]{3,2,1,0:T(8,128)(2,1)S(1)}, bf16[10,1,64,256]{3,2,1,0:T(8,128)(2,1)S(1)}, u32[]{:S(2)}, u32[]{:S(2)}) collective-permute-start(bf16[10,1,64,256]{3,2,1,0:T(8,128)(2,1)S(1)} %get-tuple-element.101), channel_id=1, source_target_pairs={{1,0},{2,1},{3,2},{5,4},{6,5},{7,6},{9,8},{10,9},{11,10},{13,12},{... | collective-permute-start | bytes 983048 | tf_op jit(solution)/shard_map/ppermute | solution.py:26
  169.5 3.1 copy-start.6
  169.5 4.0 %copy-start.11 = (bf16[3,3,3,256,256]{4,3,2,1,0:T(8,128)(2,1)S(1)}, bf16[3,3,3,256,256]{4,3,2,1,0:T(8,128)(2,1)}, u32[]{:S(2)}) copy-start(bf16[3,3,3,256,256]{4,3,2,1,0:T(8,128)(2,1)} %param.21) | copy-start | bytes 10616836
  173.5 1.9 copy-start.4
  175.4 1.9 copy-start.2
  177.3 1.9 copy-start
  182.2 1.9 copy-start.9
  184.1 134.0 %copy-start.14 = (f32[256]{0:T(256)S(1)}, f32[256]{0:T(256)}, u32[]{:S(2)}) copy-start(f32[256]{0:T(256)} %param.26) | copy-start | bytes 3076
  184.1 134.0 %copy-start.15 = (f32[256]{0:T(256)S(1)}, f32[256]{0:T(256)}, u32[]{:S(2)}) copy-start(f32[256]{0:T(256)} %param.25) | copy-start | bytes 3076
  318.8 8.0 %collective-permute-start.3 = (bf16[2,4,64,256]{3,2,1,0:T(8,128)(2,1)S(1)}, bf16[2,4,64,256]{3,2,1,0:T(8,128)(2,1)S(1)}, u32[]{:S(2)}, u32[]{:S(2)}) collective-permute-start(bf16[2,4,64,256]{3,2,1,0:T(8,128)(2,1)S(1)} %slice.325), channel_id=1, source_target_pairs={{0,4},{4,8},{8,12},{12,16},{16,20},{20,24},{24,28},{28,32},{32,36}... | collective-permute-start | bytes 786440 | tf_op jit(solution)/shard_map/ppermute | solution.py:15
  326.9 8.9 %collective-permute-start.4 = (bf16[10,1,64,256]{3,2,1,0:T(8,128)(2,1)S(1)}, bf16[10,1,64,256]{3,2,1,0:T(8,128)(2,1)S(1)}, u32[]{:S(2)}, u32[]{:S(2)}) collective-permute-start(bf16[10,1,64,256]{3,2,1,0:T(8,128)(2,1)S(1)} %get-tuple-element.98), channel_id=1, source_target_pairs={{0,1},{1,2},{2,3},{4,5},{5,6},{6,7},{8,9},{9,10},{10,11},{12,13},{... | collective-permute-start | bytes 983048 | tf_op jit(solution)/shard_map/ppermute | solution.py:23
  331.7 8.4 %collective-permute-start.5 = (bf16[10,1,64,256]{3,2,1,0:T(8,128)(2,1)S(1)}, bf16[10,1,64,256]{3,2,1,0:T(8,128)(2,1)S(1)}, u32[]{:S(2)}, u32[]{:S(2)}) collective-permute-start(bf16[10,1,64,256]{3,2,1,0:T(8,128)(2,1)S(1)} %get-tuple-element.99), channel_id=1, source_target_pairs={{1,0},{2,1},{3,2},{5,4},{6,5},{7,6},{9,8},{10,9},{11,10},{13,12},{... | collective-permute-start | bytes 983048 | tf_op jit(solution)/shard_map/ppermute | solution.py:26
  350.5 3.1 copy-start.7
  350.6 4.0 %copy-start.12 = (bf16[3,3,3,256,256]{4,3,2,1,0:T(8,128)(2,1)S(1)}, bf16[3,3,3,256,256]{4,3,2,1,0:T(8,128)(2,1)}, u32[]{:S(2)}) copy-start(bf16[3,3,3,256,256]{4,3,2,1,0:T(8,128)(2,1)} %param.24) | copy-start | bytes 10616836
  354.6 1.9 copy-start.5
  356.5 1.9 copy-start.3
  358.4 1.9 copy-start.1
  363.2 1.9 copy-start.10
  365.1 1.5 copy-start.8
  365.1 1.5 copy-start.16
  373.2 5.4 %all-to-all-start = ((bf16[4,2,32,256]{3,1,0,2:T(2,128)(2,1)}), bf16[4,2,32,256]{3,1,0,2:T(2,128)(2,1)S(1)}, u32[]{:S(2)}, u32[]{:S(2)}) async-start(bf16[4,2,32,256]{3,1,0,2:T(2,128)(2,1)} %copy.34), calls=%async_computation | async-start | bytes 262144 | tf_op jit(solution)/shard_map/all_to_all | solution.py:115
  376.9 2.4 copy-start.13
where the time goes:
time: 383 us; the launch traced here: 379 us
  blocking collectives  261 us (68%)
  local copies, waits for them, and re-layouts  32.2 us (8%)
  matrix products  24.4 us (6%)
  waiting for transfers between devices  24.3 us (6%)
  starting transfers between devices  23.1 us (6%)
  other arithmetic  12.7 us (3%)
    psum x2, blocking collectives, norm_stats(): total = lax.psum(jnp.sum(grouped, axis=(0, 1, 2, 4)), ('frames', 'rows'))  136 us
    psum x2, blocking collectives, norm_stats(): lax.psum(jnp.sum(centred * centred, axis=(0, 1, 2, 4)), ('frames', 'rows'))  125 us
    dot_general x18, matrix products, conv_valid(): jnp.dot(window, kernel_rows[lag_time, lag_row], preferred_element_type=jn...  24.4 us
    slice x2, local copies, waits for them, and re-layouts, conv_valid(): widened[lag_time:lag_time + frames_out, lag_row:lag_row + rows_out]  14.7 us
    ppermute x2, waiting for transfers between devices, shifted(): return lax.ppermute(block, axis, route)  9.92 us
    unnamed x34, local copies, waits for them, and re-layouts  8.96 us
    ppermute x2, starting transfers between devices, padded_2(): lax.ppermute(lax.slice_in_dim(block, block.shape[dim] - width, None, axis...  8.86 us
    ppermute x2, waiting for transfers between devices, padded_2(): lax.ppermute(lax.slice_in_dim(block, 0, width, axis=dim), axis, backward)  8.79 us
  transfers between devices with their start and end apart: 7, of which 7 were waited for; matrix products, arithmetic and copies ran while one was open for 0% of the time, Pallas kernels for 0%

commit v1 on v0

v1 whole, which is shorter than its diff:
```python
import functools

import jax
import jax.numpy as jnp
from jax import lax
from jax.experimental import pallas as pl
from jax.experimental.pallas import tpu as pltpu
from jax.sharding import PartitionSpec as P

GROUPS = 32
EPS = 1e-06
VMEM = pl.BlockSpec(memory_space=pltpu.VMEM)
LANES = 128
HIGHEST = lax.Precision.HIGHEST


def exact_dot(left, right):
    return jnp.dot(left, right, precision=HIGHEST, preferred_element_type=jnp.float32)


def group_of_channel(rows, cols, row_is_channel, span, shift):
    row = lax.broadcasted_iota(jnp.int32, (rows, cols), 0)
    col = lax.broadcasted_iota(jnp.int32, (rows, cols), 1)
    channel, lane = (row, col) if row_is_channel else (col, row)
    return jnp.where(channel // span + shift == lane, 1.0, 0.0)


def local_stats(values_ref, out_ref):
    frames, rows, cols, chans = values_ref.shape
    span = chans // GROUPS
    count = float(frames * rows * cols * span)

    def block(index):
        return values_ref[index].astype(jnp.float32).reshape(rows * cols // 8, 8, chans)

    def add_sum(index, total):
        return total + jnp.sum(block(index), axis=0)

    total = lax.fori_loop(0, frames, add_sum, jnp.zeros((8, chans), jnp.float32))
    gather = group_of_channel(chans, LANES, True, span, 0)
    spread = group_of_channel(LANES, chans, False, span, 0)
    means = jnp.sum(exact_dot(total, gather), axis=0, keepdims=True) / count
    means = jnp.broadcast_to(means, (8, LANES))
    centre = exact_dot(means, spread)

    def add_square(index, total):
        away = block(index) - centre
        return total + jnp.sum(away * away, axis=0)

    squares = lax.fori_loop(0, frames, add_square, jnp.zeros((8, chans), jnp.float32))
    gather_high = group_of_channel(chans, LANES, True, span, GROUPS)
    squares = jnp.sum(exact_dot(squares, gather_high), axis=0, keepdims=True)
    out_ref[...] = jnp.broadcast_to(means[0:1] + squares, out_ref.shape)


def norm_terms(stats_ref, gain_ref, chans, count):
    stats = stats_ref[...]
    devices = stats.shape[0]
    average = jnp.sum(stats, axis=0, keepdims=True) / devices
    away = stats - average
    between = jnp.sum(away * away, axis=0, keepdims=True) / devices
    lane = lax.broadcasted_iota(jnp.int32, (1, LANES), 1)
    first = jnp.where(lane < GROUPS, average, 0.0)
    second = jnp.where(lane < GROUPS, between, jnp.where(lane < 2 * GROUPS, average / count, 0.0))
    span = chans // GROUPS
    spread = group_of_channel(LANES, chans, False, span, 0) + group_of_channel(
        LANES, chans, False, span, GROUPS
    )
    mean = exact_dot(jnp.broadcast_to(first, (8, LANES)), spread)[0:1]
    var = exact_dot(jnp.broadcast_to(second, (8, LANES)), spread)[0:1]
    return mean, gain_ref[...] / jnp.sqrt(var + EPS)


def build_windows(
    own_ref, past_ref, near_ref, far_ref, near_past_ref, far_past_ref, mean, scale, offset, wide_ref
):
    frames, rows, cols, chans = own_ref.shape
    frame_place = lax.axis_index("frames")
    row_place = lax.axis_index("rows")
    odd = lax.rem(row_place, 2) == 1
    has_past = frame_place > 0
    has_above = row_place > 0
    has_below = row_place < lax.axis_size("rows") - 1
    column = lax.broadcasted_iota(jnp.int32, (cols, chans), 0)

    def put(frame, row, value, valid):
        value = (value.astype(jnp.float32) - mean) * scale + offset
        value = 0.5 * value * (1.0 + jnp.tanh(0.5 * value))
        if valid is not None:
            value = jnp.where(valid, value, 0.0)
        left = jnp.where(column == 0, 0.0, pltpu.roll(value, 1, 0))
        right = jnp.where(column == cols - 1, 0.0, pltpu.roll(value, cols - 1, 0))
        wide_ref[frame, row, :, 0:chans] = left.astype(jnp.bfloat16)
        wide_ref[frame, row, :, chans : 2 * chans] = value.astype(jnp.bfloat16)
        wide_ref[frame, row, :, 2 * chans :] = right.astype(jnp.bfloat16)

    def edges(frame, near, far, valid):
        above = jnp.logical_and(has_above, valid)
        below = jnp.logical_and(has_below, valid)
        put(frame, 0, jnp.where(odd, near, far), above)
        put(frame, rows + 1, jnp.where(odd, far, near), below)

    def past(frame, carry):
        for row in range(rows):
            put(frame, row + 1, past_ref[frame, row], has_past)
        edges(frame, near_past_ref[frame], far_past_ref[frame], has_past)
        return carry

    def own(frame, carry):
        for row in range(rows):
            put(frame + 2, row + 1, own_ref[frame, row], None)
        edges(frame + 2, near_ref[frame], far_ref[frame], True)
        return carry

    lax.fori_loop(0, 2, past, 0)
    lax.fori_loop(0, frames, own, 0)


def conv_frames(wide_ref, kernel_ref, start, count, rows, cols, chans):
    total = None
    for lag_time in range(3):
        for lag_row in range(3):
            window = wide_ref[pl.ds(start + lag_time, count), lag_row : lag_row + rows]
            term = jnp.dot(
                window.reshape(count * rows * cols, 3 * chans),
                kernel_ref[lag_time, lag_row],
                preferred_element_type=jnp.float32,
            )
            total = term if total is None else total + term
    return total.reshape(count, rows, cols, -1)


def columns_apart(line, pair_ref):
    cols, chans = line.shape
    halves = range(chans // LANES)
    for half in halves:
        pair_ref[half] = line[:, half * LANES : (half + 1) * LANES]
    return (
        jnp.concatenate([pair_ref[half, pl.ds(k, cols // 2, stride=2)] for half in halves], axis=1)
        for k in range(2)
    )


def stats_kernel(values_ref, out_ref):
    local_stats(values_ref, out_ref)


def first_kernel(
    own_ref, past_ref, near_ref, far_ref, near_past_ref, far_past_ref,
    stats_ref, gain_ref, offset_ref, kernel_ref,
    hidden_ref, out_stats_ref, wide_ref,
):
    frames, rows, cols, chans = own_ref.shape
    count = frames * rows * cols * (chans // GROUPS)
    mean, scale = norm_terms(stats_ref, gain_ref, chans, count)
    build_windows(
        own_ref, past_ref, near_ref, far_ref, near_past_ref, far_past_ref,
        mean, scale, offset_ref[...], wide_ref,
    )
    step = 2

    def some(index, carry):
        start = index * step
        conv = conv_frames(wide_ref, kernel_ref, start, step, rows, cols, chans)
        hidden_ref[pl.ds(start, step)] = conv.astype(jnp.bfloat16)
        return carry

    lax.fori_loop(0, frames // step, some, 0)
    local_stats(hidden_ref, out_stats_ref)


def second_kernel(
    own_ref, past_ref, near_ref, far_ref, near_past_ref, far_past_ref,
    stats_ref, gain_ref, offset_ref, kernel_ref, source_ref, bias_ref,
    low_ref, high_ref, wide_ref, pair_ref,
):
    frames, rows, cols, chans = own_ref.shape
    count = frames * rows * cols * (chans // GROUPS)
    mean, scale = norm_terms(stats_ref, gain_ref, chans, count)
    build_windows(
        own_ref, past_ref, near_ref, far_ref, near_past_ref, far_past_ref,
        mean, scale, offset_ref[...], wide_ref,
    )
    factor = 0.5 ** 1.5
    bands = low_ref.shape[0]
    width = cols // 2 // bands

    def some(index, carry):
        start = index * 2
        conv = conv_frames(wide_ref, kernel_ref, start, 2, rows, cols, chans)
        summed = source_ref[pl.ds(start, 2)].astype(jnp.float32) + conv + bias_ref[...]
        for time_band in range(2):
            mixed = summed[0] - summed[1] if time_band else summed[0] + summed[1]
            for pair in range(rows // 2):
                upper, lower = mixed[2 * pair], mixed[2 * pair + 1]
                for row_band in range(2):
                    line = (upper - lower if row_band else upper + lower) * factor
                    even, uneven = columns_apart(line, pair_ref)
                    for col_band in range(2):
                        value = even - uneven if col_band else even + uneven
                        value = value.astype(jnp.bfloat16)
                        band = 4 * time_band + 2 * row_band + col_band
                        if band:
                            high_ref[band - 1, index, pair] = value
                        else:
                            for target in range(bands):
                                low_ref[target, index, pair] = value[
                                    target * width : (target + 1) * width
                                ]
        return carry

    lax.fori_loop(0, frames // 2, some, 0)


def exchange(values):
    frame_count, row_count = lax.axis_size("frames"), lax.axis_size("rows")
    axes = ("frames", "rows")
    odd = lax.rem(lax.axis_index("rows"), 2) == 1
    rows = values.shape[1]
    top, bottom = values[:, 0], values[:, rows - 1]
    near = jnp.where(odd, top, bottom)
    far = jnp.where(odd, bottom, top)

    def place(frame, row):
        return frame * row_count + row

    every = range(frame_count)
    later = range(frame_count - 1)
    near_rows = [(r, r ^ 1) for r in range(row_count) if (r ^ 1) < row_count]
    far_rows = [(r, ((r + 1) ^ 1) - 1) for r in range(1, row_count - 1)]

    def route(frames, shift, pairs):
        return [(place(f, r), place(f + shift, s)) for f in frames for r, s in pairs]

    same = [(r, r) for r in range(row_count)]
    past = lax.ppermute(values[-2:], axes, route(later, 1, same))
    got_near = lax.ppermute(near, axes, route(every, 0, near_rows))
    got_far = lax.ppermute(far, axes, route(every, 0, far_rows))
    got_near_past = lax.ppermute(near[-2:], axes, route(later, 1, near_rows))
    got_far_past = lax.ppermute(far[-2:], axes, route(later, 1, far_rows))
    return past, got_near, got_far, got_near_past, got_far_past


def share(stats):
    return lax.all_to_all(stats, ("frames", "rows"), 0, 0, tiled=True)


def body(inputs, kernel_one, gain_one, offset_one, kernel_two, gain_two, offset_two, bias_two):
    frames, rows, cols, chans = inputs.shape
    devices = lax.axis_size("frames") * lax.axis_size("rows")
    bands = lax.axis_size("rows")
    stats_shape = jax.ShapeDtypeStruct((devices, LANES), jnp.float32)
    wide = pltpu.VMEM((frames + 2, rows + 2, cols, 3 * chans), jnp.bfloat16)
    weights_one = kernel_one.reshape(3, 3, 3 * chans, chans)
    weights_two = kernel_two.reshape(3, 3, 3 * chans, chans)

    stats_one = pl.pallas_call(
        stats_kernel, out_shape=stats_shape, in_specs=[VMEM], out_specs=VMEM,
        compiler_params=pltpu.CompilerParams(vmem_limit_bytes=8 * 2**20),
        name="stats_one",
    )(inputs)
    parts = exchange(inputs)
    stats_one = share(stats_one)
    hidden, stats_two = pl.pallas_call(
        first_kernel,
        out_shape=(jax.ShapeDtypeStruct(inputs.shape, jnp.bfloat16), stats_shape),
        in_specs=[VMEM] * 10, out_specs=(VMEM, VMEM), scratch_shapes=[wide],
        compiler_params=pltpu.CompilerParams(vmem_limit_bytes=32 * 2**20),
        name="conv_one",
    )(inputs, *parts, stats_one, gain_one[None], offset_one[None], weights_one)
    stats_two = share(stats_two)
    parts = exchange(hidden)
    low, high = pl.pallas_call(
        second_kernel,
        out_shape=(
            jax.ShapeDtypeStruct(
                (bands, frames // 2, rows // 2, cols // 2 // bands, chans), jnp.bfloat16
            ),
            jax.ShapeDtypeStruct((7, frames // 2, rows // 2, cols // 2, chans), jnp.bfloat16),
        ),
        in_specs=[VMEM] * 12, out_specs=(VMEM, VMEM),
        scratch_shapes=[wide, pltpu.VMEM((chans // LANES, cols, LANES), jnp.float32)],
        compiler_params=pltpu.CompilerParams(vmem_limit_bytes=32 * 2**20),
        name="conv_two",
    )(
        hidden, *parts, stats_two, gain_two[None], offset_two[None], weights_two, inputs,
        bias_two[None],
    )
    tiles = lax.all_to_all(low, "rows", split_axis=0, concat_axis=0, tiled=True)
    tiles = jnp.transpose(tiles, (1, 0, 2, 3, 4)).reshape(
        frames // 2, bands * (rows // 2), cols // 2 // bands, chans
    )
    return tiles, high


def solution(mesh):
    in_specs = (P("frames", "rows", None, None), P(), P(), P(), P(), P(), P(), P())
    out_specs = (P("frames", None, "rows", None), P(None, "frames", "rows", None, None))
    return jax.shard_map(body, mesh=mesh, in_specs=in_specs, out_specs=out_specs, check_vma=False)
```

time: 383 us -> 103 us (0.27)
  blocking collectives: 261 us -> 41 us
  local copies, waits for them, and re-layouts: 32.2 us -> 6.36 us
  matrix products: 24.4 us -> 0 us
  waiting for transfers between devices: 24.3 us -> 0.03 us
  Pallas kernels: 0 us -> 24.2 us
  other arithmetic: 12.7 us -> 1.18 us
  starting transfers between devices: 23.1 us -> 29 us
    psum x4 -> x0, blocking collectives: 261 us -> none  [the longest x2 136 us: norm_stats(): total = lax.psum(jnp.sum(grouped, axis=(0, 1, 2, 4)), ('frames', 'rows'))]
    all_to_all x0 -> x3, blocking collectives: none -> 41 us  [the longest x2 34.3 us: share(): return lax.all_to_all(stats, ('frames', 'rows'), 0, 0, tiled=True)]
    dot_general x18 -> x0, matrix products: 24.4 us -> none  [conv_valid(): jnp.dot(window, kernel_rows[lag_time, lag_row], preferred_element_type=jn...]
    pallas_call x0 -> x3, Pallas kernels: none -> 24.2 us  [the longest x1 11.5 us: body(): pl.pallas_call(second_kernel, out_shape=(jax.ShapeDtypeStruct((bands, fra...]
    ppermute x6 -> x10, waiting for transfers between devices: 22.7 us -> 0.03 us  [the longest x2 0.01 us: exchange(): got_near = lax.ppermute(near, axes, route(every, 0, near_rows))]
    slice x6, local copies, waits for them, and re-layouts: 17.4 us -> 1.1 us  [the longest x2 1.08 us: exchange(): past = lax.ppermute(values[-2:], axes, route(later, 1, same))]
    ppermute x6 -> x10, starting transfers between devices: 19.8 us -> 29 us  [the longest x2 8.48 us: exchange(): past = lax.ppermute(values[-2:], axes, route(later, 1, same))]
    unnamed x34 -> x18, local copies, waits for them, and re-layouts: 8.96 us -> 4.59 us
  transfers between devices with their start and end apart: 7 -> 10, of which waited for: 7 -> 0; matrix products, arithmetic and copies ran while one was open for 0% -> 1% of each run, Pallas kernels for 0% -> 1%
where the time goes in v1:
time: 103 us
  blocking collectives  41 us (40%)
  starting transfers between devices  29 us (28%)
  Pallas kernels  24.2 us (23%)
  local copies, waits for them, and re-layouts  6.36 us (6%)
  other arithmetic  1.18 us (1%)
    all_to_all x2, blocking collectives, share(): return lax.all_to_all(stats, ('frames', 'rows'), 0, 0, tiled=True)  34.3 us
    pallas_call x1, Pallas kernels, body(): pl.pallas_call(second_kernel, out_shape=(jax.ShapeDtypeStruct((bands, fra...  11.5 us
    pallas_call x1, Pallas kernels, body(): pl.pallas_call(first_kernel, out_shape=(jax.ShapeDtypeStruct(inputs.shape...  11.4 us
    ppermute x2, starting transfers between devices, exchange(): past = lax.ppermute(values[-2:], axes, route(later, 1, same))  8.48 us
    ppermute x2, starting transfers between devices, exchange(): got_far_past = lax.ppermute(far[-2:], axes, route(later, 1, far_rows))  7.44 us
    all_to_all x1, blocking collectives, body(): tiles = lax.all_to_all(low, 'rows', split_axis=0, concat_axis=0, tiled=True)  6.72 us
    ppermute x2, starting transfers between devices, exchange(): got_near_past = lax.ppermute(near[-2:], axes, route(later, 1, near_rows))  6.17 us
    ppermute x2, starting transfers between devices, exchange(): got_far = lax.ppermute(far, axes, route(every, 0, far_rows))  5.86 us
  transfers between devices with their start and end apart: 10, of which 0 were waited for; matrix products, arithmetic and copies ran while one was open for 1% of the time, Pallas kernels for 1%

profile of v1, /device:TPU:1, one launch (start us, length us, event | category | flops | bytes accessed | tf_op | source)
XLA Modules:
  0.0 102.6 jit_solution(12804101465493322338)
XLA Ops:
  0.6 0.0 copy-start.1
  0.6 1.1 %slice.42 = bf16[2,4,64,256]{3,2,1,0:T(8,128)(2,1)S(1)} slice(bf16[8,4,64,256]{3,2,1,0:T(8,128)(2,1)} %source_ref.1), slice={[6:8], [0:4], [0:64], [0:256]} | slice | bytes 524288 | tf_op jit(solution)/shard_map/slice | solution.py:236
  1.7 5.5 %collective-permute-start = (bf16[2,4,64,256]{3,2,1,0:T(8,128)(2,1)S(1)}, bf16[2,4,64,256]{3,2,1,0:T(8,128)(2,1)S(1)}, u32[]{:S(2)}, u32[]{:S(2)}) collective-permute-start(bf16[2,4,64,256]{3,2,1,0:T(8,128)(2,1)S(1)} %slice.42), channel_id=1, source_target_pairs={{0,4},{1,5},{2,6},{3,7},{4,8},{5,9},{6,10},{7,11},{8,12},{9,13},{1... | collective-permute-start | bytes 786440 | tf_op jit(solution)/shard_map/ppermute | solution.py:236
  7.2 1.1 %bitcast_select_fusion = (bf16[8,1,64,256]{3,2,0,1:T(8,128)(2,1)S(1)}, bf16[8,1,64,256]{3,2,0,1:T(8,128)(2,1)S(1)}) fusion(pred[]{:T(512)S(6)} %eq.4, bf16[8,4,64,256]{3,2,1,0:T(8,128)(2,1)} %source_ref.1), kind=kLoop, calls=%fused_computation | loop fusion | flops 262144 | bytes 1048577 | tf_op jit(solution)/shard_map/jit(_where)/select_n | solution.py:222
  8.3 4.0 %collective-permute-start.3 = (bf16[2,64,256]{2,1,0:T(8,128)(2,1)S(1)}, bf16[2,64,256]{2,1,0:T(8,128)(2,1)S(1)}, u32[]{:S(2)}, u32[]{:S(2)}) collective-permute-start(bf16[2,64,256]{2,1,0:T(8,128)(2,1)S(1)} %slice_bitcast_fusion.3), channel_id=1, source_target_pairs={{0,5},{1,4},{2,7},{3,6},{4,9},{5,8},{6,11},{7,10},{8,13},{9,12},{1... | collective-permute-start | bytes 196616 | tf_op jit(solution)/shard_map/ppermute | solution.py:239
  12.3 0.1 collective-permute-start.1
  12.4 3.5 %collective-permute-start.2 = (bf16[8,64,256]{2,1,0:T(8,128)(2,1)S(1)}, bf16[8,64,256]{2,1,0:T(8,128)(2,1)S(1)}, u32[]{:S(2)}, u32[]{:S(2)}) collective-permute-start(bf16[8,64,256]{2,1,0:T(8,128)(2,1)S(1)} %bitcast.49), channel_id=1, source_target_pairs={{1,2},{2,1},{5,6},{6,5},{9,10},{10,9},{13,14},{14,13},{17,18},{18,... | collective-permute-start | bytes 786440 | tf_op jit(solution)/shard_map/ppermute | solution.py:238
  15.9 3.6 %collective-permute-start.4 = (bf16[2,64,256]{2,1,0:T(8,128)(2,1)S(1)}, bf16[2,64,256]{2,1,0:T(8,128)(2,1)S(1)}, u32[]{:S(2)}, u32[]{:S(2)}) collective-permute-start(bf16[2,64,256]{2,1,0:T(8,128)(2,1)S(1)} %slice_bitcast_fusion.2), channel_id=1, source_target_pairs={{1,6},{2,5},{5,10},{6,9},{9,14},{10,13},{13,18},{14,17},{17,22},{1... | collective-permute-start | bytes 196616 | tf_op jit(solution)/shard_map/ppermute | solution.py:240
  19.5 0.0 copy-start
  19.5 1.2 %copy-done = bf16[8,4,64,256]{3,2,1,0:T(8,128)(2,1)S(1)} copy-done((bf16[8,4,64,256]{3,2,1,0:T(8,128)(2,1)S(1)}, bf16[8,4,64,256]{3,2,1,0:T(8,128)(2,1)}, u32[]{:S(2)}) %copy-start) | copy-done | bytes 1048600
  20.8 1.2 %stats_one.1 = f32[128,128]{1,0:T(8,128)S(1)} custom-call(bf16[8,4,64,256]{3,2,1,0:T(8,128)(2,1)S(1)} %copy-done), custom_call_target="tpu_custom_call" | custom-call | tf_op jit(solution)/shard_map/stats_one/pallas_call | solution.py:257
  22.0 18.4 %all_to_all.27 = f32[128,1,128]{2,1,0:T(1,128)S(1)} all-to-all(f32[128,1,128]{2,1,0:T(1,128)S(1)} %bitcast.38), channel_id=1, replica_groups=mesh['frames'=32,'rows'=4] {'frames','rows'}, dimensions={0} | all-to-all | bytes 131072 | tf_op jit(solution)/shard_map/all_to_all | solution.py:245
  40.4 0.0 collective-permute-done.3.near_past_ref
  40.4 0.0 collective-permute-done.4.far_past_ref
  40.4 0.0 collective-permute-done.past_ref
  40.4 0.0 collective-permute-done.1.near_ref
  40.4 0.0 collective-permute-done.2.far_ref
  40.4 0.0 copy-done.1
  40.4 0.0 copy-start.2
  40.4 2.0 %copy-done.2 = bf16[3,3,3,256,256]{4,3,2,1,0:T(8,128)(2,1)S(1)} copy-done((bf16[3,3,3,256,256]{4,3,2,1,0:T(8,128)(2,1)S(1)}, bf16[3,3,3,256,256]{4,3,2,1,0:T(8,128)(2,1)}, u32[]{:S(2)}) %copy-start.2) | copy-done | bytes 3538968
  42.4 0.0 copy-start.4
  42.4 0.7 copy-done.4
  43.1 0.0 copy-start.5
  43.1 0.7 copy-done.5
  43.8 0.0 copy-start.3
  43.8 0.0 copy-start.6
  43.8 0.0 copy-start.7
  43.8 0.0 copy-start.8
  43.8 11.4 %conv_one.1 = (bf16[8,4,64,256]{3,2,1,0:T(8,128)(2,1)S(1)}, f32[128,128]{1,0:T(8,128)S(1)}) custom-call(bf16[8,4,64,256]{3,2,1,0:T(8,128)(2,1)S(1)} %copy-done.1, bf16[2,4,64,256]{3,2,1,0:T(8,128)(2,1)S(1)} %collective-permute-done.past_ref, bf16[8,64,256]{2,1,0:T(8,128)(2,1)S(1)} %collective-permute-done.1.near_ref, ...), custom_call_target="tpu_custom_call" | custom-call | tf_op jit(solution)/shard_map/conv_one/pallas_call | solution.py:264
  55.2 0.1 broadcast_select_fusion
  55.4 3.0 %collective-permute-start.5 = (bf16[2,4,64,256]{3,2,1,0:T(8,128)(2,1)S(1)}, bf16[2,4,64,256]{3,2,1,0:T(8,128)(2,1)S(1)}, u32[]{:S(2)}, u32[]{:S(2)}) collective-permute-start(bf16[2,4,64,256]{3,2,1,0:T(8,128)(2,1)S(1)} %slice.49), channel_id=1, source_target_pairs={{0,4},{1,5},{2,6},{3,7},{4,8},{5,9},{6,10},{7,11},{8,12},{9,13},{1... | collective-permute-start | bytes 786440 | tf_op jit(solution)/shard_map/ppermute | solution.py:236
  58.4 1.0 collective-permute-start.6
  59.3 2.4 %collective-permute-start.7 = (bf16[8,64,256]{2,1,0:T(8,128)(2,1)S(1)}, bf16[8,64,256]{2,1,0:T(8,128)(2,1)S(1)}, u32[]{:S(2)}, u32[]{:S(2)}) collective-permute-start(bf16[8,64,256]{2,1,0:T(8,128)(2,1)S(1)} %bitcast.47), channel_id=1, source_target_pairs={{1,2},{2,1},{5,6},{6,5},{9,10},{10,9},{13,14},{14,13},{17,18},{18,... | collective-permute-start | bytes 786440 | tf_op jit(solution)/shard_map/ppermute | solution.py:238
  61.7 2.2 %collective-permute-start.8 = (bf16[2,64,256]{2,1,0:T(8,128)(2,1)S(1)}, bf16[2,64,256]{2,1,0:T(8,128)(2,1)S(1)}, u32[]{:S(2)}, u32[]{:S(2)}) collective-permute-start(bf16[2,64,256]{2,1,0:T(8,128)(2,1)S(1)} %slice_bitcast_fusion.1), channel_id=1, source_target_pairs={{0,5},{1,4},{2,7},{3,6},{4,9},{5,8},{6,11},{7,10},{8,13},{9,12},{1... | collective-permute-start | bytes 196616 | tf_op jit(solution)/shard_map/ppermute | solution.py:239
  63.9 3.8 %collective-permute-start.9 = (bf16[2,64,256]{2,1,0:T(8,128)(2,1)S(1)}, bf16[2,64,256]{2,1,0:T(8,128)(2,1)S(1)}, u32[]{:S(2)}, u32[]{:S(2)}) collective-permute-start(bf16[2,64,256]{2,1,0:T(8,128)(2,1)S(1)} %slice_bitcast_fusion), channel_id=1, source_target_pairs={{1,6},{2,5},{5,10},{6,9},{9,14},{10,13},{13,18},{14,17},{17,22},{1... | collective-permute-start | bytes 196616 | tf_op jit(solution)/shard_map/ppermute | solution.py:240
  67.7 15.9 %all_to_all.28 = f32[128,1,128]{2,1,0:T(1,128)S(1)} all-to-all(f32[128,1,128]{2,1,0:T(1,128)S(1)} %bitcast.40), channel_id=1, replica_groups=mesh['frames'=32,'rows'=4] {'frames','rows'}, dimensions={0} | all-to-all | bytes 131072 | tf_op jit(solution)/shard_map/all_to_all | solution.py:245
  83.6 0.0 collective-permute-done.8.near_past_ref
  83.6 0.0 collective-permute-done.9.far_past_ref
  83.7 0.0 collective-permute-done.5.past_ref
  83.7 0.0 collective-permute-done.6.near_ref
  83.7 0.0 collective-permute-done.7.far_ref
  83.7 0.0 copy-done.3
  83.7 0.0 copy-done.6
  83.7 0.0 copy-done.7
  83.7 0.0 copy-done.8
  83.7 11.5 %conv_two.1 = (bf16[4,4,2,8,256]{4,3,2,1,0:T(8,128)(2,1)S(1)}, bf16[7,4,2,32,256]{4,3,2,1,0:T(8,128)(2,1)}) custom-call(bf16[8,4,64,256]{3,2,1,0:T(8,128)(2,1)S(1)} %get-tuple-element.6.own_ref, bf16[2,4,64,256]{3,2,1,0:T(8,128)(2,1)S(1)} %collective-permute-done.5.past_ref, bf16[8,64,256]{2,1,0:T(8,128)(2,1)S(1)} %collective-permute-done.6.near_ref, ...), custom_call_target="tpu_custom_call" | custom-call | tf_op jit(solution)/shard_map/conv_two/pallas_call | solution.py:273
  95.3 6.7 %all_to_all.29 = bf16[4,4,2,8,256]{4,3,2,1,0:T(8,128)(2,1)S(1)} all-to-all(bf16[4,4,2,8,256]{4,3,2,1,0:T(8,128)(2,1)S(1)} %get-tuple-element.8), channel_id=1, replica_groups=mesh['frames'=32,'rows'=4] {'rows'}, dimensions={0} | all-to-all | bytes 262144 | tf_op jit(solution)/shard_map/all_to_all | solution.py:289
  102.0 0.7 copy.25
  (5 shorter events, 0.0 us)
Async XLA Ops:
  0.6 39.8 %copy-start.1 = (bf16[8,4,64,256]{3,2,1,0:T(8,128)(2,1)S(1)}, bf16[8,4,64,256]{3,2,1,0:T(8,128)(2,1)}, u32[]{:S(2)}) copy-start(bf16[8,4,64,256]{3,2,1,0:T(8,128)(2,1)} %source_ref.1) | copy-start | bytes 3145732
  1.7 38.7 %collective-permute-start = (bf16[2,4,64,256]{3,2,1,0:T(8,128)(2,1)S(1)}, bf16[2,4,64,256]{3,2,1,0:T(8,128)(2,1)S(1)}, u32[]{:S(2)}, u32[]{:S(2)}) collective-permute-start(bf16[2,4,64,256]{3,2,1,0:T(8,128)(2,1)S(1)} %slice.42), channel_id=1, source_target_pairs={{0,4},{1,5},{2,6},{3,7},{4,8},{5,9},{6,10},{7,11},{8,12},{9,13},{1... | collective-permute-start | bytes 786440 | tf_op jit(solution)/shard_map/ppermute | solution.py:236
  8.3 32.1 %collective-permute-start.3 = (bf16[2,64,256]{2,1,0:T(8,128)(2,1)S(1)}, bf16[2,64,256]{2,1,0:T(8,128)(2,1)S(1)}, u32[]{:S(2)}, u32[]{:S(2)}) collective-permute-start(bf16[2,64,256]{2,1,0:T(8,128)(2,1)S(1)} %slice_bitcast_fusion.3), channel_id=1, source_target_pairs={{0,5},{1,4},{2,7},{3,6},{4,9},{5,8},{6,11},{7,10},{8,13},{9,12},{1... | collective-permute-start | bytes 196616 | tf_op jit(solution)/shard_map/ppermute | solution.py:239
  12.3 28.1 %collective-permute-start.1 = (bf16[8,64,256]{2,1,0:T(8,128)(2,1)S(1)}, bf16[8,64,256]{2,1,0:T(8,128)(2,1)S(1)}, u32[]{:S(2)}, u32[]{:S(2)}) collective-permute-start(bf16[8,64,256]{2,1,0:T(8,128)(2,1)S(1)} %bitcast.50), channel_id=1, source_target_pairs={{0,1},{1,0},{2,3},{3,2},{4,5},{5,4},{6,7},{7,6},{8,9},{9,8},{10,11... | collective-permute-start | bytes 786440 | tf_op jit(solution)/shard_map/ppermute | solution.py:237
  12.4 28.0 %collective-permute-start.2 = (bf16[8,64,256]{2,1,0:T(8,128)(2,1)S(1)}, bf16[8,64,256]{2,1,0:T(8,128)(2,1)S(1)}, u32[]{:S(2)}, u32[]{:S(2)}) collective-permute-start(bf16[8,64,256]{2,1,0:T(8,128)(2,1)S(1)} %bitcast.49), channel_id=1, source_target_pairs={{1,2},{2,1},{5,6},{6,5},{9,10},{10,9},{13,14},{14,13},{17,18},{18,... | collective-permute-start | bytes 786440 | tf_op jit(solution)/shard_map/ppermute | solution.py:238
  15.9 24.5 %collective-permute-start.4 = (bf16[2,64,256]{2,1,0:T(8,128)(2,1)S(1)}, bf16[2,64,256]{2,1,0:T(8,128)(2,1)S(1)}, u32[]{:S(2)}, u32[]{:S(2)}) collective-permute-start(bf16[2,64,256]{2,1,0:T(8,128)(2,1)S(1)} %slice_bitcast_fusion.2), channel_id=1, source_target_pairs={{1,6},{2,5},{5,10},{6,9},{9,14},{10,13},{13,18},{14,17},{17,22},{1... | collective-permute-start | bytes 196616 | tf_op jit(solution)/shard_map/ppermute | solution.py:240
  19.5 1.2 %copy-start = (bf16[8,4,64,256]{3,2,1,0:T(8,128)(2,1)S(1)}, bf16[8,4,64,256]{3,2,1,0:T(8,128)(2,1)}, u32[]{:S(2)}) copy-start(bf16[8,4,64,256]{3,2,1,0:T(8,128)(2,1)} %source_ref.1) | copy-start | bytes 3145732
  40.4 2.0 %copy-start.2 = (bf16[3,3,3,256,256]{4,3,2,1,0:T(8,128)(2,1)S(1)}, bf16[3,3,3,256,256]{4,3,2,1,0:T(8,128)(2,1)}, u32[]{:S(2)}) copy-start(bf16[3,3,3,256,256]{4,3,2,1,0:T(8,128)(2,1)} %param.9) | copy-start | bytes 10616836
  42.4 0.7 copy-start.4
  43.1 0.7 copy-start.5
  43.8 39.9 %copy-start.3 = (bf16[3,3,3,256,256]{4,3,2,1,0:T(8,128)(2,1)S(1)}, bf16[3,3,3,256,256]{4,3,2,1,0:T(8,128)(2,1)}, u32[]{:S(2)}) copy-start(bf16[3,3,3,256,256]{4,3,2,1,0:T(8,128)(2,1)} %param.12) | copy-start | bytes 10616836
  43.8 39.9 %copy-start.6 = (f32[256]{0:T(256)S(1)}, f32[256]{0:T(256)}, u32[]{:S(2)}) copy-start(f32[256]{0:T(256)} %param.13) | copy-start | bytes 3076
  43.8 39.9 %copy-start.7 = (f32[256]{0:T(256)S(1)}, f32[256]{0:T(256)}, u32[]{:S(2)}) copy-start(f32[256]{0:T(256)} %param.14) | copy-start | bytes 3076
  43.8 39.9 %copy-start.8 = (f32[256]{0:T(256)S(1)}, f32[256]{0:T(256)}, u32[]{:S(2)}) copy-start(f32[256]{0:T(256)} %param.15) | copy-start | bytes 3076
  55.4 28.3 %collective-permute-start.5 = (bf16[2,4,64,256]{3,2,1,0:T(8,128)(2,1)S(1)}, bf16[2,4,64,256]{3,2,1,0:T(8,128)(2,1)S(1)}, u32[]{:S(2)}, u32[]{:S(2)}) collective-permute-start(bf16[2,4,64,256]{3,2,1,0:T(8,128)(2,1)S(1)} %slice.49), channel_id=1, source_target_pairs={{0,4},{1,5},{2,6},{3,7},{4,8},{5,9},{6,10},{7,11},{8,12},{9,13},{1... | collective-permute-start | bytes 786440 | tf_op jit(solution)/shard_map/ppermute | solution.py:236
  58.4 25.3 %collective-permute-start.6 = (bf16[8,64,256]{2,1,0:T(8,128)(2,1)S(1)}, bf16[8,64,256]{2,1,0:T(8,128)(2,1)S(1)}, u32[]{:S(2)}, u32[]{:S(2)}) collective-permute-start(bf16[8,64,256]{2,1,0:T(8,128)(2,1)S(1)} %bitcast.48), channel_id=1, source_target_pairs={{0,1},{1,0},{2,3},{3,2},{4,5},{5,4},{6,7},{7,6},{8,9},{9,8},{10,11... | collective-permute-start | bytes 786440 | tf_op jit(solution)/shard_map/ppermute | solution.py:237
  59.3 24.3 %collective-permute-start.7 = (bf16[8,64,256]{2,1,0:T(8,128)(2,1)S(1)}, bf16[8,64,256]{2,1,0:T(8,128)(2,1)S(1)}, u32[]{:S(2)}, u32[]{:S(2)}) collective-permute-start(bf16[8,64,256]{2,1,0:T(8,128)(2,1)S(1)} %bitcast.47), channel_id=1, source_target_pairs={{1,2},{2,1},{5,6},{6,5},{9,10},{10,9},{13,14},{14,13},{17,18},{18,... | collective-permute-start | bytes 786440 | tf_op jit(solution)/shard_map/ppermute | solution.py:238
  61.7 21.9 %collective-permute-start.8 = (bf16[2,64,256]{2,1,0:T(8,128)(2,1)S(1)}, bf16[2,64,256]{2,1,0:T(8,128)(2,1)S(1)}, u32[]{:S(2)}, u32[]{:S(2)}) collective-permute-start(bf16[2,64,256]{2,1,0:T(8,128)(2,1)S(1)} %slice_bitcast_fusion.1), channel_id=1, source_target_pairs={{0,5},{1,4},{2,7},{3,6},{4,9},{5,8},{6,11},{7,10},{8,13},{9,12},{1... | collective-permute-start | bytes 196616 | tf_op jit(solution)/shard_map/ppermute | solution.py:239
  63.9 19.7 %collective-permute-start.9 = (bf16[2,64,256]{2,1,0:T(8,128)(2,1)S(1)}, bf16[2,64,256]{2,1,0:T(8,128)(2,1)S(1)}, u32[]{:S(2)}, u32[]{:S(2)}) collective-permute-start(bf16[2,64,256]{2,1,0:T(8,128)(2,1)S(1)} %slice_bitcast_fusion), channel_id=1, source_target_pairs={{1,6},{2,5},{5,10},{6,9},{9,14},{10,13},{13,18},{14,17},{17,22},{1... | collective-permute-start | bytes 196616 | tf_op jit(solution)/shard_map/ppermute | solution.py:240

commit v2 on v1

v2 whole, which is shorter than its diff:
```python
import functools

import jax
import jax.numpy as jnp
from jax import lax
from jax.experimental import pallas as pl
from jax.experimental.pallas import tpu as pltpu
from jax.sharding import PartitionSpec as P

GROUPS = 32
EPS = 1e-06
VMEM = pl.BlockSpec(memory_space=pltpu.VMEM)
LANES = 128
HIGHEST = lax.Precision.HIGHEST


def exact_dot(left, right):
    return jnp.dot(left, right, precision=HIGHEST, preferred_element_type=jnp.float32)


def group_of_channel(rows, cols, row_is_channel, span, shift):
    row = lax.broadcasted_iota(jnp.int32, (rows, cols), 0)
    col = lax.broadcasted_iota(jnp.int32, (rows, cols), 1)
    channel, lane = (row, col) if row_is_channel else (col, row)
    return jnp.where(channel // span + shift == lane, 1.0, 0.0)


def local_stats(values_ref, first, out_ref):
    last, rows, cols, chans = values_ref.shape
    frames = last - first
    span = chans // GROUPS
    count = float(frames * rows * cols * span)

    def block(index):
        return values_ref[index].astype(jnp.float32).reshape(rows * cols // 8, 8, chans)

    def add_sum(index, total):
        return total + jnp.sum(block(index), axis=0)

    total = lax.fori_loop(first, last, add_sum, jnp.zeros((8, chans), jnp.float32))
    gather = group_of_channel(chans, LANES, True, span, 0)
    spread = group_of_channel(LANES, chans, False, span, 0)
    means = jnp.sum(exact_dot(total, gather), axis=0, keepdims=True) / count
    means = jnp.broadcast_to(means, (8, LANES))
    centre = exact_dot(means, spread)

    def add_square(index, total):
        away = block(index) - centre
        return total + jnp.sum(away * away, axis=0)

    squares = lax.fori_loop(first, last, add_square, jnp.zeros((8, chans), jnp.float32))
    gather_high = group_of_channel(chans, LANES, True, span, GROUPS)
    squares = jnp.sum(exact_dot(squares, gather_high), axis=0, keepdims=True)
    out_ref[...] = jnp.broadcast_to(means[0:1] + squares, out_ref.shape)


def norm_terms(stats_ref, gain_ref, chans, count):
    stats = stats_ref[...]
    devices = stats.shape[0]
    average = jnp.sum(stats, axis=0, keepdims=True) / devices
    away = stats - average
    between = jnp.sum(away * away, axis=0, keepdims=True) / devices
    lane = lax.broadcasted_iota(jnp.int32, (1, LANES), 1)
    first = jnp.where(lane < GROUPS, average, 0.0)
    second = jnp.where(lane < GROUPS, between, jnp.where(lane < 2 * GROUPS, average / count, 0.0))
    span = chans // GROUPS
    spread = group_of_channel(LANES, chans, False, span, 0) + group_of_channel(
        LANES, chans, False, span, GROUPS
    )
    mean = exact_dot(jnp.broadcast_to(first, (8, LANES)), spread)[0:1]
    var = exact_dot(jnp.broadcast_to(second, (8, LANES)), spread)[0:1]
    return mean, gain_ref[...] / jnp.sqrt(var + EPS)


def near_and_far(rows):
    odd = lax.rem(lax.axis_index("rows"), 2)
    return (1 - odd) * (rows - 1), odd * (rows - 1)


def edges_kernel(values_ref, past_ref, near_ref, far_ref, near_past_ref, far_past_ref, sems):
    frames, rows = values_ref.shape[:2]
    lags = past_ref.shape[0]
    near, far = near_and_far(rows)
    late = pl.ds(frames - lags, lags)
    copies = [
        pltpu.make_async_copy(source, target, sems.at[index])
        for index, (source, target) in enumerate(
            (
                (values_ref.at[late], past_ref),
                (values_ref.at[:, near], near_ref),
                (values_ref.at[:, far], far_ref),
                (values_ref.at[late, near], near_past_ref),
                (values_ref.at[late, far], far_past_ref),
            )
        )
    ]
    for copy in copies:
        copy.start()
    for copy in copies:
        copy.wait()


def build_windows(body_of, edges_of, shape, mean, scale, offset, wide_ref):
    frames, rows, cols, chans = shape
    odd = lax.rem(lax.axis_index("rows"), 2) == 1
    has_past = lax.axis_index("frames") > 0
    has_above = lax.axis_index("rows") > 0
    has_below = lax.axis_index("rows") < lax.axis_size("rows") - 1
    column = lax.broadcasted_iota(jnp.int32, (cols, chans), 0)

    def put(frame, row, value, valid):
        value = (value.astype(jnp.float32) - mean) * scale + offset
        value = 0.5 * value * (1.0 + jnp.tanh(0.5 * value))
        if valid is not None:
            value = jnp.where(valid, value, 0.0)
        left = jnp.where(column == 0, 0.0, pltpu.roll(value, 1, 0))
        right = jnp.where(column == cols - 1, 0.0, pltpu.roll(value, cols - 1, 0))
        wide_ref[frame, row, :, 0:chans] = left.astype(jnp.bfloat16)
        wide_ref[frame, row, :, chans : 2 * chans] = value.astype(jnp.bfloat16)
        wide_ref[frame, row, :, 2 * chans :] = right.astype(jnp.bfloat16)

    def one(frame, valid):
        for row in range(rows):
            put(frame, row + 1, body_of(frame, row), valid)
        near, far = edges_of(frame)
        above = has_above if valid is None else jnp.logical_and(has_above, valid)
        below = has_below if valid is None else jnp.logical_and(has_below, valid)
        put(frame, 0, jnp.where(odd, near, far), above)
        put(frame, rows + 1, jnp.where(odd, far, near), below)

    return one, has_past


def conv_frames(wide_ref, kernel_ref, start, count, rows, cols, chans):
    total = None
    for lag_time in range(3):
        for lag_row in range(3):
            window = wide_ref[pl.ds(start + lag_time, count), lag_row : lag_row + rows]
            term = jnp.dot(
                window.reshape(count * rows * cols, 3 * chans),
                kernel_ref[lag_time, lag_row],
                preferred_element_type=jnp.float32,
            )
            total = term if total is None else total + term
    return total.reshape(count, rows, cols, -1)


def columns_apart(line, pair_ref):
    cols, chans = line.shape
    halves = range(chans // LANES)
    for half in halves:
        pair_ref[half] = line[:, half * LANES : (half + 1) * LANES]
    return (
        jnp.concatenate([pair_ref[half, pl.ds(k, cols // 2, stride=2)] for half in halves], axis=1)
        for k in range(2)
    )


def stats_kernel(values_ref, out_ref):
    local_stats(values_ref, 0, out_ref)


def first_kernel(
    own_ref, past_ref, near_ref, far_ref, near_past_ref, far_past_ref,
    stats_ref, gain_ref, offset_ref, kernel_ref,
    hidden_ref, out_stats_ref, out_near_ref, out_far_ref, wide_ref,
):
    frames, rows, cols, chans = own_ref.shape
    lags = past_ref.shape[0]
    count = frames * rows * cols * (chans // GROUPS)
    mean, scale = norm_terms(stats_ref, gain_ref, chans, count)
    terms = ((frames + lags, rows, cols, chans), mean, scale, offset_ref[...], wide_ref)
    put_past, has_past = build_windows(
        lambda f, r: past_ref[f, r], lambda f: (near_past_ref[f], far_past_ref[f]), *terms
    )
    put_own, _ = build_windows(
        lambda f, r: own_ref[f - lags, r], lambda f: (near_ref[f - lags], far_ref[f - lags]), *terms
    )

    def past(frame, carry):
        put_past(frame, has_past)
        return carry

    def own(frame, carry):
        put_own(frame, None)
        return carry

    lax.fori_loop(0, lags, past, 0)
    lax.fori_loop(lags, lags + frames, own, 0)
    step = 2
    near, far = near_and_far(rows)

    def some(index, carry):
        start = index * step
        conv = conv_frames(wide_ref, kernel_ref, start, step, rows, cols, chans)
        hidden_ref[pl.ds(start, step)] = conv.astype(jnp.bfloat16)
        return carry

    lax.fori_loop(0, (frames + 2) // step, some, 0)
    out_near_ref[...] = hidden_ref[:, near]
    out_far_ref[...] = hidden_ref[:, far]
    local_stats(hidden_ref, 2, out_stats_ref)


def second_kernel(
    hidden_ref, near_ref, far_ref, stats_ref, gain_ref, offset_ref, kernel_ref, source_ref,
    bias_ref, low_ref, high_ref, wide_ref, pair_ref,
):
    frames, rows, cols, chans = source_ref.shape
    count = frames * rows * cols * (chans // GROUPS)
    mean, scale = norm_terms(stats_ref, gain_ref, chans, count)
    put, has_past = build_windows(
        lambda f, r: hidden_ref[f, r], lambda f: (near_ref[f], far_ref[f]),
        hidden_ref.shape, mean, scale, offset_ref[...], wide_ref,
    )

    def past(frame, carry):
        put(frame, has_past)
        return carry

    def own(frame, carry):
        put(frame, None)
        return carry

    lax.fori_loop(0, 2, past, 0)
    lax.fori_loop(2, frames + 2, own, 0)
    factor = 0.5 ** 1.5
    bands = low_ref.shape[0]
    width = cols // 2 // bands

    def some(index, carry):
        start = index * 2
        conv = conv_frames(wide_ref, kernel_ref, start, 2, rows, cols, chans)
        summed = source_ref[pl.ds(start, 2)].astype(jnp.float32) + conv + bias_ref[...]
        for time_band in range(2):
            mixed = summed[0] - summed[1] if time_band else summed[0] + summed[1]
            for pair in range(rows // 2):
                upper, lower = mixed[2 * pair], mixed[2 * pair + 1]
                for row_band in range(2):
                    line = (upper - lower if row_band else upper + lower) * factor
                    even, uneven = columns_apart(line, pair_ref)
                    for col_band in range(2):
                        value = even - uneven if col_band else even + uneven
                        value = value.astype(jnp.bfloat16)
                        band = 4 * time_band + 2 * row_band + col_band
                        if band:
                            high_ref[band - 1, index, pair] = value
                        else:
                            for target in range(bands):
                                low_ref[target, index, pair] = value[
                                    target * width : (target + 1) * width
                                ]
        return carry

    lax.fori_loop(0, frames // 2, some, 0)


def routes():
    frame_count, row_count = lax.axis_size("frames"), lax.axis_size("rows")
    same = [(r, r) for r in range(row_count)]
    near = [(r, r ^ 1) for r in range(row_count)]
    far = [(r, ((r + 1) ^ 1) - 1) for r in range(1, row_count - 1)]

    def route(shift, pairs):
        return [
            (f * row_count + r, (f + shift) * row_count + s)
            for f in range(frame_count - shift)
            for r, s in pairs
        ]

    return route(0, near), route(0, far), route(1, same), route(1, near), route(1, far)


def send(values, route):
    return lax.ppermute(values, ("frames", "rows"), route)


def share(stats):
    return lax.all_to_all(stats, ("frames", "rows"), 0, 0, tiled=True)


def body(inputs, kernel_one, gain_one, offset_one, kernel_two, gain_two, offset_two, bias_two):
    frames, rows, cols, chans = inputs.shape
    devices = lax.axis_size("frames") * lax.axis_size("rows")
    bands = lax.axis_size("rows")
    lags = 4
    stats_shape = jax.ShapeDtypeStruct((devices, LANES), jnp.float32)
    weights_one = kernel_one.reshape(3, 3, 3 * chans, chans)
    weights_two = kernel_two.reshape(3, 3, 3 * chans, chans)

    def half(*shape):
        return jax.ShapeDtypeStruct(shape, jnp.bfloat16)

    def wide(count):
        return pltpu.VMEM((count, rows + 2, cols, 3 * chans), jnp.bfloat16)

    def call(kernel, name, mib, ins, out_shape, scratch=(), cost=None, space=VMEM):
        return pl.pallas_call(
            kernel, out_shape=out_shape, in_specs=[space] * len(ins),
            out_specs=jax.tree.map(lambda _: VMEM, out_shape), scratch_shapes=list(scratch),
            compiler_params=pltpu.CompilerParams(vmem_limit_bytes=mib * 2**20), name=name,
            cost_estimate=cost,
        )(*ins)

    to_near, to_far, to_next, to_next_near, to_next_far = routes()
    past, near, far, near_past, far_past = call(
        edges_kernel, "edges", 8, (inputs,),
        (
            half(lags, rows, cols, chans), half(frames, cols, chans), half(frames, cols, chans),
            half(lags, cols, chans), half(lags, cols, chans),
        ),
        [pltpu.SemaphoreType.DMA((5,))], space=pl.BlockSpec(memory_space=pl.ANY),
    )
    halos = (
        send(past, to_next), send(near, to_near), send(far, to_far),
        send(near_past, to_next_near), send(far_past, to_next_far),
    )
    stats = call(
        stats_kernel, "stats_one", 8, (inputs,), stats_shape,
        cost=pl.CostEstimate(flops=10**10, bytes_accessed=10**6, transcendentals=0),
    )
    stats = share(stats)
    hidden, stats, near, far = call(
        first_kernel, "conv_one", 32,
        (inputs, *halos, stats, gain_one[None], offset_one[None], weights_one),
        (
            half(frames + 2, rows, cols, chans), stats_shape,
            half(frames + 2, cols, chans), half(frames + 2, cols, chans),
        ),
        [wide(frames + lags)],
    )
    near, far = send(near, to_near), send(far, to_far)
    stats = share(stats)
    low, high = call(
        second_kernel, "conv_two", 32,
        (
            hidden, near, far, stats, gain_two[None], offset_two[None], weights_two, inputs,
            bias_two[None],
        ),
        (
            half(bands, frames // 2, rows // 2, cols // 2 // bands, chans),
            half(7, frames // 2, rows // 2, cols // 2, chans),
        ),
        [wide(frames + 2), pltpu.VMEM((chans // LANES, cols, LANES), jnp.float32)],
    )
    tiles = lax.all_to_all(low, "rows", split_axis=0, concat_axis=0, tiled=True)
    tiles = jnp.transpose(tiles, (1, 0, 2, 3, 4)).reshape(
        frames // 2, bands * (rows // 2), cols // 2 // bands, chans
    )
    return tiles, high


def solution(mesh):
    in_specs = (P("frames", "rows", None, None), P(), P(), P(), P(), P(), P(), P())
    out_specs = (P("frames", None, "rows", None), P(None, "frames", "rows", None, None))
    return jax.shard_map(body, mesh=mesh, in_specs=in_specs, out_specs=out_specs, check_vma=False)
```

time: 103 us -> 89 us (0.86)
  starting transfers between devices: 29 us -> 20.2 us
  local copies, waits for them, and re-layouts: 6.36 us -> 1.93 us
  Pallas kernels: 24.2 us -> 26.8 us
  blocking collectives: 41 us -> 38.9 us
  other arithmetic: 1.18 us -> 0 us
    ppermute x10 -> x7, starting transfers between devices: 29 us -> 20.2 us  [send(): return lax.ppermute(values, ('frames', 'rows'), route)]
    unnamed x18, local copies, waits for them, and re-layouts: 4.59 us -> 1.27 us
    pallas_call x3 -> x4, Pallas kernels: 24.2 us -> 26.8 us  [call(): pl.pallas_call(kernel, out_shape=out_shape, in_specs=[space] * len(ins),...]
    all_to_all x2, blocking collectives: 34.3 us -> 32.1 us  [share(): return lax.all_to_all(stats, ('frames', 'rows'), 0, 0, tiled=True)]
    select_n x2 -> x0, other arithmetic: 1.18 us -> none  [exchange(): far = jnp.where(odd, bottom, top)]
    slice x6 -> x0, local copies, waits for them, and re-layouts: 1.1 us -> none  [the longest x2 1.08 us: exchange(): past = lax.ppermute(values[-2:], axes, route(later, 1, same))]
  transfers between devices with their start and end apart: 10 -> 7, of which waited for: 0 -> 0; matrix products, arithmetic and copies ran while one was open for 1% -> 0% of each run, Pallas kernels for 1% -> 1%
where the time goes in v2:
time: 89 us; the launch traced here: 88.8 us
  blocking collectives  38.9 us (44%)
  Pallas kernels  26.8 us (30%)
  starting transfers between devices  20.2 us (23%)
  local copies, waits for them, and re-layouts  1.93 us (2%)
    all_to_all x2, blocking collectives, share(): return lax.all_to_all(stats, ('frames', 'rows'), 0, 0, tiled=True)  32.1 us
    pallas_call x4, Pallas kernels, call(): pl.pallas_call(kernel, out_shape=out_shape, in_specs=[space] * len(ins),...  26.8 us
    ppermute x7, starting transfers between devices, send(): return lax.ppermute(values, ('frames', 'rows'), route)  20.2 us
    all_to_all x1, blocking collectives, body(): tiles = lax.all_to_all(low, 'rows', split_axis=0, concat_axis=0, tiled=True)  6.72 us
  transfers between devices with their start and end apart: 7, of which 0 were waited for; matrix products, arithmetic and copies ran while one was open for 0% of the time, Pallas kernels for 1%

profile of v2, /device:TPU:1, one launch (start us, length us, event | category | flops | bytes accessed | tf_op | source)
XLA Modules:
  0.0 88.8 jit_solution(1825801650569997472)
XLA Ops:
  0.6 0.0 copy-start
  0.6 1.2 %copy-done = bf16[8,4,64,256]{3,2,1,0:T(8,128)(2,1)S(1)} copy-done((bf16[8,4,64,256]{3,2,1,0:T(8,128)(2,1)S(1)}, bf16[8,4,64,256]{3,2,1,0:T(8,128)(2,1)}, u32[]{:S(2)}) %copy-start) | copy-done | bytes 1048600
  1.9 0.2 edges.1
  2.1 6.0 %collective-permute-start.3 = (bf16[4,64,256]{2,1,0:T(8,128)(2,1)S(1)}, bf16[4,64,256]{2,1,0:T(8,128)(2,1)S(1)}, u32[]{:S(2)}, u32[]{:S(2)}) collective-permute-start(bf16[4,64,256]{2,1,0:T(8,128)(2,1)S(1)} %get-tuple-element.16), channel_id=1, source_target_pairs={{0,5},{1,4},{2,7},{3,6},{4,9},{5,8},{6,11},{7,10},{8,13},{9,12},{1... | collective-permute-start | bytes 393224 | tf_op jit(solution)/shard_map/ppermute | solution.py:275
  8.1 3.5 %collective-permute-start.4 = (bf16[4,64,256]{2,1,0:T(8,128)(2,1)S(1)}, bf16[4,64,256]{2,1,0:T(8,128)(2,1)S(1)}, u32[]{:S(2)}, u32[]{:S(2)}) collective-permute-start(bf16[4,64,256]{2,1,0:T(8,128)(2,1)S(1)} %get-tuple-element.17), channel_id=1, source_target_pairs={{1,6},{2,5},{5,10},{6,9},{9,14},{10,13},{13,18},{14,17},{17,22},{1... | collective-permute-start | bytes 393224 | tf_op jit(solution)/shard_map/ppermute | solution.py:275
  11.6 0.1 collective-permute-start.1
  11.7 1.9 %collective-permute-start.2 = (bf16[8,64,256]{2,1,0:T(8,128)(2,1)S(1)}, bf16[8,64,256]{2,1,0:T(8,128)(2,1)S(1)}, u32[]{:S(2)}, u32[]{:S(2)}) collective-permute-start(bf16[8,64,256]{2,1,0:T(8,128)(2,1)S(1)} %get-tuple-element.15), channel_id=1, source_target_pairs={{1,2},{2,1},{5,6},{6,5},{9,10},{10,9},{13,14},{14,13},{17,18},{18,... | collective-permute-start | bytes 786440 | tf_op jit(solution)/shard_map/ppermute | solution.py:275
  13.7 0.0 copy-start.1
  13.7 0.0 copy-start.2
  13.7 0.0 copy-start.4
  13.7 0.0 copy-start.5
  13.7 5.7 %collective-permute-start = (bf16[4,4,64,256]{3,2,1,0:T(8,128)(2,1)S(1)}, bf16[4,4,64,256]{3,2,1,0:T(8,128)(2,1)S(1)}, u32[]{:S(2)}, u32[]{:S(2)}) collective-permute-start(bf16[4,4,64,256]{3,2,1,0:T(8,128)(2,1)S(1)} %get-tuple-element.13), channel_id=1, source_target_pairs={{0,4},{1,5},{2,6},{3,7},{4,8},{5,9},{6,10},{7,11},{8,12},{9,13},{1... | collective-permute-start | bytes 1572872 | tf_op jit(solution)/shard_map/ppermute | solution.py:275
  19.5 1.2 %stats_one.1 = f32[128,128]{1,0:T(8,128)S(1)} custom-call(bf16[8,4,64,256]{3,2,1,0:T(8,128)(2,1)S(1)} %copy-done), custom_call_target="tpu_custom_call" | custom-call | flops 10000000000 | bytes 1000000 | tf_op jit(solution)/shard_map/stats_one/pallas_call | solution.py:298
  20.7 0.0 copy-start.3
  20.7 0.0 copy-start.6
  20.7 0.0 copy-start.7
  20.7 0.0 copy-start.8
  20.7 18.0 %all_to_all.27 = f32[128,1,128]{2,1,0:T(1,128)S(1)} all-to-all(f32[128,1,128]{2,1,0:T(1,128)S(1)} %bitcast.22), channel_id=1, replica_groups=mesh['frames'=32,'rows'=4] {'frames','rows'}, dimensions={0} | all-to-all | bytes 131072 | tf_op jit(solution)/shard_map/all_to_all | solution.py:279
  38.7 0.0 collective-permute-done.3.near_past_ref
  38.7 0.0 collective-permute-done.4.far_past_ref
  38.7 0.0 collective-permute-done.1.near_ref
  38.8 0.0 collective-permute-done.2.far_ref
  38.8 0.0 collective-permute-done.past_ref
  38.8 0.0 copy-done.1
  38.8 0.0 copy-done.2
  38.8 0.0 copy-done.4
  38.8 0.0 copy-done.5
  38.8 13.8 %conv_one.1 = (bf16[10,4,64,256]{3,2,1,0:T(8,128)(2,1)S(1)}, f32[128,128]{1,0:T(8,128)S(1)}, bf16[10,64,256]{2,1,0:T(8,128)(2,1)S(1)}, bf16[10,64,256]{2,1,0:T(8,128)(2,1)S(1)}) custom-call(bf16[8,4,64,256]{3,2,1,0:T(8,128)(2,1)S(1)} %copy-done.1, bf16[4,4,64,256]{3,2,1,0:T(8,128)(2,1)S(1)} %collective-permute-done.past_ref, ...), custom_call_target="tpu_custom_call" | custom-call | tf_op jit(solution)/shard_map/conv_one/pallas_call | solution.py:298
  52.7 0.8 collective-permute-start.5
  53.5 2.1 %collective-permute-start.6 = (bf16[10,64,256]{2,1,0:T(8,128)(2,1)S(1)}, bf16[10,64,256]{2,1,0:T(8,128)(2,1)S(1)}, u32[]{:S(2)}, u32[]{:S(2)}) collective-permute-start(bf16[10,64,256]{2,1,0:T(8,128)(2,1)S(1)} %get-tuple-element.20), channel_id=1, source_target_pairs={{1,2},{2,1},{5,6},{6,5},{9,10},{10,9},{13,14},{14,13},{17,18},{18,... | collective-permute-start | bytes 983048 | tf_op jit(solution)/shard_map/ppermute | solution.py:275
  55.6 14.2 %all_to_all.28 = f32[128,1,128]{2,1,0:T(1,128)S(1)} all-to-all(f32[128,1,128]{2,1,0:T(1,128)S(1)} %bitcast.21), channel_id=1, replica_groups=mesh['frames'=32,'rows'=4] {'frames','rows'}, dimensions={0} | all-to-all | bytes 131072 | tf_op jit(solution)/shard_map/all_to_all | solution.py:279
  69.8 0.0 collective-permute-done.5.near_ref
  69.8 0.0 collective-permute-done.6.far_ref
  69.8 0.0 copy-done.3
  69.8 0.0 copy-done.6
  69.8 0.0 copy-done.7
  69.8 0.0 copy-done.8
  69.8 11.6 %conv_two.1 = (bf16[4,4,2,8,256]{4,3,2,1,0:T(8,128)(2,1)S(1)}, bf16[7,4,2,32,256]{4,3,2,1,0:T(8,128)(2,1)}) custom-call(bf16[10,4,64,256]{3,2,1,0:T(8,128)(2,1)S(1)} %get-tuple-element.18.hidden_ref, bf16[10,64,256]{2,1,0:T(8,128)(2,1)S(1)} %collective-permute-done.5.near_ref, bf16[10,64,256]{2,1,0:T(8,128)(2,1)S(1)} %collective-permute-done.6.far_ref, ...), custom_call_target="tpu_custom_call" | custom-call | tf_op jit(solution)/shard_map/conv_two/pallas_call | solution.py:298
  81.4 6.7 %all_to_all.29 = bf16[4,4,2,8,256]{4,3,2,1,0:T(8,128)(2,1)S(1)} all-to-all(bf16[4,4,2,8,256]{4,3,2,1,0:T(8,128)(2,1)S(1)} %get-tuple-element.22), channel_id=1, replica_groups=mesh['frames'=32,'rows'=4] {'rows'}, dimensions={0} | all-to-all | bytes 262144 | tf_op jit(solution)/shard_map/all_to_all | solution.py:346
  88.1 0.7 copy.13
Async XLA Ops:
  0.6 1.2 %copy-start = (bf16[8,4,64,256]{3,2,1,0:T(8,128)(2,1)S(1)}, bf16[8,4,64,256]{3,2,1,0:T(8,128)(2,1)}, u32[]{:S(2)}) copy-start(bf16[8,4,64,256]{3,2,1,0:T(8,128)(2,1)} %source_ref.1) | copy-start | bytes 3145732
  2.1 36.7 %collective-permute-start.3 = (bf16[4,64,256]{2,1,0:T(8,128)(2,1)S(1)}, bf16[4,64,256]{2,1,0:T(8,128)(2,1)S(1)}, u32[]{:S(2)}, u32[]{:S(2)}) collective-permute-start(bf16[4,64,256]{2,1,0:T(8,128)(2,1)S(1)} %get-tuple-element.16), channel_id=1, source_target_pairs={{0,5},{1,4},{2,7},{3,6},{4,9},{5,8},{6,11},{7,10},{8,13},{9,12},{1... | collective-permute-start | bytes 393224 | tf_op jit(solution)/shard_map/ppermute | solution.py:275
  8.1 30.6 %collective-permute-start.4 = (bf16[4,64,256]{2,1,0:T(8,128)(2,1)S(1)}, bf16[4,64,256]{2,1,0:T(8,128)(2,1)S(1)}, u32[]{:S(2)}, u32[]{:S(2)}) collective-permute-start(bf16[4,64,256]{2,1,0:T(8,128)(2,1)S(1)} %get-tuple-element.17), channel_id=1, source_target_pairs={{1,6},{2,5},{5,10},{6,9},{9,14},{10,13},{13,18},{14,17},{17,22},{1... | collective-permute-start | bytes 393224 | tf_op jit(solution)/shard_map/ppermute | solution.py:275
  11.6 27.1 %collective-permute-start.1 = (bf16[8,64,256]{2,1,0:T(8,128)(2,1)S(1)}, bf16[8,64,256]{2,1,0:T(8,128)(2,1)S(1)}, u32[]{:S(2)}, u32[]{:S(2)}) collective-permute-start(bf16[8,64,256]{2,1,0:T(8,128)(2,1)S(1)} %get-tuple-element.14), channel_id=1, source_target_pairs={{0,1},{1,0},{2,3},{3,2},{4,5},{5,4},{6,7},{7,6},{8,9},{9,8},{10,11... | collective-permute-start | bytes 786440 | tf_op jit(solution)/shard_map/ppermute | solution.py:275
  11.7 27.0 %collective-permute-start.2 = (bf16[8,64,256]{2,1,0:T(8,128)(2,1)S(1)}, bf16[8,64,256]{2,1,0:T(8,128)(2,1)S(1)}, u32[]{:S(2)}, u32[]{:S(2)}) collective-permute-start(bf16[8,64,256]{2,1,0:T(8,128)(2,1)S(1)} %get-tuple-element.15), channel_id=1, source_target_pairs={{1,2},{2,1},{5,6},{6,5},{9,10},{10,9},{13,14},{14,13},{17,18},{18,... | collective-permute-start | bytes 786440 | tf_op jit(solution)/shard_map/ppermute | solution.py:275
  13.7 25.1 %copy-start.1 = (bf16[8,4,64,256]{3,2,1,0:T(8,128)(2,1)S(1)}, bf16[8,4,64,256]{3,2,1,0:T(8,128)(2,1)}, u32[]{:S(2)}) copy-start(bf16[8,4,64,256]{3,2,1,0:T(8,128)(2,1)} %source_ref.1) | copy-start | bytes 3145732
  13.7 25.1 %copy-start.2 = (bf16[3,3,3,256,256]{4,3,2,1,0:T(8,128)(2,1)S(1)}, bf16[3,3,3,256,256]{4,3,2,1,0:T(8,128)(2,1)}, u32[]{:S(2)}) copy-start(bf16[3,3,3,256,256]{4,3,2,1,0:T(8,128)(2,1)} %param.9) | copy-start | bytes 10616836
  13.7 25.1 %copy-start.4 = (f32[256]{0:T(256)S(1)}, f32[256]{0:T(256)}, u32[]{:S(2)}) copy-start(f32[256]{0:T(256)} %param.10) | copy-start | bytes 3076
  13.7 25.1 %copy-start.5 = (f32[256]{0:T(256)S(1)}, f32[256]{0:T(256)}, u32[]{:S(2)}) copy-start(f32[256]{0:T(256)} %param.11) | copy-start | bytes 3076
  13.7 25.1 %collective-permute-start = (bf16[4,4,64,256]{3,2,1,0:T(8,128)(2,1)S(1)}, bf16[4,4,64,256]{3,2,1,0:T(8,128)(2,1)S(1)}, u32[]{:S(2)}, u32[]{:S(2)}) collective-permute-start(bf16[4,4,64,256]{3,2,1,0:T(8,128)(2,1)S(1)} %get-tuple-element.13), channel_id=1, source_target_pairs={{0,4},{1,5},{2,6},{3,7},{4,8},{5,9},{6,10},{7,11},{8,12},{9,13},{1... | collective-permute-start | bytes 1572872 | tf_op jit(solution)/shard_map/ppermute | solution.py:275
  20.7 49.1 %copy-start.3 = (bf16[3,3,3,256,256]{4,3,2,1,0:T(8,128)(2,1)S(1)}, bf16[3,3,3,256,256]{4,3,2,1,0:T(8,128)(2,1)}, u32[]{:S(2)}) copy-start(bf16[3,3,3,256,256]{4,3,2,1,0:T(8,128)(2,1)} %param.12) | copy-start | bytes 10616836
  20.7 49.1 %copy-start.6 = (f32[256]{0:T(256)S(1)}, f32[256]{0:T(256)}, u32[]{:S(2)}) copy-start(f32[256]{0:T(256)} %param.13) | copy-start | bytes 3076
  20.7 49.1 %copy-start.7 = (f32[256]{0:T(256)S(1)}, f32[256]{0:T(256)}, u32[]{:S(2)}) copy-start(f32[256]{0:T(256)} %param.14) | copy-start | bytes 3076
  20.7 49.1 %copy-start.8 = (f32[256]{0:T(256)S(1)}, f32[256]{0:T(256)}, u32[]{:S(2)}) copy-start(f32[256]{0:T(256)} %param.15) | copy-start | bytes 3076
  52.7 17.1 %collective-permute-start.5 = (bf16[10,64,256]{2,1,0:T(8,128)(2,1)S(1)}, bf16[10,64,256]{2,1,0:T(8,128)(2,1)S(1)}, u32[]{:S(2)}, u32[]{:S(2)}) collective-permute-start(bf16[10,64,256]{2,1,0:T(8,128)(2,1)S(1)} %get-tuple-element.19), channel_id=1, source_target_pairs={{0,1},{1,0},{2,3},{3,2},{4,5},{5,4},{6,7},{7,6},{8,9},{9,8},{10,11... | collective-permute-start | bytes 983048 | tf_op jit(solution)/shard_map/ppermute | solution.py:275
  53.5 16.3 %collective-permute-start.6 = (bf16[10,64,256]{2,1,0:T(8,128)(2,1)S(1)}, bf16[10,64,256]{2,1,0:T(8,128)(2,1)S(1)}, u32[]{:S(2)}, u32[]{:S(2)}) collective-permute-start(bf16[10,64,256]{2,1,0:T(8,128)(2,1)S(1)} %get-tuple-element.20), channel_id=1, source_target_pairs={{1,2},{2,1},{5,6},{6,5},{9,10},{10,9},{13,14},{14,13},{17,18},{18,... | collective-permute-start | bytes 983048 | tf_op jit(solution)/shard_map/ppermute | solution.py:275

commit v3 on v0

v3 whole, which is shorter than its diff:
```python
import functools

import jax
import jax.numpy as jnp
from jax import lax
from jax.experimental import pallas as pl
from jax.experimental.pallas import tpu as pltpu
from jax.sharding import PartitionSpec as P

GROUPS = 32
EPS = 1e-06
LANES = 128
LAGS = 4
VMEM = pl.BlockSpec(memory_space=pltpu.VMEM)
HBM = pl.BlockSpec(memory_space=pltpu.HBM)
HIGHEST = lax.Precision.HIGHEST


def exact_dot(left, right):
    return jnp.dot(left, right, precision=HIGHEST, preferred_element_type=jnp.float32)


def ties(rows, cols, row_is_channel, span, shifts):
    row = lax.broadcasted_iota(jnp.int32, (rows, cols), 0)
    col = lax.broadcasted_iota(jnp.int32, (rows, cols), 1)
    channel, lane = (row, col) if row_is_channel else (col, row)
    total = 0.0
    for shift in shifts:
        total = total + jnp.where(channel // span + shift == lane, 1.0, 0.0)
    return total


def to_lanes(sums):
    chans = sums.shape[1]
    matrix = ties(chans, LANES, True, chans // GROUPS, (0, GROUPS))
    return jnp.sum(exact_dot(sums, matrix), axis=0, keepdims=True)


def to_channels(lanes, chans, shifts):
    matrix = ties(LANES, chans, False, chans // GROUPS, shifts)
    return exact_dot(jnp.broadcast_to(lanes, (8, LANES)), matrix)[0:1]


def folded(values):
    return values.astype(jnp.float32).reshape(-1, 8, values.shape[-1])


def put_stats(out_ref, total, squares, centre, count):
    mean = to_lanes(total) / count
    away = mean - centre
    spread = to_lanes(squares) - count * (away * away)
    lane = lax.broadcasted_iota(jnp.int32, (1, LANES), 1)
    row = jnp.where(lane < GROUPS, mean, jnp.where(lane < 2 * GROUPS, spread, 0.0))
    out_ref[...] = jnp.broadcast_to(row, out_ref.shape)


def norm_terms(stats_ref, gain_ref, chans, count):
    stats = stats_ref[...]
    devices = stats.shape[0]
    average = jnp.sum(stats, axis=0, keepdims=True) / devices
    away = stats - average
    between = jnp.sum(away * away, axis=0, keepdims=True) / devices
    lane = lax.broadcasted_iota(jnp.int32, (1, LANES), 1)
    first = jnp.where(lane < GROUPS, average, 0.0)
    second = jnp.where(lane < GROUPS, between, jnp.where(lane < 2 * GROUPS, average / count, 0.0))
    mean = to_channels(first, chans, (0,))
    var = to_channels(second, chans, (0, GROUPS))
    return mean, gain_ref[...] / jnp.sqrt(var + EPS)


def near_and_far(rows):
    odd = lax.rem(lax.axis_index("rows"), 2)
    return (1 - odd) * (rows - 1), odd * (rows - 1)


def has_past():
    return lax.axis_index("frames") > 0


class Window:
    def __init__(self, wide_ref, mean, scale, offset):
        self.wide_ref = wide_ref
        self.terms = mean, scale, offset
        self.rows, self.cols = wide_ref.shape[1] - 2, wide_ref.shape[2]
        self.chans = wide_ref.shape[3] // 3
        place = lax.axis_index("rows")
        self.odd = lax.rem(place, 2) == 1
        self.above = place > 0
        self.below = place < lax.axis_size("rows") - 1
        self.column = lax.broadcasted_iota(jnp.int32, (self.cols, self.chans), 0)

    def put_row(self, frame, row, value, valid):
        mean, scale, offset = self.terms
        chans, cols = self.chans, self.cols
        value = (value.astype(jnp.float32) - mean) * scale + offset
        value = 0.5 * value * (1.0 + jnp.tanh(0.5 * value))
        if valid is not None:
            value = jnp.where(valid, value, 0.0)
        left = jnp.where(self.column == 0, 0.0, pltpu.roll(value, 1, 0))
        right = jnp.where(self.column == cols - 1, 0.0, pltpu.roll(value, cols - 1, 0))
        self.wide_ref[frame, row, :, 0:chans] = left.astype(jnp.bfloat16)
        self.wide_ref[frame, row, :, chans : 2 * chans] = value.astype(jnp.bfloat16)
        self.wide_ref[frame, row, :, 2 * chans :] = right.astype(jnp.bfloat16)

    def put(self, frame, body, near, far, valid):
        for row in range(self.rows):
            self.put_row(frame, row + 1, body[row], valid)
        above, below = self.above, self.below
        if valid is not None:
            above, below = jnp.logical_and(above, valid), jnp.logical_and(below, valid)
        self.put_row(frame, 0, jnp.where(self.odd, near, far), above)
        self.put_row(frame, self.rows + 1, jnp.where(self.odd, far, near), below)

    def conv(self, start, kernel_ref):
        total = None
        for lag_time in range(3):
            for lag_row in range(3):
                window = self.wide_ref[start + lag_time, lag_row : lag_row + self.rows]
                term = jnp.dot(
                    window.reshape(self.rows * self.cols, 3 * self.chans),
                    kernel_ref[lag_time, lag_row],
                    preferred_element_type=jnp.float32,
                )
                total = term if total is None else total + term
        return total


def edges_kernel(values_ref, past_ref, near_ref, far_ref, sems):
    frames, rows = values_ref.shape[:2]
    near, far = near_and_far(rows)
    pairs = (
        (values_ref.at[pl.ds(frames - LAGS, LAGS)], past_ref),
        (values_ref.at[:, near], near_ref),
        (values_ref.at[:, far], far_ref),
    )
    copies = [pltpu.make_async_copy(*pair, sems.at[i]) for i, pair in enumerate(pairs)]
    for copy in copies:
        copy.start()
    for copy in copies:
        copy.wait()


def past_edges_kernel(past_ref, near_ref, far_ref):
    near, far = near_and_far(past_ref.shape[1])
    near_ref[...] = past_ref[:, near]
    far_ref[...] = past_ref[:, far]


def stats_kernel(values_ref, out_ref):
    frames, rows, cols, chans = values_ref.shape
    count = float(frames * rows * cols * (chans // GROUPS))
    zero = jnp.zeros((8, chans), jnp.float32)

    def add(index, total):
        return total + jnp.sum(folded(values_ref[index]), axis=0)

    total = lax.fori_loop(0, frames, add, zero)
    lanes = to_lanes(total) / count
    centre = to_channels(lanes, chans, (0,))

    def add_square(index, total):
        away = folded(values_ref[index]) - centre
        return total + jnp.sum(away * away, axis=0)

    squares = lax.fori_loop(0, frames, add_square, zero)
    put_stats(out_ref, total, squares, lanes, count)


def group_count(frames, rows, cols, chans):
    return float(frames * rows * cols * (chans // GROUPS))


def first_kernel_own(
    own_ref, near_ref, far_ref, stats_ref, gain_ref, offset_ref, kernel_ref,
    hidden_ref, sums_ref, wide_ref,
):
    frames, rows, cols, chans = own_ref.shape
    mean, scale = norm_terms(stats_ref, gain_ref, chans, group_count(*own_ref.shape))
    window = Window(wide_ref, mean, scale, offset_ref[...])
    total = jnp.zeros((8, chans), jnp.float32)
    for frame in range(frames):
        window.put(frame, own_ref.at[frame], near_ref[frame], far_ref[frame], None)
        if frame < 2:
            continue
        hidden = window.conv(frame - 2, kernel_ref).astype(jnp.bfloat16)
        hidden_ref[frame - 2] = hidden.reshape(rows, cols, chans)
        total = total + jnp.sum(folded(hidden), axis=0)
    sums_ref[...] = total


def first_kernel_past(
    own_ref, near_ref, far_ref, past_ref, near_past_ref, far_past_ref,
    stats_ref, gain_ref, offset_ref, kernel_ref, later_ref, sums_ref,
    hidden_ref, out_stats_ref, out_near_ref, out_far_ref, wide_ref,
):
    frames, rows, cols, chans = own_ref.shape
    count = group_count(*own_ref.shape)
    mean, scale = norm_terms(stats_ref, gain_ref, chans, count)
    window = Window(wide_ref, mean, scale, offset_ref[...])
    sums = sums_ref[...]
    lanes = to_lanes(sums) / group_count(*later_ref.shape)
    centre = to_channels(lanes, chans, (0,))
    squares = jnp.zeros((8, chans), jnp.float32)
    later = 0
    for frame in range(LAGS + 2):
        own = frame - LAGS
        if own < 0:
            window.put(
                frame, past_ref.at[frame], near_past_ref[frame], far_past_ref[frame], has_past()
            )
        else:
            window.put(frame, own_ref.at[own], near_ref[own], far_ref[own], None)
        if frame < 2:
            continue
        hidden = window.conv(frame - 2, kernel_ref).astype(jnp.bfloat16)
        hidden_ref[frame - 2] = hidden.reshape(rows, cols, chans)
        blocks = [hidden] if own >= 0 else []
        while later * LAGS < later_ref.shape[0] * (frame - 1):
            blocks.append(later_ref[later])
            later += 1
        for block in blocks:
            away = folded(block) - centre
            squares = squares + jnp.sum(away * away, axis=0)
        if own >= 0:
            sums = sums + jnp.sum(folded(hidden), axis=0)
    put_stats(out_stats_ref, sums, squares, lanes, count)
    near, far = near_and_far(rows)
    for source, out_ref in ((near, out_near_ref), (far, out_far_ref)):
        out_ref[0:LAGS] = hidden_ref[:, source]
        out_ref[LAGS:] = later_ref[:, source]


def columns_apart(line, pair_ref):
    cols, chans = line.shape
    halves = range(chans // LANES)
    for half in halves:
        pair_ref[half] = line[:, half * LANES : (half + 1) * LANES]
    return (
        jnp.concatenate([pair_ref[half, pl.ds(k, cols // 2, stride=2)] for half in halves], axis=1)
        for k in range(2)
    )


def second_kernel(
    hidden_ref, later_ref, near_ref, far_ref, stats_ref, gain_ref, offset_ref, kernel_ref,
    source_ref, bias_ref, *rest,
):
    *low_refs, high_ref, wide_ref, pair_ref, low_ref, held_ref, sems = rest
    frames, rows, cols, chans = source_ref.shape
    mean, scale = norm_terms(stats_ref, gain_ref, chans, group_count(*source_ref.shape))
    window = Window(wide_ref, mean, scale, offset_ref[...])
    factor = 0.5**1.5
    bands = len(low_refs)
    width = cols // 2 // bands
    copies, summed = [], {}
    for frame in range(frames + 2):
        body = hidden_ref.at[frame] if frame < LAGS else later_ref.at[frame - LAGS]
        window.put(frame, body, near_ref[frame], far_ref[frame], has_past() if frame < 2 else None)
        if frame < 2:
            continue
        own = frame - 2
        conv = window.conv(own, kernel_ref).reshape(rows, cols, chans)
        summed[own % 2] = source_ref[own].astype(jnp.float32) + conv + bias_ref[...]
        if own % 2 == 0:
            continue
        index = own // 2
        for time_band in range(2):
            mixed = summed[0] - summed[1] if time_band else summed[0] + summed[1]
            for pair in range(rows // 2):
                upper, lower = mixed[2 * pair], mixed[2 * pair + 1]
                for row_band in range(2):
                    line = (upper - lower if row_band else upper + lower) * factor
                    slot = ((index * 2 + time_band) * (rows // 2) + pair) * 2 + row_band
                    even, uneven = columns_apart(line, pair_ref.at[slot % pair_ref.shape[0]])
                    for col_band in range(2):
                        value = even - uneven if col_band else even + uneven
                        value = value.astype(jnp.bfloat16)
                        band = 4 * time_band + 2 * row_band + col_band
                        if band:
                            held_ref[band - 1, index, pair] = value
                        else:
                            for target in range(bands):
                                low_ref[target, index, pair] = value[
                                    target * width : (target + 1) * width
                                ]
        copies.append(
            pltpu.make_async_copy(held_ref.at[:, index], high_ref.at[:, index], sems.at[index])
        )
        copies[-1].start()
    place = lax.axis_index("rows")
    for index, out_ref in enumerate(low_refs):
        out_ref[...] = low_ref[lax.bitwise_xor(place, index)]
    for copy in copies:
        copy.wait()


def low_kernel(*refs):
    *pieces, out_ref, sems = refs
    place = lax.axis_index("rows")
    rows = pieces[0].shape[1]
    copies = [
        pltpu.make_async_copy(
            piece, out_ref.at[:, pl.ds(lax.bitwise_xor(place, index) * rows, rows)], sems.at[index]
        )
        for index, piece in enumerate(pieces)
    ]
    for copy in copies:
        copy.start()
    for copy in copies:
        copy.wait()


def route(shift, pairs):
    frame_count, row_count = lax.axis_size("frames"), lax.axis_size("rows")
    return [
        (f * row_count + r, (f + shift) * row_count + s)
        for f in range(frame_count - shift)
        for r, s in pairs
    ]


def send(values, where):
    return lax.ppermute(values, ("frames", "rows"), where)


def share(stats):
    return lax.all_to_all(stats, ("frames", "rows"), 0, 0, tiled=True)


def half(*shape):
    return jax.ShapeDtypeStruct(shape, jnp.bfloat16)


def single(*shape):
    return jax.ShapeDtypeStruct(shape, jnp.float32)


def call(kernel, name, mib, ins, out_shape, scratch=(), cost=0, spaces=None, out_spaces=None):
    estimate = pl.CostEstimate(flops=cost, bytes_accessed=10**6, transcendentals=0)
    return pl.pallas_call(
        kernel,
        out_shape=out_shape,
        in_specs=spaces or [VMEM] * len(ins),
        out_specs=out_spaces or jax.tree.map(lambda _: VMEM, out_shape),
        scratch_shapes=list(scratch),
        compiler_params=pltpu.CompilerParams(vmem_limit_bytes=mib * 2**20),
        name=name,
        cost_estimate=estimate if cost else None,
    )(*ins)


def body(inputs, kernel_one, gain_one, offset_one, kernel_two, gain_two, offset_two, bias_two):
    frames, rows, cols, chans = inputs.shape
    bands = lax.axis_size("rows")
    devices = lax.axis_size("frames") * bands
    weights_one = kernel_one.reshape(3, 3, 3 * chans, chans)
    weights_two = kernel_two.reshape(3, 3, 3 * chans, chans)
    work = 2 * rows * cols * chans * 27 * chans
    to_near = route(0, [(r, r ^ 1) for r in range(bands)])
    to_far = route(0, [(r, ((r + 1) ^ 1) - 1) for r in range(1, bands - 1)])
    to_next = route(1, [(r, r) for r in range(bands)])

    def wide(count):
        return pltpu.VMEM((count, rows + 2, cols, 3 * chans), jnp.bfloat16)

    past, near, far = call(
        edges_kernel, "edges", 8, (inputs,),
        (half(LAGS, rows, cols, chans), half(frames, cols, chans), half(frames, cols, chans)),
        [pltpu.SemaphoreType.DMA((3,))], spaces=[HBM],
    )
    past, near, far = send(past, to_next), send(near, to_near), send(far, to_far)
    stats = call(stats_kernel, "stats_one", 8, (inputs,), single(devices, LANES), cost=10**10)
    stats = share(stats)
    near_past, far_past = call(
        past_edges_kernel, "past_edges", 8, (past,),
        (half(LAGS, cols, chans), half(LAGS, cols, chans)),
    )
    near_past, far_past = send(near_past, to_near), send(far_past, to_far)
    affine = (gain_one[None], offset_one[None])
    later, sums = call(
        first_kernel_own, "conv_one_own", 32,
        (inputs, near, far, stats, *affine, weights_one),
        (half(frames - 2, rows, cols, chans), single(8, chans)),
        [wide(frames)], cost=work * (frames - 2),
    )
    edge = half(frames + 2, cols, chans)
    hidden, stats, near, far = call(
        first_kernel_past, "conv_one_past", 32,
        (
            inputs, near, far, past, near_past, far_past, stats, *affine, weights_one, later, sums,
        ),
        (half(LAGS, rows, cols, chans), single(devices, LANES), edge, edge),
        [wide(LAGS + 2)], cost=work * LAGS,
    )
    near, far = send(near, to_near), send(far, to_far)
    stats = share(stats)
    piece = half(frames // 2, rows // 2, cols // 2 // bands, chans)
    high = half(7, frames // 2, rows // 2, cols // 2, chans)
    *pieces, high = call(
        second_kernel, "conv_two", 32,
        (
            hidden, later, near, far, stats, gain_two[None], offset_two[None], weights_two, inputs,
            bias_two[None],
        ),
        (*[piece] * bands, high),
        [
            wide(frames + 2), pltpu.VMEM((8, chans // LANES, cols, LANES), jnp.float32),
            pltpu.VMEM((bands, *piece.shape), jnp.bfloat16), pltpu.VMEM(high.shape, jnp.bfloat16),
            pltpu.SemaphoreType.DMA((frames // 2,)),
        ],
        cost=work * frames, out_spaces=(*[VMEM] * bands, HBM),
    )
    pieces = pieces[:1] + [
        send(pieces[k], route(0, [(r, r ^ k) for r in range(bands)])) for k in range(1, bands)
    ]
    low = call(
        low_kernel, "low_rows", 8, pieces,
        half(frames // 2, bands * (rows // 2), cols // 2 // bands, chans),
        [pltpu.SemaphoreType.DMA((bands,))], out_spaces=HBM,
    )
    return low, high


def solution(mesh):
    in_specs = (P("frames", "rows", None, None), P(), P(), P(), P(), P(), P(), P())
    out_specs = (P("frames", None, "rows", None), P(None, "frames", "rows", None, None))
    return jax.shard_map(body, mesh=mesh, in_specs=in_specs, out_specs=out_specs, check_vma=False)
```

time: 383 us -> 76.7 us (0.20)
  blocking collectives: 261 us -> 14.2 us
  local copies, waits for them, and re-layouts: 32.2 us -> 3.26 us
  matrix products: 24.4 us -> 0 us
  Pallas kernels: 0 us -> 22.6 us
  waiting for transfers between devices: 24.3 us -> 8.03 us
  other arithmetic: 12.7 us -> 0 us
  starting transfers between devices: 23.1 us -> 27.3 us
    psum x4 -> x0, blocking collectives: 261 us -> none  [the longest x2 136 us: norm_stats(): total = lax.psum(jnp.sum(grouped, axis=(0, 1, 2, 4)), ('frames', 'rows'))]
    dot_general x18 -> x0, matrix products: 24.4 us -> none  [conv_valid(): jnp.dot(window, kernel_rows[lag_time, lag_row], preferred_element_type=jn...]
    pallas_call x0 -> x7, Pallas kernels: none -> 22.6 us  [call(): pl.pallas_call(kernel, out_shape=out_shape, in_specs=spaces or [VMEM] * l...]
    ppermute x6 -> x10, waiting for transfers between devices: 22.7 us -> 2.31 us  [send(): return lax.ppermute(values, ('frames', 'rows'), where)]
    slice x6 -> x0, local copies, waits for them, and re-layouts: 17.4 us -> none  [the longest x2 14.7 us: conv_valid(): widened[lag_time:lag_time + frames_out, lag_row:lag_row + rows_out]]
    all_to_all x0 -> x1, blocking collectives: none -> 14.2 us  [share(): return lax.all_to_all(stats, ('frames', 'rows'), 0, 0, tiled=True)]
    unnamed x34 -> x20, local copies, waits for them, and re-layouts: 8.96 us -> 3.26 us
    all_to_all x1, starting transfers between devices: 3.31 us -> 8.9 us  [share(): return lax.all_to_all(stats, ('frames', 'rows'), 0, 0, tiled=True)]
  transfers between devices with their start and end apart: 7 -> 11, of which waited for: 7 -> 3; matrix products, arithmetic and copies ran while one was open for 0% -> 0% of each run, Pallas kernels for 0% -> 11%
where the time goes in v3:
time: 76.7 us; the launch traced here: 76.4 us
  starting transfers between devices  27.3 us (36%)
  Pallas kernels  22.6 us (29%)
  blocking collectives  14.2 us (19%)
  waiting for transfers between devices  8.03 us (10%)
  local copies, waits for them, and re-layouts  3.26 us (4%)
  between operations  1.03 us (1%)
    pallas_call x7, Pallas kernels, call(): pl.pallas_call(kernel, out_shape=out_shape, in_specs=spaces or [VMEM] * l...  22.6 us
    ppermute x10, starting transfers between devices, send(): return lax.ppermute(values, ('frames', 'rows'), where)  18.4 us
    all_to_all x1, blocking collectives, share(): return lax.all_to_all(stats, ('frames', 'rows'), 0, 0, tiled=True)  14.2 us
    all_to_all x1, starting transfers between devices, share(): return lax.all_to_all(stats, ('frames', 'rows'), 0, 0, tiled=True)  8.9 us
    all_to_all x1, waiting for transfers between devices, share(): return lax.all_to_all(stats, ('frames', 'rows'), 0, 0, tiled=True)  5.72 us
    unnamed x20, local copies, waits for them, and re-layouts  3.26 us
    ppermute x10, waiting for transfers between devices, send(): return lax.ppermute(values, ('frames', 'rows'), where)  2.31 us
  transfers between devices with their start and end apart: 11, of which 3 were waited for; matrix products, arithmetic and copies ran while one was open for 0% of the time, Pallas kernels for 11%

profile of v3, /device:TPU:1, one launch (start us, length us, event | category | flops | bytes accessed | tf_op | source)
XLA Modules:
  0.0 76.4 jit_solution(3740251514629941060)
XLA Ops:
  0.6 0.0 copy-start
  0.6 1.2 %copy-done = bf16[8,4,64,256]{3,2,1,0:T(8,128)(2,1)S(1)} copy-done((bf16[8,4,64,256]{3,2,1,0:T(8,128)(2,1)S(1)}, bf16[8,4,64,256]{3,2,1,0:T(8,128)(2,1)}, u32[]{:S(2)}) %copy-start) | copy-done | bytes 1048600
  1.9 0.1 edges.1
  2.0 1.5 %collective-permute-start = (bf16[8,64,256]{2,1,0:T(8,128)(2,1)S(1)}, bf16[8,64,256]{2,1,0:T(8,128)(2,1)S(1)}, u32[]{:S(2)}, u32[]{:S(2)}) collective-permute-start(bf16[8,64,256]{2,1,0:T(8,128)(2,1)S(1)} %get-tuple-element.18), channel_id=1, source_target_pairs={{0,1},{1,0},{2,3},{3,2},{4,5},{5,4},{6,7},{7,6},{8,9},{9,8},{10,11... | collective-permute-start | bytes 786440 | tf_op jit(solution)/shard_map/ppermute | solution.py:323
  3.5 3.1 %collective-permute-start.1 = (bf16[8,64,256]{2,1,0:T(8,128)(2,1)S(1)}, bf16[8,64,256]{2,1,0:T(8,128)(2,1)S(1)}, u32[]{:S(2)}, u32[]{:S(2)}) collective-permute-start(bf16[8,64,256]{2,1,0:T(8,128)(2,1)S(1)} %get-tuple-element.19), channel_id=1, source_target_pairs={{1,2},{2,1},{5,6},{6,5},{9,10},{10,9},{13,14},{14,13},{17,18},{18,... | collective-permute-start | bytes 786440 | tf_op jit(solution)/shard_map/ppermute | solution.py:323
  6.6 0.0 copy-start.1
  6.6 0.0 copy-start.5
  6.6 0.0 copy-start.6
  6.6 4.5 %collective-permute-start.2 = (bf16[4,4,64,256]{3,2,1,0:T(8,128)(2,1)S(1)}, bf16[4,4,64,256]{3,2,1,0:T(8,128)(2,1)S(1)}, u32[]{:S(2)}, u32[]{:S(2)}) collective-permute-start(bf16[4,4,64,256]{3,2,1,0:T(8,128)(2,1)S(1)} %get-tuple-element.20), channel_id=1, source_target_pairs={{0,4},{1,5},{2,6},{3,7},{4,8},{5,9},{6,10},{7,11},{8,12},{9,13},{1... | collective-permute-start | bytes 1572872 | tf_op jit(solution)/shard_map/ppermute | solution.py:323
  11.1 1.9 %stats_one.1 = f32[128,128]{1,0:T(8,128)} custom-call(bf16[8,4,64,256]{3,2,1,0:T(8,128)(2,1)S(1)} %copy-done), custom_call_target="tpu_custom_call" | custom-call | flops 10000000000 | bytes 1000000 | tf_op jit(solution)/shard_map/stats_one/pallas_call | solution.py:340
  13.0 8.9 %all-to-all-start = ((f32[128,1,128]{2,1,0:T(1,128)}), f32[128,1,128]{2,1,0:T(1,128)S(1)}, u32[]{:S(2)}, u32[]{:S(2)}) async-start(f32[128,1,128]{2,1,0:T(1,128)} %bitcast.1), calls=%async_computation | async-start | bytes 131072 | tf_op jit(solution)/shard_map/all_to_all | solution.py:327
  21.9 0.0 collective-permute-done.2.past_ref
  22.0 1.1 %collective-permute-start.3 = (bf16[4,64,256]{2,1,0:T(8,128)(2,1)S(1)}, bf16[4,64,256]{2,1,0:T(8,128)(2,1)S(1)}, u32[]{:S(2)}, u32[]{:S(2)}) collective-permute-start(bf16[4,64,256]{2,1,0:T(8,128)(2,1)S(1)} %get-tuple-element.21), channel_id=1, source_target_pairs={{0,1},{1,0},{2,3},{3,2},{4,5},{5,4},{6,7},{7,6},{8,9},{9,8},{10,11... | collective-permute-start | bytes 393224 | tf_op jit(solution)/shard_map/ppermute | solution.py:323
  23.1 2.6 %collective-permute-start.4 = (bf16[4,64,256]{2,1,0:T(8,128)(2,1)S(1)}, bf16[4,64,256]{2,1,0:T(8,128)(2,1)S(1)}, u32[]{:S(2)}, u32[]{:S(2)}) collective-permute-start(bf16[4,64,256]{2,1,0:T(8,128)(2,1)S(1)} %get-tuple-element.22), channel_id=1, source_target_pairs={{1,2},{2,1},{5,6},{6,5},{9,10},{10,9},{13,14},{14,13},{17,18},{18,... | collective-permute-start | bytes 393224 | tf_op jit(solution)/shard_map/ppermute | solution.py:323
  25.7 5.7 %all-to-all-done = f32[128,1,128]{2,1,0:T(1,128)S(1)} async-done(((f32[128,1,128]{2,1,0:T(1,128)}), f32[128,1,128]{2,1,0:T(1,128)S(1)}, u32[]{:S(2)}, u32[]{:S(2)}) %all-to-all-start) | async-done | bytes 65568 | tf_op jit(solution)/shard_map/all_to_all | solution.py:327
  31.5 0.0 collective-permute-done.near_ref
  31.5 0.0 collective-permute-done.1.far_ref
  31.5 0.0 copy-done.1
  31.5 0.0 copy-done.5
  31.5 0.0 copy-done.6
  31.5 0.0 copy-start.2
  31.5 2.0 %copy-done.2 = bf16[3,3,3,256,256]{4,3,2,1,0:T(8,128)(2,1)S(1)} copy-done((bf16[3,3,3,256,256]{4,3,2,1,0:T(8,128)(2,1)S(1)}, bf16[3,3,3,256,256]{4,3,2,1,0:T(8,128)(2,1)}, u32[]{:S(2)}) %copy-start.2) | copy-done | bytes 3538968
  33.5 0.0 copy-start.3
  33.5 6.3 %conv_one_own.1 = (bf16[6,4,64,256]{3,2,1,0:T(8,128)(2,1)S(1)}, f32[8,256]{1,0:T(8,128)S(1)}) custom-call(bf16[8,4,64,256]{3,2,1,0:T(8,128)(2,1)S(1)} %copy-done.1, bf16[8,64,256]{2,1,0:T(8,128)(2,1)S(1)} %collective-permute-done.near_ref, bf16[8,64,256]{2,1,0:T(8,128)(2,1)S(1)} %collective-permute-done.1.far_ref, f32[128,128]{1,0:T(8,128)S(1)} %bitcast.15, ...), custom_call_target="tpu_custom_call" | custom-call | flops 5435817984 | bytes 1000000 | tf_op jit(solution)/shard_map/conv_one_own/pallas_call | solution.py:340
  39.8 0.0 collective-permute-done.3.near_past_ref
  39.8 0.0 collective-permute-done.4.far_past_ref
  39.8 0.0 copy-done.3
  39.8 0.0 copy-start.4
  39.8 0.0 copy-start.7
  39.9 0.0 copy-start.8
  39.9 0.0 copy-start.9
  39.9 4.7 %conv_one_past.1 = (bf16[4,4,64,256]{3,2,1,0:T(8,128)(2,1)S(1)}, f32[128,128]{1,0:T(8,128)S(1)}, bf16[10,64,256]{2,1,0:T(8,128)(2,1)S(1)}, bf16[10,64,256]{2,1,0:T(8,128)(2,1)S(1)}) custom-call(bf16[8,4,64,256]{3,2,1,0:T(8,128)(2,1)S(1)} %copy-done.1, bf16[8,64,256]{2,1,0:T(8,128)(2,1)S(1)} %collective-permute-done.near_ref, ...), custom_call_target="tpu_custom_call" | custom-call | flops 3623878656 | bytes 1000000 | tf_op jit(solution)/shard_map/conv_one_past/pallas_call | solution.py:340
  44.6 0.8 %collective-permute-start.5 = (bf16[10,64,256]{2,1,0:T(8,128)(2,1)S(1)}, bf16[10,64,256]{2,1,0:T(8,128)(2,1)S(1)}, u32[]{:S(2)}, u32[]{:S(2)}) collective-permute-start(bf16[10,64,256]{2,1,0:T(8,128)(2,1)S(1)} %get-tuple-element.26), channel_id=1, source_target_pairs={{0,1},{1,0},{2,3},{3,2},{4,5},{5,4},{6,7},{7,6},{8,9},{9,8},{10,11... | collective-permute-start | bytes 983048 | tf_op jit(solution)/shard_map/ppermute | solution.py:323
  45.4 2.1 %collective-permute-start.6 = (bf16[10,64,256]{2,1,0:T(8,128)(2,1)S(1)}, bf16[10,64,256]{2,1,0:T(8,128)(2,1)S(1)}, u32[]{:S(2)}, u32[]{:S(2)}) collective-permute-start(bf16[10,64,256]{2,1,0:T(8,128)(2,1)S(1)} %get-tuple-element.27), channel_id=1, source_target_pairs={{1,2},{2,1},{5,6},{6,5},{9,10},{10,9},{13,14},{14,13},{17,18},{18,... | collective-permute-start | bytes 983048 | tf_op jit(solution)/shard_map/ppermute | solution.py:323
  47.5 14.2 %all_to_all.22 = f32[128,1,128]{2,1,0:T(1,128)S(1)} all-to-all(f32[128,1,128]{2,1,0:T(1,128)S(1)} %bitcast.17), channel_id=1, replica_groups=mesh['frames'=32,'rows'=4] {'frames','rows'}, dimensions={0} | all-to-all | bytes 131072 | tf_op jit(solution)/shard_map/all_to_all | solution.py:327
  61.7 0.0 collective-permute-done.5.near_ref
  61.7 0.0 collective-permute-done.6.far_ref
  61.7 0.0 copy-done.4
  61.7 0.0 copy-done.7
  61.7 0.0 copy-done.8
  61.7 0.0 copy-done.9
  61.7 8.9 %conv_two.1 = (bf16[4,2,8,256]{3,2,1,0:T(8,128)(2,1)S(1)}, bf16[4,2,8,256]{3,2,1,0:T(8,128)(2,1)S(1)}, bf16[4,2,8,256]{3,2,1,0:T(8,128)(2,1)S(1)}, bf16[4,2,8,25...) custom-call(bf16[4,4,64,256]{3,2,1,0:T(8,128)(2,1)S(1)} %get-tuple-element.25.hidden_ref, ...), custom_call_target="tpu_custom_call" | custom-call | flops 7247757312 | bytes 1000000 | tf_op jit(solution)/shard_map/conv_two/pallas_call | solution.py:340
  70.7 0.8 %collective-permute-start.7 = (bf16[4,2,8,256]{3,2,1,0:T(8,128)(2,1)S(1)}, bf16[4,2,8,256]{3,2,1,0:T(8,128)(2,1)S(1)}, u32[]{:S(2)}, u32[]{:S(2)}) collective-permute-start(bf16[4,2,8,256]{3,2,1,0:T(8,128)(2,1)S(1)} %get-tuple-element.30), channel_id=1, source_target_pairs={{0,1},{1,0},{2,3},{3,2},{4,5},{5,4},{6,7},{7,6},{8,9},{9,8},{10,11... | collective-permute-start | bytes 98312 | tf_op jit(solution)/shard_map/ppermute | solution.py:323
  71.5 0.3 collective-permute-start.8
  71.8 1.4 %collective-permute-start.9 = (bf16[4,2,8,256]{3,2,1,0:T(8,128)(2,1)S(1)}, bf16[4,2,8,256]{3,2,1,0:T(8,128)(2,1)S(1)}, u32[]{:S(2)}, u32[]{:S(2)}) collective-permute-start(bf16[4,2,8,256]{3,2,1,0:T(8,128)(2,1)S(1)} %get-tuple-element.32), channel_id=1, source_target_pairs={{0,3},{1,2},{2,1},{3,0},{4,7},{5,6},{6,5},{7,4},{8,11},{9,10},{10,... | collective-permute-start | bytes 98312 | tf_op jit(solution)/shard_map/ppermute | solution.py:323
  73.2 0.0 collective-permute-done.7.refs_1_
  73.2 1.1 %collective-permute-done.8.refs_2_ = bf16[4,2,8,256]{3,2,1,0:T(8,128)(2,1)S(1)} collective-permute-done((bf16[4,2,8,256]{3,2,1,0:T(8,128)(2,1)S(1)}, bf16[4,2,8,256]{3,2,1,0:T(8,128)(2,1)S(1)}, u32[]{:S(2)}, u32[]{:S(2)}) %collective-permute-start.8) | collective-permute-done | bytes 32800 | tf_op jit(solution)/shard_map/ppermute | solution.py:323
  74.3 1.2 %collective-permute-done.9.refs_3_ = bf16[4,2,8,256]{3,2,1,0:T(8,128)(2,1)S(1)} collective-permute-done((bf16[4,2,8,256]{3,2,1,0:T(8,128)(2,1)S(1)}, bf16[4,2,8,256]{3,2,1,0:T(8,128)(2,1)S(1)}, u32[]{:S(2)}, u32[]{:S(2)}) %collective-permute-start.9) | collective-permute-done | bytes 32800 | tf_op jit(solution)/shard_map/ppermute | solution.py:323
  75.5 0.7 low_rows.1
  (1 shorter events, 0.0 us)
Async XLA Ops:
  0.6 1.2 %copy-start = (bf16[8,4,64,256]{3,2,1,0:T(8,128)(2,1)S(1)}, bf16[8,4,64,256]{3,2,1,0:T(8,128)(2,1)}, u32[]{:S(2)}) copy-start(bf16[8,4,64,256]{3,2,1,0:T(8,128)(2,1)} %source_ref.1) | copy-start | bytes 3145732
  2.0 29.5 %collective-permute-start = (bf16[8,64,256]{2,1,0:T(8,128)(2,1)S(1)}, bf16[8,64,256]{2,1,0:T(8,128)(2,1)S(1)}, u32[]{:S(2)}, u32[]{:S(2)}) collective-permute-start(bf16[8,64,256]{2,1,0:T(8,128)(2,1)S(1)} %get-tuple-element.18), channel_id=1, source_target_pairs={{0,1},{1,0},{2,3},{3,2},{4,5},{5,4},{6,7},{7,6},{8,9},{9,8},{10,11... | collective-permute-start | bytes 786440 | tf_op jit(solution)/shard_map/ppermute | solution.py:323
  3.5 28.0 %collective-permute-start.1 = (bf16[8,64,256]{2,1,0:T(8,128)(2,1)S(1)}, bf16[8,64,256]{2,1,0:T(8,128)(2,1)S(1)}, u32[]{:S(2)}, u32[]{:S(2)}) collective-permute-start(bf16[8,64,256]{2,1,0:T(8,128)(2,1)S(1)} %get-tuple-element.19), channel_id=1, source_target_pairs={{1,2},{2,1},{5,6},{6,5},{9,10},{10,9},{13,14},{14,13},{17,18},{18,... | collective-permute-start | bytes 786440 | tf_op jit(solution)/shard_map/ppermute | solution.py:323
  6.6 24.9 %copy-start.1 = (bf16[8,4,64,256]{3,2,1,0:T(8,128)(2,1)S(1)}, bf16[8,4,64,256]{3,2,1,0:T(8,128)(2,1)}, u32[]{:S(2)}) copy-start(bf16[8,4,64,256]{3,2,1,0:T(8,128)(2,1)} %source_ref.1) | copy-start | bytes 3145732
  6.6 24.9 %copy-start.5 = (f32[256]{0:T(256)S(1)}, f32[256]{0:T(256)}, u32[]{:S(2)}) copy-start(f32[256]{0:T(256)} %param.10) | copy-start | bytes 3076
  6.6 24.9 %copy-start.6 = (f32[256]{0:T(256)S(1)}, f32[256]{0:T(256)}, u32[]{:S(2)}) copy-start(f32[256]{0:T(256)} %param.11) | copy-start | bytes 3076
  6.6 15.3 %collective-permute-start.2 = (bf16[4,4,64,256]{3,2,1,0:T(8,128)(2,1)S(1)}, bf16[4,4,64,256]{3,2,1,0:T(8,128)(2,1)S(1)}, u32[]{:S(2)}, u32[]{:S(2)}) collective-permute-start(bf16[4,4,64,256]{3,2,1,0:T(8,128)(2,1)S(1)} %get-tuple-element.20), channel_id=1, source_target_pairs={{0,4},{1,5},{2,6},{3,7},{4,8},{5,9},{6,10},{7,11},{8,12},{9,13},{1... | collective-permute-start | bytes 1572872 | tf_op jit(solution)/shard_map/ppermute | solution.py:323
  13.0 18.4 %all-to-all-start = ((f32[128,1,128]{2,1,0:T(1,128)}), f32[128,1,128]{2,1,0:T(1,128)S(1)}, u32[]{:S(2)}, u32[]{:S(2)}) async-start(f32[128,1,128]{2,1,0:T(1,128)} %bitcast.1), calls=%async_computation | async-start | bytes 131072 | tf_op jit(solution)/shard_map/all_to_all | solution.py:327
  22.0 17.8 %collective-permute-start.3 = (bf16[4,64,256]{2,1,0:T(8,128)(2,1)S(1)}, bf16[4,64,256]{2,1,0:T(8,128)(2,1)S(1)}, u32[]{:S(2)}, u32[]{:S(2)}) collective-permute-start(bf16[4,64,256]{2,1,0:T(8,128)(2,1)S(1)} %get-tuple-element.21), channel_id=1, source_target_pairs={{0,1},{1,0},{2,3},{3,2},{4,5},{5,4},{6,7},{7,6},{8,9},{9,8},{10,11... | collective-permute-start | bytes 393224 | tf_op jit(solution)/shard_map/ppermute | solution.py:323
  23.1 16.7 %collective-permute-start.4 = (bf16[4,64,256]{2,1,0:T(8,128)(2,1)S(1)}, bf16[4,64,256]{2,1,0:T(8,128)(2,1)S(1)}, u32[]{:S(2)}, u32[]{:S(2)}) collective-permute-start(bf16[4,64,256]{2,1,0:T(8,128)(2,1)S(1)} %get-tuple-element.22), channel_id=1, source_target_pairs={{1,2},{2,1},{5,6},{6,5},{9,10},{10,9},{13,14},{14,13},{17,18},{18,... | collective-permute-start | bytes 393224 | tf_op jit(solution)/shard_map/ppermute | solution.py:323
  31.5 2.0 %copy-start.2 = (bf16[3,3,3,256,256]{4,3,2,1,0:T(8,128)(2,1)S(1)}, bf16[3,3,3,256,256]{4,3,2,1,0:T(8,128)(2,1)}, u32[]{:S(2)}) copy-start(bf16[3,3,3,256,256]{4,3,2,1,0:T(8,128)(2,1)} %param.9) | copy-start | bytes 10616836
  33.5 6.3 %copy-start.3 = (bf16[3,3,3,256,256]{4,3,2,1,0:T(8,128)(2,1)S(1)}, bf16[3,3,3,256,256]{4,3,2,1,0:T(8,128)(2,1)}, u32[]{:S(2)}) copy-start(bf16[3,3,3,256,256]{4,3,2,1,0:T(8,128)(2,1)} %param.9) | copy-start | bytes 10616836
  39.8 21.8 %copy-start.4 = (bf16[3,3,3,256,256]{4,3,2,1,0:T(8,128)(2,1)S(1)}, bf16[3,3,3,256,256]{4,3,2,1,0:T(8,128)(2,1)}, u32[]{:S(2)}) copy-start(bf16[3,3,3,256,256]{4,3,2,1,0:T(8,128)(2,1)} %param.12) | copy-start | bytes 10616836
  39.8 21.8 %copy-start.7 = (f32[256]{0:T(256)S(1)}, f32[256]{0:T(256)}, u32[]{:S(2)}) copy-start(f32[256]{0:T(256)} %param.13) | copy-start | bytes 3076
  39.9 21.8 %copy-start.8 = (f32[256]{0:T(256)S(1)}, f32[256]{0:T(256)}, u32[]{:S(2)}) copy-start(f32[256]{0:T(256)} %param.14) | copy-start | bytes 3076
  39.9 21.8 %copy-start.9 = (f32[256]{0:T(256)S(1)}, f32[256]{0:T(256)}, u32[]{:S(2)}) copy-start(f32[256]{0:T(256)} %param.15) | copy-start | bytes 3076
  44.6 17.1 %collective-permute-start.5 = (bf16[10,64,256]{2,1,0:T(8,128)(2,1)S(1)}, bf16[10,64,256]{2,1,0:T(8,128)(2,1)S(1)}, u32[]{:S(2)}, u32[]{:S(2)}) collective-permute-start(bf16[10,64,256]{2,1,0:T(8,128)(2,1)S(1)} %get-tuple-element.26), channel_id=1, source_target_pairs={{0,1},{1,0},{2,3},{3,2},{4,5},{5,4},{6,7},{7,6},{8,9},{9,8},{10,11... | collective-permute-start | bytes 983048 | tf_op jit(solution)/shard_map/ppermute | solution.py:323
  45.4 16.3 %collective-permute-start.6 = (bf16[10,64,256]{2,1,0:T(8,128)(2,1)S(1)}, bf16[10,64,256]{2,1,0:T(8,128)(2,1)S(1)}, u32[]{:S(2)}, u32[]{:S(2)}) collective-permute-start(bf16[10,64,256]{2,1,0:T(8,128)(2,1)S(1)} %get-tuple-element.27), channel_id=1, source_target_pairs={{1,2},{2,1},{5,6},{6,5},{9,10},{10,9},{13,14},{14,13},{17,18},{18,... | collective-permute-start | bytes 983048 | tf_op jit(solution)/shard_map/ppermute | solution.py:323
  70.7 2.6 %collective-permute-start.7 = (bf16[4,2,8,256]{3,2,1,0:T(8,128)(2,1)S(1)}, bf16[4,2,8,256]{3,2,1,0:T(8,128)(2,1)S(1)}, u32[]{:S(2)}, u32[]{:S(2)}) collective-permute-start(bf16[4,2,8,256]{3,2,1,0:T(8,128)(2,1)S(1)} %get-tuple-element.30), channel_id=1, source_target_pairs={{0,1},{1,0},{2,3},{3,2},{4,5},{5,4},{6,7},{7,6},{8,9},{9,8},{10,11... | collective-permute-start | bytes 98312 | tf_op jit(solution)/shard_map/ppermute | solution.py:323
  71.5 2.8 %collective-permute-start.8 = (bf16[4,2,8,256]{3,2,1,0:T(8,128)(2,1)S(1)}, bf16[4,2,8,256]{3,2,1,0:T(8,128)(2,1)S(1)}, u32[]{:S(2)}, u32[]{:S(2)}) collective-permute-start(bf16[4,2,8,256]{3,2,1,0:T(8,128)(2,1)S(1)} %get-tuple-element.31), channel_id=1, source_target_pairs={{0,2},{1,3},{2,0},{3,1},{4,6},{5,7},{6,4},{7,5},{8,10},{9,11},{10,... | collective-permute-start | bytes 98312 | tf_op jit(solution)/shard_map/ppermute | solution.py:323
  71.8 3.7 %collective-permute-start.9 = (bf16[4,2,8,256]{3,2,1,0:T(8,128)(2,1)S(1)}, bf16[4,2,8,256]{3,2,1,0:T(8,128)(2,1)S(1)}, u32[]{:S(2)}, u32[]{:S(2)}) collective-permute-start(bf16[4,2,8,256]{3,2,1,0:T(8,128)(2,1)S(1)} %get-tuple-element.32), channel_id=1, source_target_pairs={{0,3},{1,2},{2,1},{3,0},{4,7},{5,6},{6,5},{7,4},{8,11},{9,10},{10,... | collective-permute-start | bytes 98312 | tf_op jit(solution)/shard_map/ppermute | solution.py:323

commit v4 on v3

v4 whole, which is shorter than its diff:
```python
import functools

import jax
import jax.numpy as jnp
from jax import lax
from jax.experimental import pallas as pl
from jax.experimental.pallas import tpu as pltpu
from jax.sharding import PartitionSpec as P

GROUPS = 32
EPS = 1e-06
LANES = 128
LAGS = 4
STEP = 2
VMEM = pl.BlockSpec(memory_space=pltpu.VMEM)
HBM = pl.BlockSpec(memory_space=pltpu.HBM)


def group_sums(values):
    lane = lax.broadcasted_iota(jnp.int32, values.shape, 1)
    for bit in (1, 2, 4):
        partner = jnp.where(
            jnp.bitwise_and(lane, bit) == 0,
            pltpu.roll(values, LANES - bit, 1),
            pltpu.roll(values, bit, 1),
        )
        values = values + partner
    return values


def channel_group_sums(sums):
    sums = jnp.sum(sums, axis=0, keepdims=True)
    halves = [sums[:, at : at + LANES] for at in range(0, sums.shape[1], LANES)]
    return jnp.concatenate(
        [group_sums(jnp.broadcast_to(part, (8, LANES)))[0:1] for part in halves], axis=1
    )


def folded(values):
    return values.astype(jnp.float32).reshape(-1, 8, values.shape[-1])


def put_stats(out_ref, total, squares, centre, count):
    mean = channel_group_sums(total) / count
    away = mean - centre
    spread = channel_group_sums(squares) - count * (away * away)
    kind = jnp.bitwise_and(lax.broadcasted_iota(jnp.int32, (1, LANES), 1), 7)
    row = jnp.zeros((1, LANES), jnp.float32)
    for index, part in enumerate(
        (mean[:, :LANES], spread[:, :LANES], mean[:, LANES:], spread[:, LANES:])
    ):
        row = jnp.where(kind == index, part, row)
    out_ref[...] = jnp.broadcast_to(row, out_ref.shape)


def norm_terms(stats_ref, gain_ref, count):
    stats = stats_ref[...]
    devices = stats.shape[0]
    average = jnp.sum(stats, axis=0, keepdims=True) / devices
    away = stats - average
    between = jnp.sum(away * away, axis=0, keepdims=True) / devices
    within = average / count
    kind = jnp.bitwise_and(lax.broadcasted_iota(jnp.int32, (8, LANES), 1), 7)
    row = lax.broadcasted_iota(jnp.int32, (8, LANES), 0)
    terms = jnp.zeros((8, LANES), jnp.float32)
    for index, (lane, part) in enumerate(
        ((0, average), (2, average), (0, between), (2, between))
    ):
        terms = jnp.where(jnp.logical_and(row == index, kind == lane), part, terms)
    for index, lane in ((2, 1), (3, 3)):
        terms = jnp.where(jnp.logical_and(row == index, kind == lane), within, terms)
    terms = group_sums(terms)
    mean = jnp.concatenate([terms[0:1], terms[1:2]], axis=1)
    var = jnp.concatenate([terms[2:3], terms[3:4]], axis=1)
    return mean, gain_ref[...] / jnp.sqrt(var + EPS)


def near_and_far(rows):
    odd = lax.rem(lax.axis_index("rows"), 2)
    return (1 - odd) * (rows - 1), odd * (rows - 1)


def has_past():
    return lax.axis_index("frames") > 0


class Window:
    def __init__(self, wide_ref, mean, scale, offset, cols):
        self.wide_ref = wide_ref
        self.terms = mean, scale, offset
        self.cols, self.chans = cols, wide_ref.shape[3]
        self.pairs = wide_ref.shape[2] // cols
        self.rows = 2 * self.pairs
        place = lax.axis_index("rows")
        self.odd = lax.rem(place, 2) == 1
        self.above = place > 0
        self.below = place < lax.axis_size("rows") - 1

    def active(self, value, valid):
        mean, scale, offset = self.terms
        value = (value.astype(jnp.float32) - mean) * scale + offset
        value = 0.5 * value * (1.0 + jnp.tanh(0.5 * value))
        return value if valid is None else jnp.where(valid, value, 0.0)

    def put(self, frame, body, near, far, valid):
        above, below = self.above, self.below
        if valid is not None:
            above, below = jnp.logical_and(above, valid), jnp.logical_and(below, valid)
        lines = [self.active(jnp.where(self.odd, near, far), above)]
        lines += [self.active(body[row], valid) for row in range(self.rows)]
        lines += [self.active(jnp.where(self.odd, far, near), below)]
        for pair in range(self.pairs):
            first, second, third, fourth = lines[2 * pair : 2 * pair + 4]
            mixed = (
                first - third, 0.5 * (second + third), 0.5 * (third - second), second - fourth
            )
            for index, value in enumerate(mixed):
                self.wide_ref[frame, index, pair * self.cols : (pair + 1) * self.cols] = (
                    value.astype(jnp.bfloat16)
                )

    def conv(self, start, count, kernel_ref, mixed_ref, mix=False):
        shape = (count * self.pairs, self.cols, -1)
        column = lax.broadcasted_iota(jnp.int32, (1, self.cols, 1), 1)
        totals = [None, None]
        for lag_col in (1, 0, 2):
            if mix:
                mix_taps(kernel_ref, mixed_ref, lag_col)
            terms = []
            for index in range(4):
                window = jnp.concatenate(
                    [
                        self.wide_ref[start + lag : start + lag + count, index].reshape(
                            -1, self.chans
                        )
                        for lag in range(3)
                    ],
                    axis=1,
                )
                if index in (0, 3):
                    taps = [kernel_ref[lag, 2 * (index // 3), lag_col] for lag in range(3)]
                else:
                    taps = [mixed_ref[index - 1, lag, lag_col] for lag in range(3)]
                terms.append(
                    jnp.dot(
                        window, jnp.concatenate(taps, axis=0), preferred_element_type=jnp.float32
                    )
                )
            middle = terms[1] - terms[2]
            parts = terms[0] + (terms[1] + terms[2]), middle - terms[3]
            for at, part in enumerate(parts):
                part = part.reshape(shape)
                if lag_col == 0:
                    part = jnp.where(column == 0, 0.0, pltpu.roll(part, 1, 1))
                if lag_col == 2:
                    part = jnp.where(
                        column == self.cols - 1, 0.0, pltpu.roll(part, self.cols - 1, 1)
                    )
                totals[at] = part if totals[at] is None else totals[at] + part
        return [
            [totals[row % 2][frame * self.pairs + row // 2] for row in range(self.rows)]
            for frame in range(count)
        ]


def mix_taps(kernel_ref, mixed_ref, lag_col):
    for lag in range(3):
        first, second, third = (
            kernel_ref[lag, row, lag_col].astype(jnp.float32) for row in range(3)
        )
        outer = first + third
        mixed_ref[0, lag, lag_col] = (outer + second).astype(jnp.bfloat16)
        mixed_ref[1, lag, lag_col] = (outer - second).astype(jnp.bfloat16)


def edges_kernel(values_ref, past_ref, near_ref, far_ref, sems):
    frames, rows = values_ref.shape[:2]
    near, far = near_and_far(rows)
    pairs = (
        (values_ref.at[pl.ds(frames - LAGS, LAGS)], past_ref),
        (values_ref.at[:, near], near_ref),
        (values_ref.at[:, far], far_ref),
    )
    copies = [pltpu.make_async_copy(*pair, sems.at[i]) for i, pair in enumerate(pairs)]
    for copy in copies:
        copy.start()
    for copy in copies:
        copy.wait()


def past_edges_kernel(past_ref, near_ref, far_ref):
    near, far = near_and_far(past_ref.shape[1])
    near_ref[...] = past_ref[:, near]
    far_ref[...] = past_ref[:, far]


def stats_kernel(values_ref, out_ref):
    frames, rows, cols, chans = values_ref.shape
    count = float(frames * rows * cols * (chans // GROUPS))
    zero = jnp.zeros((8, chans), jnp.float32)

    def add(index, total):
        return total + jnp.sum(folded(values_ref[index]), axis=0)

    total = lax.fori_loop(0, frames, add, zero)
    centre = channel_group_sums(total) / count

    def add_square(index, total):
        away = folded(values_ref[index]) - centre
        return total + jnp.sum(away * away, axis=0)

    squares = lax.fori_loop(0, frames, add_square, zero)
    put_stats(out_ref, total, squares, centre, count)


def group_count(frames, rows, cols, chans):
    return float(frames * rows * cols * (chans // GROUPS))


def first_kernel_own(
    own_ref, near_ref, far_ref, stats_ref, gain_ref, offset_ref, kernel_ref,
    hidden_ref, sums_ref, mixed_ref, wide_ref,
):
    frames, rows, cols, chans = own_ref.shape
    mean, scale = norm_terms(stats_ref, gain_ref, group_count(*own_ref.shape))
    window = Window(wide_ref, mean, scale, offset_ref[...], cols)
    total = jnp.zeros((8, chans), jnp.float32)
    for frame in range(frames):
        window.put(frame, own_ref.at[frame], near_ref[frame], far_ref[frame], None)
        if frame < STEP + 1 or (frame - 1) % STEP:
            continue
        start = frame - 1 - STEP
        conv = window.conv(start, STEP, kernel_ref, mixed_ref, mix=start == 0)
        for at in range(STEP):
            for row in range(rows):
                hidden = conv[at][row].astype(jnp.bfloat16)
                hidden_ref[start + at, row] = hidden
                total = total + jnp.sum(folded(hidden), axis=0)
    sums_ref[...] = total


def first_kernel_past(
    own_ref, near_ref, far_ref, past_ref, near_past_ref, far_past_ref,
    stats_ref, gain_ref, offset_ref, kernel_ref, later_ref, sums_ref, mixed_ref,
    hidden_ref, out_stats_ref, out_near_ref, out_far_ref, wide_ref,
):
    frames, rows, cols, chans = own_ref.shape
    count = group_count(*own_ref.shape)
    mean, scale = norm_terms(stats_ref, gain_ref, count)
    window = Window(wide_ref, mean, scale, offset_ref[...], cols)
    sums = sums_ref[...]
    centre = channel_group_sums(sums) / group_count(*later_ref.shape)
    squares = jnp.zeros((8, chans), jnp.float32)

    def square(block):
        away = folded(block) - centre
        return jnp.sum(away * away, axis=0)

    for frame in range(LAGS + 2):
        own = frame - LAGS
        if own < 0:
            window.put(
                frame, past_ref.at[frame], near_past_ref[frame], far_past_ref[frame], has_past()
            )
        else:
            window.put(frame, own_ref.at[own], near_ref[own], far_ref[own], None)
        squares = squares + square(later_ref[frame])
        if frame < STEP + 1 or (frame - 1) % STEP:
            continue
        start = frame - 1 - STEP
        conv = window.conv(start, STEP, kernel_ref, mixed_ref)
        for at in range(STEP):
            for row in range(rows):
                hidden = conv[at][row].astype(jnp.bfloat16)
                hidden_ref[start + at, row] = hidden
                if start + at >= 2:
                    squares = squares + square(hidden)
                    sums = sums + jnp.sum(folded(hidden), axis=0)
    put_stats(out_stats_ref, sums, squares, centre, count)
    near, far = near_and_far(rows)
    for source, out_ref in ((near, out_near_ref), (far, out_far_ref)):
        out_ref[0:LAGS] = hidden_ref[:, source]
        out_ref[LAGS:] = later_ref[:, source]


def columns_apart(line, pair_ref):
    cols, chans = line.shape
    halves = range(chans // LANES)
    for half in halves:
        pair_ref[half] = line[:, half * LANES : (half + 1) * LANES]
    return (
        jnp.concatenate([pair_ref[half, pl.ds(k, cols // 2, stride=2)] for half in halves], axis=1)
        for k in range(2)
    )


def second_kernel(
    hidden_ref, later_ref, near_ref, far_ref, stats_ref, gain_ref, offset_ref, kernel_ref,
    source_ref, bias_ref, *rest,
):
    *low_refs, high_ref, wide_ref, mixed_ref, pair_ref, low_ref, held_ref, sems = rest
    frames, rows, cols, chans = source_ref.shape
    mean, scale = norm_terms(stats_ref, gain_ref, group_count(*source_ref.shape))
    window = Window(wide_ref, mean, scale, offset_ref[...], cols)
    factor = 0.5**1.5
    bands = len(low_refs)
    width = cols // 2 // bands
    copies = []
    for frame in range(frames + 2):
        body = hidden_ref.at[frame] if frame < LAGS else later_ref.at[frame - LAGS]
        window.put(frame, body, near_ref[frame], far_ref[frame], has_past() if frame < 2 else None)
        if frame < 3 or frame % 2 == 0:
            continue
        start = frame - 3
        index = start // 2
        conv = window.conv(start, 2, kernel_ref, mixed_ref, mix=start == 0)
        summed = [
            [
                source_ref[start + at, row].astype(jnp.float32) + conv[at][row] + bias_ref[...]
                for row in range(rows)
            ]
            for at in range(2)
        ]
        for time_band in range(2):
            mixed = [
                before - after if time_band else before + after
                for before, after in zip(*summed, strict=True)
            ]
            for pair in range(rows // 2):
                upper, lower = mixed[2 * pair], mixed[2 * pair + 1]
                for row_band in range(2):
                    line = (upper - lower if row_band else upper + lower) * factor
                    slot = ((index * 2 + time_band) * (rows // 2) + pair) * 2 + row_band
                    even, uneven = columns_apart(line, pair_ref.at[slot % pair_ref.shape[0]])
                    for col_band in range(2):
                        value = even - uneven if col_band else even + uneven
                        value = value.astype(jnp.bfloat16)
                        band = 4 * time_band + 2 * row_band + col_band
                        if band:
                            held_ref[band - 1, index, pair] = value
                        else:
                            for target in range(bands):
                                low_ref[target, index, pair] = value[
                                    target * width : (target + 1) * width
                                ]
        copies.append(
            pltpu.make_async_copy(held_ref.at[:, index], high_ref.at[:, index], sems.at[index])
        )
        copies[-1].start()
    place = lax.axis_index("rows")
    for index, out_ref in enumerate(low_refs):
        out_ref[...] = low_ref[lax.bitwise_xor(place, index)]
    for copy in copies:
        copy.wait()


def low_kernel(*refs):
    *pieces, out_ref, sems = refs
    place = lax.axis_index("rows")
    rows = pieces[0].shape[1]
    copies = [
        pltpu.make_async_copy(
            piece, out_ref.at[:, pl.ds(lax.bitwise_xor(place, index) * rows, rows)], sems.at[index]
        )
        for index, piece in enumerate(pieces)
    ]
    for copy in copies:
        copy.start()
    for copy in copies:
        copy.wait()


def route(shift, pairs):
    frame_count, row_count = lax.axis_size("frames"), lax.axis_size("rows")
    return [
        (f * row_count + r, (f + shift) * row_count + s)
        for f in range(frame_count - shift)
        for r, s in pairs
    ]


def send(values, where):
    return lax.ppermute(values, ("frames", "rows"), where)


def share(stats):
    return lax.all_to_all(stats, ("frames", "rows"), 0, 0, tiled=True)


def half(*shape):
    return jax.ShapeDtypeStruct(shape, jnp.bfloat16)


def single(*shape):
    return jax.ShapeDtypeStruct(shape, jnp.float32)


def call(kernel, name, mib, ins, out_shape, scratch=(), cost=0, spaces=None, out_spaces=None):
    estimate = pl.CostEstimate(flops=cost, bytes_accessed=10**6, transcendentals=0)
    return pl.pallas_call(
        kernel,
        out_shape=out_shape,
        in_specs=spaces or [VMEM] * len(ins),
        out_specs=out_spaces or jax.tree.map(lambda _: VMEM, out_shape),
        scratch_shapes=list(scratch),
        compiler_params=pltpu.CompilerParams(vmem_limit_bytes=mib * 2**20),
        name=name,
        cost_estimate=estimate if cost else None,
    )(*ins)


def body(inputs, kernel_one, gain_one, offset_one, kernel_two, gain_two, offset_two, bias_two):
    frames, rows, cols, chans = inputs.shape
    bands = lax.axis_size("rows")
    devices = lax.axis_size("frames") * bands
    work = 2 * rows * cols * chans * 18 * chans
    to_near = route(0, [(r, r ^ 1) for r in range(bands)])
    to_far = route(0, [(r, ((r + 1) ^ 1) - 1) for r in range(1, bands - 1)])
    to_next = route(1, [(r, r) for r in range(bands)])

    def wide(count):
        return pltpu.VMEM((count, 4, rows // 2 * cols, chans), jnp.bfloat16)

    past, near, far = call(
        edges_kernel, "edges", 8, (inputs,),
        (half(LAGS, rows, cols, chans), half(frames, cols, chans), half(frames, cols, chans)),
        [pltpu.SemaphoreType.DMA((3,))], spaces=[HBM],
    )
    past, near, far = send(past, to_next), send(near, to_near), send(far, to_far)
    stats = call(stats_kernel, "stats_one", 8, (inputs,), single(devices, LANES), cost=10**10)
    past, stats = lax.optimization_barrier((past, share(stats)))
    near_past, far_past = call(
        past_edges_kernel, "past_edges", 8, (past,),
        (half(LAGS, cols, chans), half(LAGS, cols, chans)),
    )
    near_past, far_past = send(near_past, to_near), send(far_past, to_far)
    affine = (gain_one[None], offset_one[None])
    mixed = half(2, 3, 3, chans, chans)
    later, sums, mixed_one = call(
        first_kernel_own, "conv_one_own", 32,
        (inputs, near, far, stats, *affine, kernel_one),
        (half(frames - 2, rows, cols, chans), single(8, chans), mixed),
        [wide(frames)], cost=work * (frames - 2),
    )
    edge = half(frames + 2, cols, chans)
    hidden, stats, near, far = call(
        first_kernel_past, "conv_one_past", 32,
        (
            inputs, near, far, past, near_past, far_past, stats, *affine, kernel_one, later, sums,
            mixed_one,
        ),
        (half(LAGS, rows, cols, chans), single(devices, LANES), edge, edge),
        [wide(LAGS + 2)], cost=work * LAGS,
    )
    near, far = send(near, to_near), send(far, to_far)
    stats = share(stats)
    piece = half(frames // 2, rows // 2, cols // 2 // bands, chans)
    high = half(7, frames // 2, rows // 2, cols // 2, chans)
    *pieces, high = call(
        second_kernel, "conv_two", 32,
        (
            hidden, later, near, far, stats, gain_two[None], offset_two[None], kernel_two, inputs,
            bias_two[None],
        ),
        (*[piece] * bands, high),
        [
            wide(frames + 2), pltpu.VMEM(mixed.shape, jnp.bfloat16), pltpu.VMEM((8, chans // LANES, cols, LANES), jnp.float32),
            pltpu.VMEM((bands, *piece.shape), jnp.bfloat16), pltpu.VMEM(high.shape, jnp.bfloat16),
            pltpu.SemaphoreType.DMA((frames // 2,)),
        ],
        cost=work * frames, out_spaces=(*[VMEM] * bands, HBM),
    )
    pieces = pieces[:1] + [
        send(pieces[k], route(0, [(r, r ^ k) for r in range(bands)])) for k in range(1, bands)
    ]
    low = call(
        low_kernel, "low_rows", 8, pieces,
        half(frames // 2, bands * (rows // 2), cols // 2 // bands, chans),
        [pltpu.SemaphoreType.DMA((bands,))], out_spaces=HBM,
    )
    return low, high


def solution(mesh):
    in_specs = (P("frames", "rows", None, None), P(), P(), P(), P(), P(), P(), P())
    out_specs = (P("frames", None, "rows", None), P(None, "frames", "rows", None, None))
    return jax.shard_map(body, mesh=mesh, in_specs=in_specs, out_specs=out_specs, check_vma=False)
```

time: 76.7 us -> 72.6 us (0.947)
  blocking collectives: 14.2 us -> 31.5 us
  starting transfers between devices: 27.3 us -> 18.3 us
  waiting for transfers between devices: 8.03 us -> 2.31 us
  Pallas kernels: 22.6 us -> 17.9 us
  local copies, waits for them, and re-layouts: 3.26 us -> 1.27 us
    all_to_all x1 -> x2, blocking collectives: 14.2 us -> 31.5 us  [share(): return lax.all_to_all(stats, ('frames', 'rows'), 0, 0, tiled=True)]
    all_to_all x1 -> x0, starting transfers between devices: 8.9 us -> none  [share(): return lax.all_to_all(stats, ('frames', 'rows'), 0, 0, tiled=True)]
    all_to_all x1 -> x0, waiting for transfers between devices: 5.72 us -> none  [share(): return lax.all_to_all(stats, ('frames', 'rows'), 0, 0, tiled=True)]
    pallas_call x7, Pallas kernels: 22.6 us -> 17.9 us  [call(): pl.pallas_call(kernel, out_shape=out_shape, in_specs=spaces or [VMEM] * l...]
    unnamed x20 -> x18, local copies, waits for them, and re-layouts: 3.26 us -> 1.27 us
  transfers between devices with their start and end apart: 11 -> 10, of which waited for: 3 -> 2; matrix products, arithmetic and copies ran while one was open for 0% -> 0% of each run, Pallas kernels for 11% -> 8%
where the time goes in v4:
time: 72.6 us; the launch traced here: 72.4 us
  blocking collectives  31.5 us (43%)
  starting transfers between devices  18.3 us (25%)
  Pallas kernels  17.9 us (25%)
  waiting for transfers between devices  2.31 us (3%)
  local copies, waits for them, and re-layouts  1.27 us (2%)
  between operations  1.04 us (1%)
    all_to_all x2, blocking collectives, share(): return lax.all_to_all(stats, ('frames', 'rows'), 0, 0, tiled=True)  31.5 us
    ppermute x10, starting transfers between devices, send(): return lax.ppermute(values, ('frames', 'rows'), where)  18.3 us
    pallas_call x7, Pallas kernels, call(): pl.pallas_call(kernel, out_shape=out_shape, in_specs=spaces or [VMEM] * l...  17.9 us
    ppermute x10, waiting for transfers between devices, send(): return lax.ppermute(values, ('frames', 'rows'), where)  2.31 us
  transfers between devices with their start and end apart: 10, of which 2 were waited for; matrix products, arithmetic and copies ran while one was open for 0% of the time, Pallas kernels for 8%

profile of v4, /device:TPU:1, one launch (start us, length us, event | category | flops | bytes accessed | tf_op | source)
XLA Modules:
  0.0 72.4 jit_solution(8470040952604880424)
XLA Ops:
  0.6 0.0 copy-start
  0.6 1.2 %copy-done = bf16[8,4,64,256]{3,2,1,0:T(8,128)(2,1)S(1)} copy-done((bf16[8,4,64,256]{3,2,1,0:T(8,128)(2,1)S(1)}, bf16[8,4,64,256]{3,2,1,0:T(8,128)(2,1)}, u32[]{:S(2)}) %copy-start) | copy-done | bytes 1048600
  1.9 0.1 edges.1
  2.0 1.5 %collective-permute-start = (bf16[8,64,256]{2,1,0:T(8,128)(2,1)S(1)}, bf16[8,64,256]{2,1,0:T(8,128)(2,1)S(1)}, u32[]{:S(2)}, u32[]{:S(2)}) collective-permute-start(bf16[8,64,256]{2,1,0:T(8,128)(2,1)S(1)} %get-tuple-element.21), channel_id=1, source_target_pairs={{0,1},{1,0},{2,3},{3,2},{4,5},{5,4},{6,7},{7,6},{8,9},{9,8},{10,11... | collective-permute-start | bytes 786440 | tf_op jit(solution)/shard_map/ppermute | solution.py:383
  3.5 3.1 %collective-permute-start.1 = (bf16[8,64,256]{2,1,0:T(8,128)(2,1)S(1)}, bf16[8,64,256]{2,1,0:T(8,128)(2,1)S(1)}, u32[]{:S(2)}, u32[]{:S(2)}) collective-permute-start(bf16[8,64,256]{2,1,0:T(8,128)(2,1)S(1)} %get-tuple-element.22), channel_id=1, source_target_pairs={{1,2},{2,1},{5,6},{6,5},{9,10},{10,9},{13,14},{14,13},{17,18},{18,... | collective-permute-start | bytes 786440 | tf_op jit(solution)/shard_map/ppermute | solution.py:383
  6.6 0.0 copy-start.1
  6.6 0.0 copy-start.2
  6.6 0.0 copy-start.3
  6.6 0.0 copy-start.4
  6.6 4.7 %collective-permute-start.2 = (bf16[4,4,64,256]{3,2,1,0:T(8,128)(2,1)S(1)}, bf16[4,4,64,256]{3,2,1,0:T(8,128)(2,1)S(1)}, u32[]{:S(2)}, u32[]{:S(2)}) collective-permute-start(bf16[4,4,64,256]{3,2,1,0:T(8,128)(2,1)S(1)} %get-tuple-element.23), channel_id=1, source_target_pairs={{0,4},{1,5},{2,6},{3,7},{4,8},{5,9},{6,10},{7,11},{8,12},{9,13},{1... | collective-permute-start | bytes 1572872 | tf_op jit(solution)/shard_map/ppermute | solution.py:383
  11.3 1.0 %stats_one.1 = f32[128,128]{1,0:T(8,128)S(1)} custom-call(bf16[8,4,64,256]{3,2,1,0:T(8,128)(2,1)S(1)} %copy-done), custom_call_target="tpu_custom_call" | custom-call | flops 10000000000 | bytes 1000000 | tf_op jit(solution)/shard_map/stats_one/pallas_call | solution.py:400
  12.3 18.4 %all_to_all.23 = f32[128,1,128]{2,1,0:T(1,128)S(1)} all-to-all(f32[128,1,128]{2,1,0:T(1,128)S(1)} %bitcast.17), channel_id=1, replica_groups=mesh['frames'=32,'rows'=4] {'frames','rows'}, dimensions={0} | all-to-all | bytes 131072 | tf_op jit(solution)/shard_map/all_to_all | solution.py:387
  30.7 0.0 collective-permute-done.2.past_ref
  30.7 0.8 %collective-permute-start.3 = (bf16[4,64,256]{2,1,0:T(8,128)(2,1)S(1)}, bf16[4,64,256]{2,1,0:T(8,128)(2,1)S(1)}, u32[]{:S(2)}, u32[]{:S(2)}) collective-permute-start(bf16[4,64,256]{2,1,0:T(8,128)(2,1)S(1)} %get-tuple-element.25), channel_id=1, source_target_pairs={{0,1},{1,0},{2,3},{3,2},{4,5},{5,4},{6,7},{7,6},{8,9},{9,8},{10,11... | collective-permute-start | bytes 393224 | tf_op jit(solution)/shard_map/ppermute | solution.py:383
  31.6 2.4 %collective-permute-start.4 = (bf16[4,64,256]{2,1,0:T(8,128)(2,1)S(1)}, bf16[4,64,256]{2,1,0:T(8,128)(2,1)S(1)}, u32[]{:S(2)}, u32[]{:S(2)}) collective-permute-start(bf16[4,64,256]{2,1,0:T(8,128)(2,1)S(1)} %get-tuple-element.26), channel_id=1, source_target_pairs={{1,2},{2,1},{5,6},{6,5},{9,10},{10,9},{13,14},{14,13},{17,18},{18,... | collective-permute-start | bytes 393224 | tf_op jit(solution)/shard_map/ppermute | solution.py:383
  34.0 0.0 collective-permute-done.near_ref
  34.0 0.0 collective-permute-done.1.far_ref
  34.0 0.0 copy-done.1
  34.0 0.0 copy-done.2
  34.0 0.0 copy-done.3
  34.0 0.0 copy-done.4
  34.0 5.0 %conv_one_own.1 = (bf16[6,4,64,256]{3,2,1,0:T(8,128)(2,1)S(1)}, f32[8,256]{1,0:T(8,128)S(1)}, bf16[2,3,3,256,256]{4,3,2,1,0:T(8,128)(2,1)S(1)}) custom-call(bf16[8,4,64,256]{3,2,1,0:T(8,128)(2,1)S(1)} %copy-done.1, bf16[8,64,256]{2,1,0:T(8,128)(2,1)S(1)} %collective-permute-done.near_ref, bf16[8,64,256]{2,1,0:T(8,128)(2,1)S(1)} %collective-permute-done.1.far_ref, ...), custom_call_target="tpu_custom_call" | custom-call | flops 3623878656 | bytes 1000000 | tf_op jit(solution)/shard_map/conv_one_own/pallas_call | solution.py:400
  39.1 0.0 collective-permute-done.3.near_past_ref
  39.1 0.0 collective-permute-done.4.far_past_ref
  39.1 0.0 copy-start.5
  39.1 0.0 copy-start.6
  39.1 0.0 copy-start.7
  39.1 0.0 copy-start.8
  39.1 3.9 %conv_one_past.1 = (bf16[4,4,64,256]{3,2,1,0:T(8,128)(2,1)S(1)}, f32[128,128]{1,0:T(8,128)S(1)}, bf16[10,64,256]{2,1,0:T(8,128)(2,1)S(1)}, bf16[10,64,256]{2,1,0:T(8,128)(2,1)S(1)}) custom-call(bf16[8,4,64,256]{3,2,1,0:T(8,128)(2,1)S(1)} %copy-done.1, bf16[8,64,256]{2,1,0:T(8,128)(2,1)S(1)} %collective-permute-done.near_ref, ...), custom_call_target="tpu_custom_call" | custom-call | flops 2415919104 | bytes 1000000 | tf_op jit(solution)/shard_map/conv_one_past/pallas_call | solution.py:400
  43.1 0.1 collective-permute-start.5
  43.2 3.1 %collective-permute-start.6 = (bf16[10,64,256]{2,1,0:T(8,128)(2,1)S(1)}, bf16[10,64,256]{2,1,0:T(8,128)(2,1)S(1)}, u32[]{:S(2)}, u32[]{:S(2)}) collective-permute-start(bf16[10,64,256]{2,1,0:T(8,128)(2,1)S(1)} %get-tuple-element.33), channel_id=1, source_target_pairs={{1,2},{2,1},{5,6},{6,5},{9,10},{10,9},{13,14},{14,13},{17,18},{18,... | collective-permute-start | bytes 983048 | tf_op jit(solution)/shard_map/ppermute | solution.py:383
  46.3 13.2 %all_to_all.24 = f32[128,1,128]{2,1,0:T(1,128)S(1)} all-to-all(f32[128,1,128]{2,1,0:T(1,128)S(1)} %bitcast.15), channel_id=1, replica_groups=mesh['frames'=32,'rows'=4] {'frames','rows'}, dimensions={0} | all-to-all | bytes 131072 | tf_op jit(solution)/shard_map/all_to_all | solution.py:387
  59.5 0.0 collective-permute-done.5.near_ref
  59.5 0.0 collective-permute-done.6.far_ref
  59.5 0.0 copy-done.5
  59.5 0.0 copy-done.6
  59.5 0.0 copy-done.7
  59.5 0.0 copy-done.8
  59.5 7.2 %conv_two.1 = (bf16[4,2,8,256]{3,2,1,0:T(8,128)(2,1)S(1)}, bf16[4,2,8,256]{3,2,1,0:T(8,128)(2,1)S(1)}, bf16[4,2,8,256]{3,2,1,0:T(8,128)(2,1)S(1)}, bf16[4,2,8,25...) custom-call(bf16[4,4,64,256]{3,2,1,0:T(8,128)(2,1)S(1)} %get-tuple-element.31.hidden_ref, ...), custom_call_target="tpu_custom_call" | custom-call | flops 4831838208 | bytes 1000000 | tf_op jit(solution)/shard_map/conv_two/pallas_call | solution.py:400
  66.7 0.8 %collective-permute-start.7 = (bf16[4,2,8,256]{3,2,1,0:T(8,128)(2,1)S(1)}, bf16[4,2,8,256]{3,2,1,0:T(8,128)(2,1)S(1)}, u32[]{:S(2)}, u32[]{:S(2)}) collective-permute-start(bf16[4,2,8,256]{3,2,1,0:T(8,128)(2,1)S(1)} %get-tuple-element.36), channel_id=1, source_target_pairs={{0,1},{1,0},{2,3},{3,2},{4,5},{5,4},{6,7},{7,6},{8,9},{9,8},{10,11... | collective-permute-start | bytes 98312 | tf_op jit(solution)/shard_map/ppermute | solution.py:383
  67.5 0.3 collective-permute-start.8
  67.8 1.4 %collective-permute-start.9 = (bf16[4,2,8,256]{3,2,1,0:T(8,128)(2,1)S(1)}, bf16[4,2,8,256]{3,2,1,0:T(8,128)(2,1)S(1)}, u32[]{:S(2)}, u32[]{:S(2)}) collective-permute-start(bf16[4,2,8,256]{3,2,1,0:T(8,128)(2,1)S(1)} %get-tuple-element.38), channel_id=1, source_target_pairs={{0,3},{1,2},{2,1},{3,0},{4,7},{5,6},{6,5},{7,4},{8,11},{9,10},{10,... | collective-permute-start | bytes 98312 | tf_op jit(solution)/shard_map/ppermute | solution.py:383
  69.2 0.0 collective-permute-done.7.refs_1_
  69.2 1.1 %collective-permute-done.8.refs_2_ = bf16[4,2,8,256]{3,2,1,0:T(8,128)(2,1)S(1)} collective-permute-done((bf16[4,2,8,256]{3,2,1,0:T(8,128)(2,1)S(1)}, bf16[4,2,8,256]{3,2,1,0:T(8,128)(2,1)S(1)}, u32[]{:S(2)}, u32[]{:S(2)}) %collective-permute-start.8) | collective-permute-done | bytes 32800 | tf_op jit(solution)/shard_map/ppermute | solution.py:383
  70.3 1.2 %collective-permute-done.9.refs_3_ = bf16[4,2,8,256]{3,2,1,0:T(8,128)(2,1)S(1)} collective-permute-done((bf16[4,2,8,256]{3,2,1,0:T(8,128)(2,1)S(1)}, bf16[4,2,8,256]{3,2,1,0:T(8,128)(2,1)S(1)}, u32[]{:S(2)}, u32[]{:S(2)}) %collective-permute-start.9) | collective-permute-done | bytes 32800 | tf_op jit(solution)/shard_map/ppermute | solution.py:383
  71.5 0.7 low_rows.1
  (1 shorter events, 0.0 us)
Async XLA Ops:
  0.6 1.2 %copy-start = (bf16[8,4,64,256]{3,2,1,0:T(8,128)(2,1)S(1)}, bf16[8,4,64,256]{3,2,1,0:T(8,128)(2,1)}, u32[]{:S(2)}) copy-start(bf16[8,4,64,256]{3,2,1,0:T(8,128)(2,1)} %source_ref.1) | copy-start | bytes 3145732
  2.0 32.0 %collective-permute-start = (bf16[8,64,256]{2,1,0:T(8,128)(2,1)S(1)}, bf16[8,64,256]{2,1,0:T(8,128)(2,1)S(1)}, u32[]{:S(2)}, u32[]{:S(2)}) collective-permute-start(bf16[8,64,256]{2,1,0:T(8,128)(2,1)S(1)} %get-tuple-element.21), channel_id=1, source_target_pairs={{0,1},{1,0},{2,3},{3,2},{4,5},{5,4},{6,7},{7,6},{8,9},{9,8},{10,11... | collective-permute-start | bytes 786440 | tf_op jit(solution)/shard_map/ppermute | solution.py:383
  3.5 30.5 %collective-permute-start.1 = (bf16[8,64,256]{2,1,0:T(8,128)(2,1)S(1)}, bf16[8,64,256]{2,1,0:T(8,128)(2,1)S(1)}, u32[]{:S(2)}, u32[]{:S(2)}) collective-permute-start(bf16[8,64,256]{2,1,0:T(8,128)(2,1)S(1)} %get-tuple-element.22), channel_id=1, source_target_pairs={{1,2},{2,1},{5,6},{6,5},{9,10},{10,9},{13,14},{14,13},{17,18},{18,... | collective-permute-start | bytes 786440 | tf_op jit(solution)/shard_map/ppermute | solution.py:383
  6.6 27.4 %copy-start.1 = (bf16[8,4,64,256]{3,2,1,0:T(8,128)(2,1)S(1)}, bf16[8,4,64,256]{3,2,1,0:T(8,128)(2,1)}, u32[]{:S(2)}) copy-start(bf16[8,4,64,256]{3,2,1,0:T(8,128)(2,1)} %source_ref.1) | copy-start | bytes 3145732
  6.6 27.4 %copy-start.2 = (bf16[3,3,3,256,256]{4,3,2,1,0:T(8,128)(2,1)S(1)}, bf16[3,3,3,256,256]{4,3,2,1,0:T(8,128)(2,1)}, u32[]{:S(2)}) copy-start(bf16[3,3,3,256,256]{4,3,2,1,0:T(8,128)(2,1)} %kernel_ref.4) | copy-start | bytes 10616836
  6.6 27.4 %copy-start.3 = (f32[256]{0:T(256)S(1)}, f32[256]{0:T(256)}, u32[]{:S(2)}) copy-start(f32[256]{0:T(256)} %param.10) | copy-start | bytes 3076
  6.6 27.4 %copy-start.4 = (f32[256]{0:T(256)S(1)}, f32[256]{0:T(256)}, u32[]{:S(2)}) copy-start(f32[256]{0:T(256)} %param.11) | copy-start | bytes 3076
  6.6 24.1 %collective-permute-start.2 = (bf16[4,4,64,256]{3,2,1,0:T(8,128)(2,1)S(1)}, bf16[4,4,64,256]{3,2,1,0:T(8,128)(2,1)S(1)}, u32[]{:S(2)}, u32[]{:S(2)}) collective-permute-start(bf16[4,4,64,256]{3,2,1,0:T(8,128)(2,1)S(1)} %get-tuple-element.23), channel_id=1, source_target_pairs={{0,4},{1,5},{2,6},{3,7},{4,8},{5,9},{6,10},{7,11},{8,12},{9,13},{1... | collective-permute-start | bytes 1572872 | tf_op jit(solution)/shard_map/ppermute | solution.py:383
  30.7 8.4 %collective-permute-start.3 = (bf16[4,64,256]{2,1,0:T(8,128)(2,1)S(1)}, bf16[4,64,256]{2,1,0:T(8,128)(2,1)S(1)}, u32[]{:S(2)}, u32[]{:S(2)}) collective-permute-start(bf16[4,64,256]{2,1,0:T(8,128)(2,1)S(1)} %get-tuple-element.25), channel_id=1, source_target_pairs={{0,1},{1,0},{2,3},{3,2},{4,5},{5,4},{6,7},{7,6},{8,9},{9,8},{10,11... | collective-permute-start | bytes 393224 | tf_op jit(solution)/shard_map/ppermute | solution.py:383
  31.6 7.5 %collective-permute-start.4 = (bf16[4,64,256]{2,1,0:T(8,128)(2,1)S(1)}, bf16[4,64,256]{2,1,0:T(8,128)(2,1)S(1)}, u32[]{:S(2)}, u32[]{:S(2)}) collective-permute-start(bf16[4,64,256]{2,1,0:T(8,128)(2,1)S(1)} %get-tuple-element.26), channel_id=1, source_target_pairs={{1,2},{2,1},{5,6},{6,5},{9,10},{10,9},{13,14},{14,13},{17,18},{18,... | collective-permute-start | bytes 393224 | tf_op jit(solution)/shard_map/ppermute | solution.py:383
  39.1 20.4 %copy-start.5 = (bf16[3,3,3,256,256]{4,3,2,1,0:T(8,128)(2,1)S(1)}, bf16[3,3,3,256,256]{4,3,2,1,0:T(8,128)(2,1)}, u32[]{:S(2)}) copy-start(bf16[3,3,3,256,256]{4,3,2,1,0:T(8,128)(2,1)} %kernel_ref.5) | copy-start | bytes 10616836
  39.1 20.4 %copy-start.6 = (f32[256]{0:T(256)S(1)}, f32[256]{0:T(256)}, u32[]{:S(2)}) copy-start(f32[256]{0:T(256)} %param.13) | copy-start | bytes 3076
  39.1 20.4 %copy-start.7 = (f32[256]{0:T(256)S(1)}, f32[256]{0:T(256)}, u32[]{:S(2)}) copy-start(f32[256]{0:T(256)} %param.14) | copy-start | bytes 3076
  39.1 20.4 %copy-start.8 = (f32[256]{0:T(256)S(1)}, f32[256]{0:T(256)}, u32[]{:S(2)}) copy-start(f32[256]{0:T(256)} %param.15) | copy-start | bytes 3076
  43.1 16.4 %collective-permute-start.5 = (bf16[10,64,256]{2,1,0:T(8,128)(2,1)S(1)}, bf16[10,64,256]{2,1,0:T(8,128)(2,1)S(1)}, u32[]{:S(2)}, u32[]{:S(2)}) collective-permute-start(bf16[10,64,256]{2,1,0:T(8,128)(2,1)S(1)} %get-tuple-element.32), channel_id=1, source_target_pairs={{0,1},{1,0},{2,3},{3,2},{4,5},{5,4},{6,7},{7,6},{8,9},{9,8},{10,11... | collective-permute-start | bytes 983048 | tf_op jit(solution)/shard_map/ppermute | solution.py:383
  43.2 16.3 %collective-permute-start.6 = (bf16[10,64,256]{2,1,0:T(8,128)(2,1)S(1)}, bf16[10,64,256]{2,1,0:T(8,128)(2,1)S(1)}, u32[]{:S(2)}, u32[]{:S(2)}) collective-permute-start(bf16[10,64,256]{2,1,0:T(8,128)(2,1)S(1)} %get-tuple-element.33), channel_id=1, source_target_pairs={{1,2},{2,1},{5,6},{6,5},{9,10},{10,9},{13,14},{14,13},{17,18},{18,... | collective-permute-start | bytes 983048 | tf_op jit(solution)/shard_map/ppermute | solution.py:383
  66.7 2.6 %collective-permute-start.7 = (bf16[4,2,8,256]{3,2,1,0:T(8,128)(2,1)S(1)}, bf16[4,2,8,256]{3,2,1,0:T(8,128)(2,1)S(1)}, u32[]{:S(2)}, u32[]{:S(2)}) collective-permute-start(bf16[4,2,8,256]{3,2,1,0:T(8,128)(2,1)S(1)} %get-tuple-element.36), channel_id=1, source_target_pairs={{0,1},{1,0},{2,3},{3,2},{4,5},{5,4},{6,7},{7,6},{8,9},{9,8},{10,11... | collective-permute-start | bytes 98312 | tf_op jit(solution)/shard_map/ppermute | solution.py:383
  67.5 2.8 %collective-permute-start.8 = (bf16[4,2,8,256]{3,2,1,0:T(8,128)(2,1)S(1)}, bf16[4,2,8,256]{3,2,1,0:T(8,128)(2,1)S(1)}, u32[]{:S(2)}, u32[]{:S(2)}) collective-permute-start(bf16[4,2,8,256]{3,2,1,0:T(8,128)(2,1)S(1)} %get-tuple-element.37), channel_id=1, source_target_pairs={{0,2},{1,3},{2,0},{3,1},{4,6},{5,7},{6,4},{7,5},{8,10},{9,11},{10,... | collective-permute-start | bytes 98312 | tf_op jit(solution)/shard_map/ppermute | solution.py:383
  67.8 3.7 %collective-permute-start.9 = (bf16[4,2,8,256]{3,2,1,0:T(8,128)(2,1)S(1)}, bf16[4,2,8,256]{3,2,1,0:T(8,128)(2,1)S(1)}, u32[]{:S(2)}, u32[]{:S(2)}) collective-permute-start(bf16[4,2,8,256]{3,2,1,0:T(8,128)(2,1)S(1)} %get-tuple-element.38), channel_id=1, source_target_pairs={{0,3},{1,2},{2,1},{3,0},{4,7},{5,6},{6,5},{7,4},{8,11},{9,10},{10,... | collective-permute-start | bytes 98312 | tf_op jit(solution)/shard_map/ppermute | solution.py:383

commit v5 on v4

--- a/solution.py
+++ b/solution.py
@@ -12,6 +12,7 @@
 LANES = 128
 LAGS = 4
 STEP = 2
+LAG_COLS = (1, 0, 2)
 VMEM = pl.BlockSpec(memory_space=pltpu.VMEM)
 HBM = pl.BlockSpec(memory_space=pltpu.HBM)
 
@@ -80,8 +81,20 @@
     return (1 - odd) * (rows - 1), odd * (rows - 1)
 
 
+def row_place():
+    place = lax.axis_index("rows")
+    return lax.rem(place, 2) == 1, place > 0, place < lax.axis_size("rows") - 1
+
+
 def has_past():
     return lax.axis_index("frames") > 0
+
+
+def active(value, terms, valid):
+    mean, scale, offset = terms
+    value = (value.astype(jnp.float32) - mean) * scale + offset
+    value = 0.5 * value * (1.0 + jnp.tanh(0.5 * value))
+    return value if valid is None else jnp.where(valid, value, 0.0)
 
 
 class Window:
@@ -91,16 +104,10 @@
         self.cols, self.chans = cols, wide_ref.shape[3]
         self.pairs = wide_ref.shape[2] // cols
         self.rows = 2 * self.pairs
-        place = lax.axis_index("rows")
-        self.odd = lax.rem(place, 2) == 1
-        self.above = place > 0
-        self.below = place < lax.axis_size("rows") - 1
+        self.odd, self.above, self.below = row_place()
 
     def active(self, value, valid):
-        mean, scale, offset = self.terms
-        value = (value.astype(jnp.float32) - mean) * scale + offset
-        value = 0.5 * value * (1.0 + jnp.tanh(0.5 * value))
-        return value if valid is None else jnp.where(valid, value, 0.0)
+        return active(value, self.terms, valid)
 
     def put(self, frame, body, near, far, valid):
         above, below = self.above, self.below
@@ -120,47 +127,47 @@
                 )
 
     def conv(self, start, count, kernel_ref, mixed_ref, mix=False):
-        shape = (count * self.pairs, self.cols, -1)
-        column = lax.broadcasted_iota(jnp.int32, (1, self.cols, 1), 1)
         totals = [None, None]
-        for lag_col in (1, 0, 2):
+        for lag_col in LAG_COLS:
             if mix:
                 mix_taps(kernel_ref, mixed_ref, lag_col)
             terms = []
             for index in range(4):
-                window = jnp.concatenate(
-                    [
-                        self.wide_ref[start + lag : start + lag + count, index].reshape(
-                            -1, self.chans
-                        )
-                        for lag in range(3)
-                    ],
-                    axis=1,
-                )
                 if index in (0, 3):
                     taps = [kernel_ref[lag, 2 * (index // 3), lag_col] for lag in range(3)]
                 else:
                     taps = [mixed_ref[index - 1, lag, lag_col] for lag in range(3)]
-                terms.append(
-                    jnp.dot(
-                        window, jnp.concatenate(taps, axis=0), preferred_element_type=jnp.float32
-                    )
-                )
+                terms.append(product(self.wide_ref, start, count, index, taps))
             middle = terms[1] - terms[2]
             parts = terms[0] + (terms[1] + terms[2]), middle - terms[3]
             for at, part in enumerate(parts):
-                part = part.reshape(shape)
-                if lag_col == 0:
-                    part = jnp.where(column == 0, 0.0, pltpu.roll(part, 1, 1))
-                if lag_col == 2:
-                    part = jnp.where(
-                        column == self.cols - 1, 0.0, pltpu.roll(part, self.cols - 1, 1)
-                    )
+                part = shifted(part, self.cols, lag_col)
                 totals[at] = part if totals[at] is None else totals[at] + part
         return [
             [totals[row % 2][frame * self.pairs + row // 2] for row in range(self.rows)]
             for frame in range(count)
         ]
+
+
+def product(wide_ref, start, count, index, taps):
+    window = jnp.concatenate(
+        [
+            wide_ref[start + lag : start + lag + count, index].reshape(-1, wide_ref.shape[3])
+            for lag in range(3)
+        ],
+        axis=1,
+    )
+    return jnp.dot(window, jnp.concatenate(taps, axis=0), preferred_element_type=jnp.float32)
+
+
+def shifted(part, cols, lag_col):
+    part = part.reshape(-1, cols, part.shape[-1])
+    column = lax.broadcasted_iota(jnp.int32, (1, cols, 1), 1)
+    if lag_col == 0:
+        part = jnp.where(column == 0, 0.0, pltpu.roll(part, 1, 1))
+    if lag_col == 2:
+        part = jnp.where(column == cols - 1, 0.0, pltpu.roll(part, cols - 1, 1))
+    return part
 
 
 def mix_taps(kernel_ref, mixed_ref, lag_col):
@@ -173,25 +180,15 @@
         mixed_ref[1, lag, lag_col] = (outer - second).astype(jnp.bfloat16)
 
 
-def edges_kernel(values_ref, past_ref, near_ref, far_ref, sems):
-    frames, rows = values_ref.shape[:2]
-    near, far = near_and_far(rows)
-    pairs = (
-        (values_ref.at[pl.ds(frames - LAGS, LAGS)], past_ref),
-        (values_ref.at[:, near], near_ref),
-        (values_ref.at[:, far], far_ref),
-    )
-    copies = [pltpu.make_async_copy(*pair, sems.at[i]) for i, pair in enumerate(pairs)]
-    for copy in copies:
-        copy.start()
-    for copy in copies:
-        copy.wait()
-
-
-def past_edges_kernel(past_ref, near_ref, far_ref):
-    near, far = near_and_far(past_ref.shape[1])
-    near_ref[...] = past_ref[:, near]
-    far_ref[...] = past_ref[:, far]
+def past_kernel(values_ref, past_ref):
+    past_ref[...] = values_ref[values_ref.shape[0] - LAGS :]
+
+
+def edges_kernel(values_ref, past_ref, near_ref, far_ref):
+    near, far = near_and_far(values_ref.shape[1])
+    for row, out_ref in ((near, near_ref), (far, far_ref)):
+        out_ref[0:LAGS] = past_ref[:, row]
+        out_ref[LAGS:] = values_ref[:, row]
 
 
 def stats_kernel(values_ref, out_ref):
@@ -217,70 +214,107 @@
     return float(frames * rows * cols * (chans // GROUPS))
 
 
-def first_kernel_own(
-    own_ref, near_ref, far_ref, stats_ref, gain_ref, offset_ref, kernel_ref,
-    hidden_ref, sums_ref, mixed_ref, wide_ref,
+def inner_kernel(
+    own_ref, past_ref, stats_ref, gain_ref, offset_ref, kernel_ref,
+    hidden_ref, partial_ref, middle_ref, sums_ref, wide_ref, side_ref, mixed_ref,
 ):
     frames, rows, cols, chans = own_ref.shape
-    mean, scale = norm_terms(stats_ref, gain_ref, group_count(*own_ref.shape))
-    window = Window(wide_ref, mean, scale, offset_ref[...], cols)
+    terms = (*norm_terms(stats_ref, gain_ref, group_count(*own_ref.shape)), offset_ref[...])
     total = jnp.zeros((8, chans), jnp.float32)
-    for frame in range(frames):
-        window.put(frame, own_ref.at[frame], near_ref[frame], far_ref[frame], None)
+    for frame in range(frames + LAGS):
+        body, valid = own_ref.at[frame - LAGS], None
+        if frame < LAGS:
+            body, valid = past_ref.at[frame], has_past()
+        lines = [active(body[row], terms, valid) for row in range(rows)]
+        for pair in range(2):
+            first, second = lines[2 * pair : 2 * pair + 2]
+            for index, value in enumerate((0.5 * (first + second), 0.5 * (second - first))):
+                wide_ref[frame, index, pair * cols : (pair + 1) * cols] = value.astype(jnp.bfloat16)
+            side_ref[frame, pair] = (lines[pair] - lines[pair + 2]).astype(jnp.bfloat16)
+            middle_ref[frame, pair] = lines[pair + 1].astype(jnp.bfloat16)
         if frame < STEP + 1 or (frame - 1) % STEP:
             continue
         start = frame - 1 - STEP
-        conv = window.conv(start, STEP, kernel_ref, mixed_ref, mix=start == 0)
+        sums = [None, None]
+        sides = [None, None]
+        for lag_col in LAG_COLS:
+            if start == 0:
+                mix_taps(kernel_ref, mixed_ref, lag_col)
+            taps = [[mixed_ref[at, lag, lag_col] for lag in range(3)] for at in range(2)]
+            plus, minus = (product(wide_ref, start, STEP, at, taps[at]) for at in range(2))
+            for at, part in enumerate((plus + minus, plus - minus)):
+                part = shifted(part, cols, lag_col)
+                sums[at] = part if sums[at] is None else sums[at] + part
+            for at in range(2):
+                taps = [kernel_ref[lag, 2 - 2 * at, lag_col] for lag in range(3)]
+                part = shifted(product(side_ref, start, STEP, at, taps), cols, lag_col)
+                sides[at] = part if sides[at] is None else sides[at] + part
         for at in range(STEP):
-            for row in range(rows):
-                hidden = conv[at][row].astype(jnp.bfloat16)
-                hidden_ref[start + at, row] = hidden
-                total = total + jnp.sum(folded(hidden), axis=0)
+            place = start + at
+            partial_ref[place, 0] = sums[0][2 * at]
+            partial_ref[place, 1] = sums[1][2 * at + 1]
+            for row, value in enumerate(
+                (sums[1][2 * at] - sides[0][at], sums[0][2 * at + 1] + sides[1][at])
+            ):
+                hidden = value.astype(jnp.bfloat16)
+                hidden_ref[place, row] = hidden
+                if place >= 2:
+                    total = total + jnp.sum(folded(hidden), axis=0)
     sums_ref[...] = total
 
 
-def first_kernel_past(
-    own_ref, near_ref, far_ref, past_ref, near_past_ref, far_past_ref,
-    stats_ref, gain_ref, offset_ref, kernel_ref, later_ref, sums_ref, mixed_ref,
-    hidden_ref, out_stats_ref, out_near_ref, out_far_ref, wide_ref,
+def outer_kernel(
+    near_ref, far_ref, stats_ref, gain_ref, offset_ref, kernel_ref,
+    hidden_ref, partial_ref, middle_ref, sums_ref,
+    out_stats_ref, out_near_ref, out_far_ref, side_ref,
 ):
-    frames, rows, cols, chans = own_ref.shape
-    count = group_count(*own_ref.shape)
-    mean, scale = norm_terms(stats_ref, gain_ref, count)
-    window = Window(wide_ref, mean, scale, offset_ref[...], cols)
+    count_frames, rows, cols, chans = hidden_ref.shape
+    frames = count_frames - 2
+    count = group_count(frames, 2 * rows, cols, chans)
+    terms = (*norm_terms(stats_ref, gain_ref, count), offset_ref[...])
+    odd, above, below = row_place()
     sums = sums_ref[...]
-    centre = channel_group_sums(sums) / group_count(*later_ref.shape)
+    centre = channel_group_sums(sums) / (count / 2)
     squares = jnp.zeros((8, chans), jnp.float32)
 
     def square(block):
         away = folded(block) - centre
         return jnp.sum(away * away, axis=0)
 
-    for frame in range(LAGS + 2):
-        own = frame - LAGS
-        if own < 0:
-            window.put(
-                frame, past_ref.at[frame], near_past_ref[frame], far_past_ref[frame], has_past()
-            )
-        else:
-            window.put(frame, own_ref.at[own], near_ref[own], far_ref[own], None)
-        squares = squares + square(later_ref[frame])
+    for frame in range(frames + LAGS):
+        valids = above, below
+        if frame < LAGS:
+            valids = [jnp.logical_and(valid, has_past()) for valid in valids]
+        near, far = near_ref[frame], far_ref[frame]
+        upper = active(jnp.where(odd, near, far), terms, valids[0])
+        lower = active(jnp.where(odd, far, near), terms, valids[1])
+        middle = [middle_ref[frame, row].astype(jnp.float32) for row in range(2)]
+        side_ref[frame, 0] = (upper - middle[0]).astype(jnp.bfloat16)
+        side_ref[frame, 1] = (middle[1] - lower).astype(jnp.bfloat16)
+        if 2 <= frame < count_frames:
+            squares = squares + square(hidden_ref[frame])
         if frame < STEP + 1 or (frame - 1) % STEP:
             continue
         start = frame - 1 - STEP
-        conv = window.conv(start, STEP, kernel_ref, mixed_ref)
+        sides = [None, None]
+        for lag_col in LAG_COLS:
+            for at in range(2):
+                taps = [kernel_ref[lag, 2 * at, lag_col] for lag in range(3)]
+                part = shifted(product(side_ref, start, STEP, at, taps), cols, lag_col)
+                sides[at] = part if sides[at] is None else sides[at] + part
         for at in range(STEP):
-            for row in range(rows):
-                hidden = conv[at][row].astype(jnp.bfloat16)
-                hidden_ref[start + at, row] = hidden
-                if start + at >= 2:
-                    squares = squares + square(hidden)
-                    sums = sums + jnp.sum(folded(hidden), axis=0)
+            place = start + at
+            edges = [
+                (partial_ref[place, 0] + sides[0][at]).astype(jnp.bfloat16),
+                (partial_ref[place, 1] - sides[1][at]).astype(jnp.bfloat16),
+            ]
+            out_near_ref[place] = jnp.where(odd, edges[0], edges[1])
+            out_far_ref[place] = jnp.where(odd, edges[1], edges[0])
+            if place >= 2:
+                for edge in edges:
+                    squares = squares + square(edge)
+                    sums = sums + jnp.sum(folded(edge), axis=0)
     put_stats(out_stats_ref, sums, squares, centre, count)
-    near, far = near_and_far(rows)
-    for source, out_ref in ((near, out_near_ref), (far, out_far_ref)):
-        out_ref[0:LAGS] = hidden_ref[:, source]
-        out_ref[LAGS:] = later_ref[:, source]
 
 
 def columns_apart(line, pair_ref):
@@ -295,8 +329,8 @@
 
 
 def second_kernel(
-    hidden_ref, later_ref, near_ref, far_ref, stats_ref, gain_ref, offset_ref, kernel_ref,
-    source_ref, bias_ref, *rest,
+    hidden_ref, own_near_ref, own_far_ref, near_ref, far_ref, stats_ref, gain_ref, offset_ref,
+    kernel_ref, source_ref, bias_ref, *rest,
 ):
     *low_refs, high_ref, wide_ref, mixed_ref, pair_ref, low_ref, held_ref, sems = rest
     frames, rows, cols, chans = source_ref.shape
@@ -307,7 +341,11 @@
     width = cols // 2 // bands
     copies = []
     for frame in range(frames + 2):
-        body = hidden_ref.at[frame] if frame < LAGS else later_ref.at[frame - LAGS]
+        near, far = own_near_ref[frame], own_far_ref[frame]
+        body = (
+            jnp.where(window.odd, near, far), hidden_ref[frame, 0], hidden_ref[frame, 1],
+            jnp.where(window.odd, far, near),
+        )
         window.put(frame, body, near_ref[frame], far_ref[frame], has_past() if frame < 2 else None)
         if frame < 3 or frame % 2 == 0:
             continue
@@ -418,54 +456,53 @@
     to_far = route(0, [(r, ((r + 1) ^ 1) - 1) for r in range(1, bands - 1)])
     to_next = route(1, [(r, r) for r in range(bands)])
 
-    def wide(count):
-        return pltpu.VMEM((count, 4, rows // 2 * cols, chans), jnp.bfloat16)
-
-    past, near, far = call(
-        edges_kernel, "edges", 8, (inputs,),
-        (half(LAGS, rows, cols, chans), half(frames, cols, chans), half(frames, cols, chans)),
-        [pltpu.SemaphoreType.DMA((3,))], spaces=[HBM],
-    )
-    past, near, far = send(past, to_next), send(near, to_near), send(far, to_far)
+    def window(*shape):
+        return pltpu.VMEM(shape, jnp.bfloat16)
+
+    past = call(past_kernel, "past", 8, (inputs,), half(LAGS, rows, cols, chans))
+    past = send(past, to_next)
     stats = call(stats_kernel, "stats_one", 8, (inputs,), single(devices, LANES), cost=10**10)
     past, stats = lax.optimization_barrier((past, share(stats)))
-    near_past, far_past = call(
-        past_edges_kernel, "past_edges", 8, (past,),
-        (half(LAGS, cols, chans), half(LAGS, cols, chans)),
-    )
-    near_past, far_past = send(near_past, to_near), send(far_past, to_far)
+    reach = frames + LAGS
+    near, far = call(
+        edges_kernel, "edges", 8, (inputs, past),
+        (half(reach, cols, chans), half(reach, cols, chans)),
+    )
+    near, far = send(near, to_near), send(far, to_far)
     affine = (gain_one[None], offset_one[None])
-    mixed = half(2, 3, 3, chans, chans)
-    later, sums, mixed_one = call(
-        first_kernel_own, "conv_one_own", 32,
-        (inputs, near, far, stats, *affine, kernel_one),
-        (half(frames - 2, rows, cols, chans), single(8, chans), mixed),
-        [wide(frames)], cost=work * (frames - 2),
+    inner, partial, middle, sums = call(
+        inner_kernel, "conv_inner", 32, (inputs, past, stats, *affine, kernel_one),
+        (
+            half(frames + 2, 2, cols, chans), single(frames + 2, 2, cols, chans),
+            half(reach, 2, cols, chans), single(8, chans),
+        ),
+        [
+            window(reach, 2, 2 * cols, chans), window(reach, 2, cols, chans),
+            window(2, 3, 3, chans, chans),
+        ],
+        cost=work * (frames + 2),
     )
     edge = half(frames + 2, cols, chans)
-    hidden, stats, near, far = call(
-        first_kernel_past, "conv_one_past", 32,
-        (
-            inputs, near, far, past, near_past, far_past, stats, *affine, kernel_one, later, sums,
-            mixed_one,
-        ),
-        (half(LAGS, rows, cols, chans), single(devices, LANES), edge, edge),
-        [wide(LAGS + 2)], cost=work * LAGS,
-    )
-    near, far = send(near, to_near), send(far, to_far)
+    stats, own_near, own_far = call(
+        outer_kernel, "conv_outer", 32,
+        (near, far, stats, *affine, kernel_one, inner, partial, middle, sums),
+        (single(devices, LANES), edge, edge), [window(reach, 2, cols, chans)], cost=work * 4,
+    )
+    near, far = send(own_near, to_near), send(own_far, to_far)
     stats = share(stats)
     piece = half(frames // 2, rows // 2, cols // 2 // bands, chans)
     high = half(7, frames // 2, rows // 2, cols // 2, chans)
     *pieces, high = call(
         second_kernel, "conv_two", 32,
         (
-            hidden, later, near, far, stats, gain_two[None], offset_two[None], kernel_two, inputs,
+            inner, own_near, own_far, near, far, stats, gain_two[None], offset_two[None], kernel_two, inputs,
             bias_two[None],
         ),
         (*[piece] * bands, high),
         [
-            wide(frames + 2), pltpu.VMEM(mixed.shape, jnp.bfloat16), pltpu.VMEM((8, chans // LANES, cols, LANES), jnp.float32),
-            pltpu.VMEM((bands, *piece.shape), jnp.bfloat16), pltpu.VMEM(high.shape, jnp.bfloat16),
+            window(frames + 2, 4, rows // 2 * cols, chans), window(2, 3, 3, chans, chans),
+            pltpu.VMEM((8, chans // LANES, cols, LANES), jnp.float32),
+            window(bands, *piece.shape), window(*high.shape),
             pltpu.SemaphoreType.DMA((frames // 2,)),
         ],
         cost=work * frames, out_spaces=(*[VMEM] * bands, HBM),

time: 72.6 us -> 70.5 us (0.971)
  starting transfers between devices: 18.3 us -> 14.4 us
  blocking collectives: 31.5 us -> 33.2 us
    ppermute x10 -> x8, starting transfers between devices: 18.3 us -> 14.4 us  [send(): return lax.ppermute(values, ('frames', 'rows'), where)]
    all_to_all x2, blocking collectives: 31.5 us -> 33.2 us  [share(): return lax.all_to_all(stats, ('frames', 'rows'), 0, 0, tiled=True)]
    ppermute x10 -> x8, waiting for transfers between devices: 2.31 us -> 2.96 us  [send(): return lax.ppermute(values, ('frames', 'rows'), where)]
  transfers between devices with their start and end apart: 10 -> 8, of which waited for: 2 -> 3; matrix products, arithmetic and copies ran while one was open for 0% -> 0% of each run, Pallas kernels for 8% -> 10%
where the time goes in v5:
time: 70.5 us; the launch traced here: 70.3 us
  blocking collectives  33.2 us (47%)
  Pallas kernels  17.5 us (25%)
  starting transfers between devices  14.4 us (20%)
  waiting for transfers between devices  2.96 us (4%)
  local copies, waits for them, and re-layouts  1.26 us (2%)
  between operations  0.97 us (1%)
    all_to_all x2, blocking collectives, share(): return lax.all_to_all(stats, ('frames', 'rows'), 0, 0, tiled=True)  33.2 us
    pallas_call x7, Pallas kernels, call(): pl.pallas_call(kernel, out_shape=out_shape, in_specs=spaces or [VMEM] * l...  17.5 us
    ppermute x8, starting transfers between devices, send(): return lax.ppermute(values, ('frames', 'rows'), where)  14.4 us
    ppermute x8, waiting for transfers between devices, send(): return lax.ppermute(values, ('frames', 'rows'), where)  2.96 us
  transfers between devices with their start and end apart: 8, of which 3 were waited for; matrix products, arithmetic and copies ran while one was open for 0% of the time, Pallas kernels for 10%

profile of v5, /device:TPU:1, one launch (start us, length us, event | category | flops | bytes accessed | tf_op | source)
XLA Modules:
  0.0 70.3 jit_solution(2877614103496573326)
XLA Ops:
  0.6 0.0 copy-start
  0.6 1.2 %copy-done = bf16[8,4,64,256]{3,2,1,0:T(8,128)(2,1)S(1)} copy-done((bf16[8,4,64,256]{3,2,1,0:T(8,128)(2,1)S(1)}, bf16[8,4,64,256]{3,2,1,0:T(8,128)(2,1)}, u32[]{:S(2)}) %copy-start) | copy-done | bytes 1048600
  1.9 0.0 copy-start.1
  1.9 0.0 copy-start.2
  1.9 0.0 copy-start.4
  1.9 0.0 copy-start.5
  1.9 5.8 %collective-permute-start = (bf16[4,4,64,256]{3,2,1,0:T(8,128)(2,1)S(1)}, bf16[4,4,64,256]{3,2,1,0:T(8,128)(2,1)S(1)}, u32[]{:S(2)}, u32[]{:S(2)}) collective-permute-start(bf16[4,4,64,256]{3,2,1,0:T(8,128)(2,1)S(1)} %past.1), channel_id=1, source_target_pairs={{0,4},{1,5},{2,6},{3,7},{4,8},{5,9},{6,10},{7,11},{8,12},{9,13},{1... | collective-permute-start | bytes 1572872 | tf_op jit(solution)/shard_map/ppermute | solution.py:421
  7.7 1.0 %stats_one.1 = f32[128,128]{1,0:T(8,128)S(1)} custom-call(bf16[8,4,64,256]{3,2,1,0:T(8,128)(2,1)S(1)} %copy-done), custom_call_target="tpu_custom_call" | custom-call | flops 10000000000 | bytes 1000000 | tf_op jit(solution)/shard_map/stats_one/pallas_call | solution.py:438
  8.8 19.2 %all_to_all.23 = f32[128,1,128]{2,1,0:T(1,128)S(1)} all-to-all(f32[128,1,128]{2,1,0:T(1,128)S(1)} %bitcast.17), channel_id=1, replica_groups=mesh['frames'=32,'rows'=4] {'frames','rows'}, dimensions={0} | all-to-all | bytes 131072 | tf_op jit(solution)/shard_map/all_to_all | solution.py:425
  27.9 0.0 collective-permute-done.past_ref
  27.9 0.1 edges.1
  28.0 0.8 %collective-permute-start.1 = (bf16[12,64,256]{2,1,0:T(8,128)(2,1)S(1)}, bf16[12,64,256]{2,1,0:T(8,128)(2,1)S(1)}, u32[]{:S(2)}, u32[]{:S(2)}) collective-permute-start(bf16[12,64,256]{2,1,0:T(8,128)(2,1)S(1)} %get-tuple-element.21), channel_id=1, source_target_pairs={{0,1},{1,0},{2,3},{3,2},{4,5},{5,4},{6,7},{7,6},{8,9},{9,8},{10,11... | collective-permute-start | bytes 1179656 | tf_op jit(solution)/shard_map/ppermute | solution.py:421
  28.8 2.6 %collective-permute-start.2 = (bf16[12,64,256]{2,1,0:T(8,128)(2,1)S(1)}, bf16[12,64,256]{2,1,0:T(8,128)(2,1)S(1)}, u32[]{:S(2)}, u32[]{:S(2)}) collective-permute-start(bf16[12,64,256]{2,1,0:T(8,128)(2,1)S(1)} %get-tuple-element.22), channel_id=1, source_target_pairs={{1,2},{2,1},{5,6},{6,5},{9,10},{10,9},{13,14},{14,13},{17,18},{18,... | collective-permute-start | bytes 1179656 | tf_op jit(solution)/shard_map/ppermute | solution.py:421
  31.4 0.0 copy-done.1
  31.4 0.0 copy-done.2
  31.4 0.0 copy-done.4
  31.4 0.0 copy-done.5
  31.5 5.8 %conv_inner.1 = (bf16[10,2,64,256]{3,2,1,0:T(8,128)(2,1)S(1)}, f32[10,2,64,256]{3,2,1,0:T(8,128)S(1)}, bf16[12,2,64,256]{3,2,1,0:T(8,128)(2,1)S(1)}, f32[8,256]{1,0:T(8,128)S(1)}) custom-call(bf16[8,4,64,256]{3,2,1,0:T(8,128)(2,1)S(1)} %copy-done.1, bf16[4,4,64,256]{3,2,1,0:T(8,128)(2,1)S(1)} %collective-permute-done.past_ref, f32[128,128]{1,0:T(8,128)S(1)} %bitcast.13, ...), custom_call_target="tpu_custom_call" | custom-call | flops 6039797760 | bytes 1000000 | tf_op jit(solution)/shard_map/conv_inner/pallas_call | solution.py:438
  37.3 0.0 collective-permute-done.1.near_ref
  37.3 0.7 collective-permute-done.2.far_ref
  37.9 0.0 copy-start.3
  37.9 0.0 copy-start.6
  37.9 0.0 copy-start.7
  37.9 0.0 copy-start.8
  37.9 2.7 %conv_outer.1 = (f32[128,128]{1,0:T(8,128)S(1)}, bf16[10,64,256]{2,1,0:T(8,128)(2,1)S(1)}, bf16[10,64,256]{2,1,0:T(8,128)(2,1)S(1)}) custom-call(bf16[12,64,256]{2,1,0:T(8,128)(2,1)S(1)} %collective-permute-done.1.near_ref, bf16[12,64,256]{2,1,0:T(8,128)(2,1)S(1)} %collective-permute-done.2.far_ref, f32[128,128]{1,0:T(8,128)S(1)} %bitcast.14, ...), custom_call_target="tpu_custom_call" | custom-call | flops 2415919104 | bytes 1000000 | tf_op jit(solution)/shard_map/conv_outer/pallas_call | solution.py:438
  40.6 0.1 collective-permute-start.3
  40.7 2.6 %collective-permute-start.4 = (bf16[10,64,256]{2,1,0:T(8,128)(2,1)S(1)}, bf16[10,64,256]{2,1,0:T(8,128)(2,1)S(1)}, u32[]{:S(2)}, u32[]{:S(2)}) collective-permute-start(bf16[10,64,256]{2,1,0:T(8,128)(2,1)S(1)} %get-tuple-element.27.own_far_ref), channel_id=1, source_target_pairs={{1,2},{2,1},{5,6},{6,5},{9,10},{10,9},{13,14},{14,13},{17,18},{18,... | collective-permute-start | bytes 983048 | tf_op jit(solution)/shard_map/ppermute | solution.py:421
  43.3 14.0 %all_to_all.24 = f32[128,1,128]{2,1,0:T(1,128)S(1)} all-to-all(f32[128,1,128]{2,1,0:T(1,128)S(1)} %bitcast.15), channel_id=1, replica_groups=mesh['frames'=32,'rows'=4] {'frames','rows'}, dimensions={0} | all-to-all | bytes 131072 | tf_op jit(solution)/shard_map/all_to_all | solution.py:425
  57.3 0.0 collective-permute-done.3.near_ref
  57.3 0.0 collective-permute-done.4.far_ref
  57.3 0.0 copy-done.3
  57.4 0.0 copy-done.6
  57.4 0.0 copy-done.7
  57.4 0.0 copy-done.8
  57.4 7.2 %conv_two.1 = (bf16[4,2,8,256]{3,2,1,0:T(8,128)(2,1)S(1)}, bf16[4,2,8,256]{3,2,1,0:T(8,128)(2,1)S(1)}, bf16[4,2,8,256]{3,2,1,0:T(8,128)(2,1)S(1)}, bf16[4,2,8,25...) custom-call(bf16[10,2,64,256]{3,2,1,0:T(8,128)(2,1)S(1)} %get-tuple-element.20.hidden_ref, ...), custom_call_target="tpu_custom_call" | custom-call | flops 4831838208 | bytes 1000000 | tf_op jit(solution)/shard_map/conv_two/pallas_call | solution.py:438
  64.6 0.8 %collective-permute-start.5 = (bf16[4,2,8,256]{3,2,1,0:T(8,128)(2,1)S(1)}, bf16[4,2,8,256]{3,2,1,0:T(8,128)(2,1)S(1)}, u32[]{:S(2)}, u32[]{:S(2)}) collective-permute-start(bf16[4,2,8,256]{3,2,1,0:T(8,128)(2,1)S(1)} %get-tuple-element.30), channel_id=1, source_target_pairs={{0,1},{1,0},{2,3},{3,2},{4,5},{5,4},{6,7},{7,6},{8,9},{9,8},{10,11... | collective-permute-start | bytes 98312 | tf_op jit(solution)/shard_map/ppermute | solution.py:421
  65.4 0.3 collective-permute-start.6
  65.7 1.4 %collective-permute-start.7 = (bf16[4,2,8,256]{3,2,1,0:T(8,128)(2,1)S(1)}, bf16[4,2,8,256]{3,2,1,0:T(8,128)(2,1)S(1)}, u32[]{:S(2)}, u32[]{:S(2)}) collective-permute-start(bf16[4,2,8,256]{3,2,1,0:T(8,128)(2,1)S(1)} %get-tuple-element.32), channel_id=1, source_target_pairs={{0,3},{1,2},{2,1},{3,0},{4,7},{5,6},{6,5},{7,4},{8,11},{9,10},{10,... | collective-permute-start | bytes 98312 | tf_op jit(solution)/shard_map/ppermute | solution.py:421
  67.2 0.0 collective-permute-done.5.refs_1_
  67.2 1.1 %collective-permute-done.6.refs_2_ = bf16[4,2,8,256]{3,2,1,0:T(8,128)(2,1)S(1)} collective-permute-done((bf16[4,2,8,256]{3,2,1,0:T(8,128)(2,1)S(1)}, bf16[4,2,8,256]{3,2,1,0:T(8,128)(2,1)S(1)}, u32[]{:S(2)}, u32[]{:S(2)}) %collective-permute-start.6) | collective-permute-done | bytes 32800 | tf_op jit(solution)/shard_map/ppermute | solution.py:421
  68.2 1.2 %collective-permute-done.7.refs_3_ = bf16[4,2,8,256]{3,2,1,0:T(8,128)(2,1)S(1)} collective-permute-done((bf16[4,2,8,256]{3,2,1,0:T(8,128)(2,1)S(1)}, bf16[4,2,8,256]{3,2,1,0:T(8,128)(2,1)S(1)}, u32[]{:S(2)}, u32[]{:S(2)}) %collective-permute-start.7) | collective-permute-done | bytes 32800 | tf_op jit(solution)/shard_map/ppermute | solution.py:421
  69.4 0.7 low_rows.1
  (1 shorter events, 0.0 us)
Async XLA Ops:
  0.6 1.2 %copy-start = (bf16[8,4,64,256]{3,2,1,0:T(8,128)(2,1)S(1)}, bf16[8,4,64,256]{3,2,1,0:T(8,128)(2,1)}, u32[]{:S(2)}) copy-start(bf16[8,4,64,256]{3,2,1,0:T(8,128)(2,1)} %source_ref.1) | copy-start | bytes 3145732
  1.9 29.5 %copy-start.1 = (bf16[8,4,64,256]{3,2,1,0:T(8,128)(2,1)S(1)}, bf16[8,4,64,256]{3,2,1,0:T(8,128)(2,1)}, u32[]{:S(2)}) copy-start(bf16[8,4,64,256]{3,2,1,0:T(8,128)(2,1)} %source_ref.1) | copy-start | bytes 3145732
  1.9 29.5 %copy-start.2 = (bf16[3,3,3,256,256]{4,3,2,1,0:T(8,128)(2,1)S(1)}, bf16[3,3,3,256,256]{4,3,2,1,0:T(8,128)(2,1)}, u32[]{:S(2)}) copy-start(bf16[3,3,3,256,256]{4,3,2,1,0:T(8,128)(2,1)} %kernel_ref.4) | copy-start | bytes 10616836
  1.9 29.5 %copy-start.4 = (f32[256]{0:T(256)S(1)}, f32[256]{0:T(256)}, u32[]{:S(2)}) copy-start(f32[256]{0:T(256)} %param.10) | copy-start | bytes 3076
  1.9 29.5 %copy-start.5 = (f32[256]{0:T(256)S(1)}, f32[256]{0:T(256)}, u32[]{:S(2)}) copy-start(f32[256]{0:T(256)} %param.11) | copy-start | bytes 3076
  1.9 26.0 %collective-permute-start = (bf16[4,4,64,256]{3,2,1,0:T(8,128)(2,1)S(1)}, bf16[4,4,64,256]{3,2,1,0:T(8,128)(2,1)S(1)}, u32[]{:S(2)}, u32[]{:S(2)}) collective-permute-start(bf16[4,4,64,256]{3,2,1,0:T(8,128)(2,1)S(1)} %past.1), channel_id=1, source_target_pairs={{0,4},{1,5},{2,6},{3,7},{4,8},{5,9},{6,10},{7,11},{8,12},{9,13},{1... | collective-permute-start | bytes 1572872 | tf_op jit(solution)/shard_map/ppermute | solution.py:421
  28.0 9.3 %collective-permute-start.1 = (bf16[12,64,256]{2,1,0:T(8,128)(2,1)S(1)}, bf16[12,64,256]{2,1,0:T(8,128)(2,1)S(1)}, u32[]{:S(2)}, u32[]{:S(2)}) collective-permute-start(bf16[12,64,256]{2,1,0:T(8,128)(2,1)S(1)} %get-tuple-element.21), channel_id=1, source_target_pairs={{0,1},{1,0},{2,3},{3,2},{4,5},{5,4},{6,7},{7,6},{8,9},{9,8},{10,11... | collective-permute-start | bytes 1179656 | tf_op jit(solution)/shard_map/ppermute | solution.py:421
  28.8 9.1 %collective-permute-start.2 = (bf16[12,64,256]{2,1,0:T(8,128)(2,1)S(1)}, bf16[12,64,256]{2,1,0:T(8,128)(2,1)S(1)}, u32[]{:S(2)}, u32[]{:S(2)}) collective-permute-start(bf16[12,64,256]{2,1,0:T(8,128)(2,1)S(1)} %get-tuple-element.22), channel_id=1, source_target_pairs={{1,2},{2,1},{5,6},{6,5},{9,10},{10,9},{13,14},{14,13},{17,18},{18,... | collective-permute-start | bytes 1179656 | tf_op jit(solution)/shard_map/ppermute | solution.py:421
  37.9 19.4 %copy-start.3 = (bf16[3,3,3,256,256]{4,3,2,1,0:T(8,128)(2,1)S(1)}, bf16[3,3,3,256,256]{4,3,2,1,0:T(8,128)(2,1)}, u32[]{:S(2)}) copy-start(bf16[3,3,3,256,256]{4,3,2,1,0:T(8,128)(2,1)} %kernel_ref.5) | copy-start | bytes 10616836
  37.9 19.4 %copy-start.6 = (f32[256]{0:T(256)S(1)}, f32[256]{0:T(256)}, u32[]{:S(2)}) copy-start(f32[256]{0:T(256)} %param.13) | copy-start | bytes 3076
  37.9 19.4 %copy-start.7 = (f32[256]{0:T(256)S(1)}, f32[256]{0:T(256)}, u32[]{:S(2)}) copy-start(f32[256]{0:T(256)} %param.14) | copy-start | bytes 3076
  37.9 19.4 %copy-start.8 = (f32[256]{0:T(256)S(1)}, f32[256]{0:T(256)}, u32[]{:S(2)}) copy-start(f32[256]{0:T(256)} %param.15) | copy-start | bytes 3076
  40.6 16.7 %collective-permute-start.3 = (bf16[10,64,256]{2,1,0:T(8,128)(2,1)S(1)}, bf16[10,64,256]{2,1,0:T(8,128)(2,1)S(1)}, u32[]{:S(2)}, u32[]{:S(2)}) collective-permute-start(bf16[10,64,256]{2,1,0:T(8,128)(2,1)S(1)} %get-tuple-element.26.own_near_ref), channel_id=1, source_target_pairs={{0,1},{1,0},{2,3},{3,2},{4,5},{5,4},{6,7},{7,6},{8,9},{9,8},{10,11... | collective-permute-start | bytes 983048 | tf_op jit(solution)/shard_map/ppermute | solution.py:421
  40.7 16.6 %collective-permute-start.4 = (bf16[10,64,256]{2,1,0:T(8,128)(2,1)S(1)}, bf16[10,64,256]{2,1,0:T(8,128)(2,1)S(1)}, u32[]{:S(2)}, u32[]{:S(2)}) collective-permute-start(bf16[10,64,256]{2,1,0:T(8,128)(2,1)S(1)} %get-tuple-element.27.own_far_ref), channel_id=1, source_target_pairs={{1,2},{2,1},{5,6},{6,5},{9,10},{10,9},{13,14},{14,13},{17,18},{18,... | collective-permute-start | bytes 983048 | tf_op jit(solution)/shard_map/ppermute | solution.py:421
  64.6 2.6 %collective-permute-start.5 = (bf16[4,2,8,256]{3,2,1,0:T(8,128)(2,1)S(1)}, bf16[4,2,8,256]{3,2,1,0:T(8,128)(2,1)S(1)}, u32[]{:S(2)}, u32[]{:S(2)}) collective-permute-start(bf16[4,2,8,256]{3,2,1,0:T(8,128)(2,1)S(1)} %get-tuple-element.30), channel_id=1, source_target_pairs={{0,1},{1,0},{2,3},{3,2},{4,5},{5,4},{6,7},{7,6},{8,9},{9,8},{10,11... | collective-permute-start | bytes 98312 | tf_op jit(solution)/shard_map/ppermute | solution.py:421
  65.4 2.8 %collective-permute-start.6 = (bf16[4,2,8,256]{3,2,1,0:T(8,128)(2,1)S(1)}, bf16[4,2,8,256]{3,2,1,0:T(8,128)(2,1)S(1)}, u32[]{:S(2)}, u32[]{:S(2)}) collective-permute-start(bf16[4,2,8,256]{3,2,1,0:T(8,128)(2,1)S(1)} %get-tuple-element.31), channel_id=1, source_target_pairs={{0,2},{1,3},{2,0},{3,1},{4,6},{5,7},{6,4},{7,5},{8,10},{9,11},{10,... | collective-permute-start | bytes 98312 | tf_op jit(solution)/shard_map/ppermute | solution.py:421
  65.7 3.7 %collective-permute-start.7 = (bf16[4,2,8,256]{3,2,1,0:T(8,128)(2,1)S(1)}, bf16[4,2,8,256]{3,2,1,0:T(8,128)(2,1)S(1)}, u32[]{:S(2)}, u32[]{:S(2)}) collective-permute-start(bf16[4,2,8,256]{3,2,1,0:T(8,128)(2,1)S(1)} %get-tuple-element.32), channel_id=1, source_target_pairs={{0,3},{1,2},{2,1},{3,0},{4,7},{5,6},{6,5},{7,4},{8,11},{9,10},{10,... | collective-permute-start | bytes 98312 | tf_op jit(solution)/shard_map/ppermute | solution.py:421

commit v6 on v5

--- a/solution.py
+++ b/solution.py
@@ -54,7 +54,7 @@
     out_ref[...] = jnp.broadcast_to(row, out_ref.shape)
 
 
-def norm_terms(stats_ref, gain_ref, count):
+def norm_terms(stats_ref, gain_ref, offset_ref, count):
     stats = stats_ref[...]
     devices = stats.shape[0]
     average = jnp.sum(stats, axis=0, keepdims=True) / devices
@@ -73,7 +73,7 @@
     terms = group_sums(terms)
     mean = jnp.concatenate([terms[0:1], terms[1:2]], axis=1)
     var = jnp.concatenate([terms[2:3], terms[3:4]], axis=1)
-    return mean, gain_ref[...] / jnp.sqrt(var + EPS)
+    return mean, (0.5 * gain_ref[...]) / jnp.sqrt(var + EPS), 0.5 * offset_ref[...]
 
 
 def near_and_far(rows):
@@ -93,14 +93,13 @@
 def active(value, terms, valid):
     mean, scale, offset = terms
     value = (value.astype(jnp.float32) - mean) * scale + offset
-    value = 0.5 * value * (1.0 + jnp.tanh(0.5 * value))
+    value = value + value * jnp.tanh(value)
     return value if valid is None else jnp.where(valid, value, 0.0)
 
 
 class Window:
-    def __init__(self, wide_ref, mean, scale, offset, cols):
-        self.wide_ref = wide_ref
-        self.terms = mean, scale, offset
+    def __init__(self, wide_ref, terms, cols):
+        self.wide_ref, self.terms = wide_ref, terms
         self.cols, self.chans = cols, wide_ref.shape[3]
         self.pairs = wide_ref.shape[2] // cols
         self.rows = 2 * self.pairs
@@ -162,11 +161,15 @@
 
 def shifted(part, cols, lag_col):
     part = part.reshape(-1, cols, part.shape[-1])
-    column = lax.broadcasted_iota(jnp.int32, (1, cols, 1), 1)
+    column = lax.broadcasted_iota(jnp.int32, (1, 8, 1), 1)
     if lag_col == 0:
-        part = jnp.where(column == 0, 0.0, pltpu.roll(part, 1, 1))
+        part = pltpu.roll(part, 1, 1)
+        first = jnp.where(column == 0, 0.0, part[:, :8])
+        part = jnp.concatenate([first, part[:, 8:]], axis=1)
     if lag_col == 2:
-        part = jnp.where(column == cols - 1, 0.0, pltpu.roll(part, cols - 1, 1))
+        part = pltpu.roll(part, cols - 1, 1)
+        last = jnp.where(column == 7, 0.0, part[:, cols - 8 :])
+        part = jnp.concatenate([part[:, : cols - 8], last], axis=1)
     return part
 
 
@@ -196,17 +199,15 @@
     count = float(frames * rows * cols * (chans // GROUPS))
     zero = jnp.zeros((8, chans), jnp.float32)
 
-    def add(index, total):
-        return total + jnp.sum(folded(values_ref[index]), axis=0)
-
-    total = lax.fori_loop(0, frames, add, zero)
+    total = zero
+    for index in range(frames):
+        total = total + jnp.sum(folded(values_ref[index]), axis=0)
     centre = channel_group_sums(total) / count
 
-    def add_square(index, total):
+    squares = zero
+    for index in range(frames):
         away = folded(values_ref[index]) - centre
-        return total + jnp.sum(away * away, axis=0)
-
-    squares = lax.fori_loop(0, frames, add_square, zero)
+        squares = squares + jnp.sum(away * away, axis=0)
     put_stats(out_ref, total, squares, centre, count)
 
 
@@ -219,7 +220,7 @@
     hidden_ref, partial_ref, middle_ref, sums_ref, wide_ref, side_ref, mixed_ref,
 ):
     frames, rows, cols, chans = own_ref.shape
-    terms = (*norm_terms(stats_ref, gain_ref, group_count(*own_ref.shape)), offset_ref[...])
+    terms = norm_terms(stats_ref, gain_ref, offset_ref, group_count(*own_ref.shape))
     total = jnp.zeros((8, chans), jnp.float32)
     for frame in range(frames + LAGS):
         body, valid = own_ref.at[frame - LAGS], None
@@ -271,7 +272,7 @@
     count_frames, rows, cols, chans = hidden_ref.shape
     frames = count_frames - 2
     count = group_count(frames, 2 * rows, cols, chans)
-    terms = (*norm_terms(stats_ref, gain_ref, count), offset_ref[...])
+    terms = norm_terms(stats_ref, gain_ref, offset_ref, count)
     odd, above, below = row_place()
     sums = sums_ref[...]
     centre = channel_group_sums(sums) / (count / 2)
@@ -332,14 +333,13 @@
     hidden_ref, own_near_ref, own_far_ref, near_ref, far_ref, stats_ref, gain_ref, offset_ref,
     kernel_ref, source_ref, bias_ref, *rest,
 ):
-    *low_refs, high_ref, wide_ref, mixed_ref, pair_ref, low_ref, held_ref, sems = rest
+    *low_refs, high_ref, wide_ref, mixed_ref, pair_ref, low_ref = rest
     frames, rows, cols, chans = source_ref.shape
-    mean, scale = norm_terms(stats_ref, gain_ref, group_count(*source_ref.shape))
-    window = Window(wide_ref, mean, scale, offset_ref[...], cols)
+    terms = norm_terms(stats_ref, gain_ref, offset_ref, group_count(*source_ref.shape))
+    window = Window(wide_ref, terms, cols)
     factor = 0.5**1.5
     bands = len(low_refs)
     width = cols // 2 // bands
-    copies = []
     for frame in range(frames + 2):
         near, far = own_near_ref[frame], own_far_ref[frame]
         body = (
@@ -375,19 +375,23 @@
                         value = value.astype(jnp.bfloat16)
                         band = 4 * time_band + 2 * row_band + col_band
                         if band:
-                            held_ref[band - 1, index, pair] = value
+                            high_ref[band - 1, index, pair] = value
                         else:
                             for target in range(bands):
                                 low_ref[target, index, pair] = value[
                                     target * width : (target + 1) * width
                                 ]
-        copies.append(
-            pltpu.make_async_copy(held_ref.at[:, index], high_ref.at[:, index], sems.at[index])
-        )
-        copies[-1].start()
     place = lax.axis_index("rows")
     for index, out_ref in enumerate(low_refs):
         out_ref[...] = low_ref[lax.bitwise_xor(place, index)]
+
+def high_kernel(held_ref, out_ref, sems):
+    bands = held_ref.shape[0]
+    copies = [
+        pltpu.make_async_copy(held_ref.at[at], out_ref.at[at], sems.at[at]) for at in range(bands)
+    ]
+    for copy in copies:
+        copy.start()
     for copy in copies:
         copy.wait()
 
@@ -502,14 +506,17 @@
         [
             window(frames + 2, 4, rows // 2 * cols, chans), window(2, 3, 3, chans, chans),
             pltpu.VMEM((8, chans // LANES, cols, LANES), jnp.float32),
-            window(bands, *piece.shape), window(*high.shape),
-            pltpu.SemaphoreType.DMA((frames // 2,)),
+            window(bands, *piece.shape),
         ],
-        cost=work * frames, out_spaces=(*[VMEM] * bands, HBM),
+        cost=work * frames,
     )
     pieces = pieces[:1] + [
         send(pieces[k], route(0, [(r, r ^ k) for r in range(bands)])) for k in range(1, bands)
     ]
+    high = call(
+        high_kernel, "high_bands", 8, (high,), half(*high.shape),
+        [pltpu.SemaphoreType.DMA((high.shape[0],))], cost=10**9, out_spaces=HBM,
+    )
     low = call(
         low_kernel, "low_rows", 8, pieces,
         half(frames // 2, bands * (rows // 2), cols // 2 // bands, chans),

time: 70.5 us -> 69.5 us (0.986)
  waiting for transfers between devices: 2.96 us -> 1.88 us
    ppermute x8, waiting for transfers between devices: 2.96 us -> 1.88 us  [send(): return lax.ppermute(values, ('frames', 'rows'), where)]
    pallas_call x7 -> x8, Pallas kernels: 17.5 us -> 17.2 us  [call(): pl.pallas_call(kernel, out_shape=out_shape, in_specs=spaces or [VMEM] * l...]
  transfers between devices with their start and end apart: 8 -> 8, of which waited for: 3 -> 3; matrix products, arithmetic and copies ran while one was open for 0% -> 0% of each run, Pallas kernels for 10% -> 11%
where the time goes in v6:
time: 69.5 us; the launch traced here: 69.3 us
  blocking collectives  33.2 us (48%)
  Pallas kernels  17.2 us (25%)
  starting transfers between devices  14.8 us (21%)
  waiting for transfers between devices  1.88 us (3%)
  local copies, waits for them, and re-layouts  1.26 us (2%)
  between operations  0.98 us (1%)
    all_to_all x2, blocking collectives, share(): return lax.all_to_all(stats, ('frames', 'rows'), 0, 0, tiled=True)  33.2 us
    pallas_call x8, Pallas kernels, call(): pl.pallas_call(kernel, out_shape=out_shape, in_specs=spaces or [VMEM] * l...  17.2 us
    ppermute x8, starting transfers between devices, send(): return lax.ppermute(values, ('frames', 'rows'), where)  14.8 us
    ppermute x8, waiting for transfers between devices, send(): return lax.ppermute(values, ('frames', 'rows'), where)  1.88 us
  transfers between devices with their start and end apart: 8, of which 3 were waited for; matrix products, arithmetic and copies ran while one was open for 0% of the time, Pallas kernels for 11%

profile of v6, /device:TPU:1, one launch (start us, length us, event | category | flops | bytes accessed | tf_op | source)
XLA Modules:
  0.0 69.3 jit_solution(4772850211000611456)
XLA Ops:
  0.6 0.0 copy-start
  0.6 1.2 %copy-done = bf16[8,4,64,256]{3,2,1,0:T(8,128)(2,1)S(1)} copy-done((bf16[8,4,64,256]{3,2,1,0:T(8,128)(2,1)S(1)}, bf16[8,4,64,256]{3,2,1,0:T(8,128)(2,1)}, u32[]{:S(2)}) %copy-start) | copy-done | bytes 1048600
  1.9 0.0 copy-start.1
  1.9 0.0 copy-start.2
  1.9 0.0 copy-start.4
  1.9 0.0 copy-start.5
  1.9 5.8 %collective-permute-start = (bf16[4,4,64,256]{3,2,1,0:T(8,128)(2,1)S(1)}, bf16[4,4,64,256]{3,2,1,0:T(8,128)(2,1)S(1)}, u32[]{:S(2)}, u32[]{:S(2)}) collective-permute-start(bf16[4,4,64,256]{3,2,1,0:T(8,128)(2,1)S(1)} %past.1), channel_id=1, source_target_pairs={{0,4},{1,5},{2,6},{3,7},{4,8},{5,9},{6,10},{7,11},{8,12},{9,13},{1... | collective-permute-start | bytes 1572872 | tf_op jit(solution)/shard_map/ppermute | solution.py:425
  7.7 0.9 %stats_one.1 = f32[128,128]{1,0:T(8,128)S(1)} custom-call(bf16[8,4,64,256]{3,2,1,0:T(8,128)(2,1)S(1)} %copy-done), custom_call_target="tpu_custom_call" | custom-call | flops 10000000000 | bytes 1000000 | tf_op jit(solution)/shard_map/stats_one/pallas_call | solution.py:442
  8.6 19.2 %all_to_all.23 = f32[128,1,128]{2,1,0:T(1,128)S(1)} all-to-all(f32[128,1,128]{2,1,0:T(1,128)S(1)} %bitcast.17), channel_id=1, replica_groups=mesh['frames'=32,'rows'=4] {'frames','rows'}, dimensions={0} | all-to-all | bytes 131072 | tf_op jit(solution)/shard_map/all_to_all | solution.py:429
  27.8 0.0 collective-permute-done.past_ref
  27.8 0.1 edges.1
  27.8 0.8 %collective-permute-start.1 = (bf16[12,64,256]{2,1,0:T(8,128)(2,1)S(1)}, bf16[12,64,256]{2,1,0:T(8,128)(2,1)S(1)}, u32[]{:S(2)}, u32[]{:S(2)}) collective-permute-start(bf16[12,64,256]{2,1,0:T(8,128)(2,1)S(1)} %get-tuple-element.21), channel_id=1, source_target_pairs={{0,1},{1,0},{2,3},{3,2},{4,5},{5,4},{6,7},{7,6},{8,9},{9,8},{10,11... | collective-permute-start | bytes 1179656 | tf_op jit(solution)/shard_map/ppermute | solution.py:425
  28.7 2.7 %collective-permute-start.2 = (bf16[12,64,256]{2,1,0:T(8,128)(2,1)S(1)}, bf16[12,64,256]{2,1,0:T(8,128)(2,1)S(1)}, u32[]{:S(2)}, u32[]{:S(2)}) collective-permute-start(bf16[12,64,256]{2,1,0:T(8,128)(2,1)S(1)} %get-tuple-element.22), channel_id=1, source_target_pairs={{1,2},{2,1},{5,6},{6,5},{9,10},{10,9},{13,14},{14,13},{17,18},{18,... | collective-permute-start | bytes 1179656 | tf_op jit(solution)/shard_map/ppermute | solution.py:425
  31.4 0.0 copy-done.1
  31.4 0.0 copy-done.2
  31.4 0.0 copy-done.4
  31.4 0.0 copy-done.5
  31.5 5.7 %conv_inner.1 = (bf16[10,2,64,256]{3,2,1,0:T(8,128)(2,1)S(1)}, f32[10,2,64,256]{3,2,1,0:T(8,128)S(1)}, bf16[12,2,64,256]{3,2,1,0:T(8,128)(2,1)S(1)}, f32[8,256]{1,0:T(8,128)S(1)}) custom-call(bf16[8,4,64,256]{3,2,1,0:T(8,128)(2,1)S(1)} %copy-done.1, bf16[4,4,64,256]{3,2,1,0:T(8,128)(2,1)S(1)} %collective-permute-done.past_ref, f32[128,128]{1,0:T(8,128)S(1)} %bitcast.13, ...), custom_call_target="tpu_custom_call" | custom-call | flops 6039797760 | bytes 1000000 | tf_op jit(solution)/shard_map/conv_inner/pallas_call | solution.py:442
  37.2 0.0 collective-permute-done.1.near_ref
  37.2 0.6 collective-permute-done.2.far_ref
  37.7 0.0 copy-start.3
  37.7 0.0 copy-start.6
  37.8 0.0 copy-start.7
  37.8 0.0 copy-start.8
  37.8 2.6 %conv_outer.1 = (f32[128,128]{1,0:T(8,128)S(1)}, bf16[10,64,256]{2,1,0:T(8,128)(2,1)S(1)}, bf16[10,64,256]{2,1,0:T(8,128)(2,1)S(1)}) custom-call(bf16[12,64,256]{2,1,0:T(8,128)(2,1)S(1)} %collective-permute-done.1.near_ref, bf16[12,64,256]{2,1,0:T(8,128)(2,1)S(1)} %collective-permute-done.2.far_ref, f32[128,128]{1,0:T(8,128)S(1)} %bitcast.14, ...), custom_call_target="tpu_custom_call" | custom-call | flops 2415919104 | bytes 1000000 | tf_op jit(solution)/shard_map/conv_outer/pallas_call | solution.py:442
  40.4 0.1 collective-permute-start.3
  40.5 2.8 %collective-permute-start.4 = (bf16[10,64,256]{2,1,0:T(8,128)(2,1)S(1)}, bf16[10,64,256]{2,1,0:T(8,128)(2,1)S(1)}, u32[]{:S(2)}, u32[]{:S(2)}) collective-permute-start(bf16[10,64,256]{2,1,0:T(8,128)(2,1)S(1)} %get-tuple-element.27.own_far_ref), channel_id=1, source_target_pairs={{1,2},{2,1},{5,6},{6,5},{9,10},{10,9},{13,14},{14,13},{17,18},{18,... | collective-permute-start | bytes 983048 | tf_op jit(solution)/shard_map/ppermute | solution.py:425
  43.2 14.0 %all_to_all.24 = f32[128,1,128]{2,1,0:T(1,128)S(1)} all-to-all(f32[128,1,128]{2,1,0:T(1,128)S(1)} %bitcast.15), channel_id=1, replica_groups=mesh['frames'=32,'rows'=4] {'frames','rows'}, dimensions={0} | all-to-all | bytes 131072 | tf_op jit(solution)/shard_map/all_to_all | solution.py:429
  57.3 0.0 collective-permute-done.3.near_ref
  57.3 0.0 collective-permute-done.4.far_ref
  57.3 0.0 copy-done.3
  57.3 0.0 copy-done.6
  57.3 0.0 copy-done.7
  57.3 0.0 copy-done.8
  57.3 6.3 %conv_two.1 = (bf16[4,2,8,256]{3,2,1,0:T(8,128)(2,1)S(1)}, bf16[4,2,8,256]{3,2,1,0:T(8,128)(2,1)S(1)}, bf16[4,2,8,256]{3,2,1,0:T(8,128)(2,1)S(1)}, bf16[4,2,8,25...) custom-call(bf16[10,2,64,256]{3,2,1,0:T(8,128)(2,1)S(1)} %get-tuple-element.20.hidden_ref, ...), custom_call_target="tpu_custom_call" | custom-call | flops 4831838208 | bytes 1000000 | tf_op jit(solution)/shard_map/conv_two/pallas_call | solution.py:442
  63.6 0.8 %collective-permute-start.5 = (bf16[4,2,8,256]{3,2,1,0:T(8,128)(2,1)S(1)}, bf16[4,2,8,256]{3,2,1,0:T(8,128)(2,1)S(1)}, u32[]{:S(2)}, u32[]{:S(2)}) collective-permute-start(bf16[4,2,8,256]{3,2,1,0:T(8,128)(2,1)S(1)} %get-tuple-element.30), channel_id=1, source_target_pairs={{0,1},{1,0},{2,3},{3,2},{4,5},{5,4},{6,7},{7,6},{8,9},{9,8},{10,11... | collective-permute-start | bytes 98312 | tf_op jit(solution)/shard_map/ppermute | solution.py:425
  64.5 0.3 collective-permute-start.6
  64.8 1.4 %collective-permute-start.7 = (bf16[4,2,8,256]{3,2,1,0:T(8,128)(2,1)S(1)}, bf16[4,2,8,256]{3,2,1,0:T(8,128)(2,1)S(1)}, u32[]{:S(2)}, u32[]{:S(2)}) collective-permute-start(bf16[4,2,8,256]{3,2,1,0:T(8,128)(2,1)S(1)} %get-tuple-element.32), channel_id=1, source_target_pairs={{0,3},{1,2},{2,1},{3,0},{4,7},{5,6},{6,5},{7,4},{8,11},{9,10},{10,... | collective-permute-start | bytes 98312 | tf_op jit(solution)/shard_map/ppermute | solution.py:425
  66.2 1.0 %high_bands.1 = bf16[7,4,2,32,256]{4,3,2,1,0:T(8,128)(2,1)} custom-call(bf16[7,4,2,32,256]{4,3,2,1,0:T(8,128)(2,1)S(1)} %get-tuple-element.33.held_ref), custom_call_target="tpu_custom_call" | custom-call | flops 1000000000 | bytes 1000000 | tf_op jit(solution)/shard_map/high_bands/pallas_call | solution.py:442
  67.2 0.0 collective-permute-done.5.refs_1_
  67.2 0.1 collective-permute-done.6.refs_2_
  67.2 1.2 %collective-permute-done.7.refs_3_ = bf16[4,2,8,256]{3,2,1,0:T(8,128)(2,1)S(1)} collective-permute-done((bf16[4,2,8,256]{3,2,1,0:T(8,128)(2,1)S(1)}, bf16[4,2,8,256]{3,2,1,0:T(8,128)(2,1)S(1)}, u32[]{:S(2)}, u32[]{:S(2)}) %collective-permute-start.7) | collective-permute-done | bytes 32800 | tf_op jit(solution)/shard_map/ppermute | solution.py:425
  68.5 0.7 low_rows.1
  (1 shorter events, 0.0 us)
Async XLA Ops:
  0.6 1.2 %copy-start = (bf16[8,4,64,256]{3,2,1,0:T(8,128)(2,1)S(1)}, bf16[8,4,64,256]{3,2,1,0:T(8,128)(2,1)}, u32[]{:S(2)}) copy-start(bf16[8,4,64,256]{3,2,1,0:T(8,128)(2,1)} %source_ref.1) | copy-start | bytes 3145732
  1.9 29.5 %copy-start.1 = (bf16[8,4,64,256]{3,2,1,0:T(8,128)(2,1)S(1)}, bf16[8,4,64,256]{3,2,1,0:T(8,128)(2,1)}, u32[]{:S(2)}) copy-start(bf16[8,4,64,256]{3,2,1,0:T(8,128)(2,1)} %source_ref.1) | copy-start | bytes 3145732
  1.9 29.5 %copy-start.2 = (bf16[3,3,3,256,256]{4,3,2,1,0:T(8,128)(2,1)S(1)}, bf16[3,3,3,256,256]{4,3,2,1,0:T(8,128)(2,1)}, u32[]{:S(2)}) copy-start(bf16[3,3,3,256,256]{4,3,2,1,0:T(8,128)(2,1)} %kernel_ref.4) | copy-start | bytes 10616836
  1.9 29.5 %copy-start.4 = (f32[256]{0:T(256)S(1)}, f32[256]{0:T(256)}, u32[]{:S(2)}) copy-start(f32[256]{0:T(256)} %param.10) | copy-start | bytes 3076
  1.9 29.5 %copy-start.5 = (f32[256]{0:T(256)S(1)}, f32[256]{0:T(256)}, u32[]{:S(2)}) copy-start(f32[256]{0:T(256)} %param.11) | copy-start | bytes 3076
  1.9 25.8 %collective-permute-start = (bf16[4,4,64,256]{3,2,1,0:T(8,128)(2,1)S(1)}, bf16[4,4,64,256]{3,2,1,0:T(8,128)(2,1)S(1)}, u32[]{:S(2)}, u32[]{:S(2)}) collective-permute-start(bf16[4,4,64,256]{3,2,1,0:T(8,128)(2,1)S(1)} %past.1), channel_id=1, source_target_pairs={{0,4},{1,5},{2,6},{3,7},{4,8},{5,9},{6,10},{7,11},{8,12},{9,13},{1... | collective-permute-start | bytes 1572872 | tf_op jit(solution)/shard_map/ppermute | solution.py:425
  27.8 9.3 %collective-permute-start.1 = (bf16[12,64,256]{2,1,0:T(8,128)(2,1)S(1)}, bf16[12,64,256]{2,1,0:T(8,128)(2,1)S(1)}, u32[]{:S(2)}, u32[]{:S(2)}) collective-permute-start(bf16[12,64,256]{2,1,0:T(8,128)(2,1)S(1)} %get-tuple-element.21), channel_id=1, source_target_pairs={{0,1},{1,0},{2,3},{3,2},{4,5},{5,4},{6,7},{7,6},{8,9},{9,8},{10,11... | collective-permute-start | bytes 1179656 | tf_op jit(solution)/shard_map/ppermute | solution.py:425
  28.7 9.1 %collective-permute-start.2 = (bf16[12,64,256]{2,1,0:T(8,128)(2,1)S(1)}, bf16[12,64,256]{2,1,0:T(8,128)(2,1)S(1)}, u32[]{:S(2)}, u32[]{:S(2)}) collective-permute-start(bf16[12,64,256]{2,1,0:T(8,128)(2,1)S(1)} %get-tuple-element.22), channel_id=1, source_target_pairs={{1,2},{2,1},{5,6},{6,5},{9,10},{10,9},{13,14},{14,13},{17,18},{18,... | collective-permute-start | bytes 1179656 | tf_op jit(solution)/shard_map/ppermute | solution.py:425
  37.7 19.5 %copy-start.3 = (bf16[3,3,3,256,256]{4,3,2,1,0:T(8,128)(2,1)S(1)}, bf16[3,3,3,256,256]{4,3,2,1,0:T(8,128)(2,1)}, u32[]{:S(2)}) copy-start(bf16[3,3,3,256,256]{4,3,2,1,0:T(8,128)(2,1)} %kernel_ref.5) | copy-start | bytes 10616836
  37.7 19.5 %copy-start.6 = (f32[256]{0:T(256)S(1)}, f32[256]{0:T(256)}, u32[]{:S(2)}) copy-start(f32[256]{0:T(256)} %param.13) | copy-start | bytes 3076
  37.8 19.5 %copy-start.7 = (f32[256]{0:T(256)S(1)}, f32[256]{0:T(256)}, u32[]{:S(2)}) copy-start(f32[256]{0:T(256)} %param.14) | copy-start | bytes 3076
  37.8 19.5 %copy-start.8 = (f32[256]{0:T(256)S(1)}, f32[256]{0:T(256)}, u32[]{:S(2)}) copy-start(f32[256]{0:T(256)} %param.15) | copy-start | bytes 3076
  40.4 16.9 %collective-permute-start.3 = (bf16[10,64,256]{2,1,0:T(8,128)(2,1)S(1)}, bf16[10,64,256]{2,1,0:T(8,128)(2,1)S(1)}, u32[]{:S(2)}, u32[]{:S(2)}) collective-permute-start(bf16[10,64,256]{2,1,0:T(8,128)(2,1)S(1)} %get-tuple-element.26.own_near_ref), channel_id=1, source_target_pairs={{0,1},{1,0},{2,3},{3,2},{4,5},{5,4},{6,7},{7,6},{8,9},{9,8},{10,11... | collective-permute-start | bytes 983048 | tf_op jit(solution)/shard_map/ppermute | solution.py:425
  40.5 16.8 %collective-permute-start.4 = (bf16[10,64,256]{2,1,0:T(8,128)(2,1)S(1)}, bf16[10,64,256]{2,1,0:T(8,128)(2,1)S(1)}, u32[]{:S(2)}, u32[]{:S(2)}) collective-permute-start(bf16[10,64,256]{2,1,0:T(8,128)(2,1)S(1)} %get-tuple-element.27.own_far_ref), channel_id=1, source_target_pairs={{1,2},{2,1},{5,6},{6,5},{9,10},{10,9},{13,14},{14,13},{17,18},{18,... | collective-permute-start | bytes 983048 | tf_op jit(solution)/shard_map/ppermute | solution.py:425
  63.6 3.5 %collective-permute-start.5 = (bf16[4,2,8,256]{3,2,1,0:T(8,128)(2,1)S(1)}, bf16[4,2,8,256]{3,2,1,0:T(8,128)(2,1)S(1)}, u32[]{:S(2)}, u32[]{:S(2)}) collective-permute-start(bf16[4,2,8,256]{3,2,1,0:T(8,128)(2,1)S(1)} %get-tuple-element.30), channel_id=1, source_target_pairs={{0,1},{1,0},{2,3},{3,2},{4,5},{5,4},{6,7},{7,6},{8,9},{9,8},{10,11... | collective-permute-start | bytes 98312 | tf_op jit(solution)/shard_map/ppermute | solution.py:425
  64.5 2.8 %collective-permute-start.6 = (bf16[4,2,8,256]{3,2,1,0:T(8,128)(2,1)S(1)}, bf16[4,2,8,256]{3,2,1,0:T(8,128)(2,1)S(1)}, u32[]{:S(2)}, u32[]{:S(2)}) collective-permute-start(bf16[4,2,8,256]{3,2,1,0:T(8,128)(2,1)S(1)} %get-tuple-element.31), channel_id=1, source_target_pairs={{0,2},{1,3},{2,0},{3,1},{4,6},{5,7},{6,4},{7,5},{8,10},{9,11},{10,... | collective-permute-start | bytes 98312 | tf_op jit(solution)/shard_map/ppermute | solution.py:425
  64.8 3.7 %collective-permute-start.7 = (bf16[4,2,8,256]{3,2,1,0:T(8,128)(2,1)S(1)}, bf16[4,2,8,256]{3,2,1,0:T(8,128)(2,1)S(1)}, u32[]{:S(2)}, u32[]{:S(2)}) collective-permute-start(bf16[4,2,8,256]{3,2,1,0:T(8,128)(2,1)S(1)} %get-tuple-element.32), channel_id=1, source_target_pairs={{0,3},{1,2},{2,1},{3,0},{4,7},{5,6},{6,5},{7,4},{8,11},{9,10},{10,... | collective-permute-start | bytes 98312 | tf_op jit(solution)/shard_map/ppermute | solution.py:425

commit v7 on v6

--- a/solution.py
+++ b/solution.py
@@ -458,7 +458,13 @@
     work = 2 * rows * cols * chans * 18 * chans
     to_near = route(0, [(r, r ^ 1) for r in range(bands)])
     to_far = route(0, [(r, ((r + 1) ^ 1) - 1) for r in range(1, bands - 1)])
+    to_far += [
+        (f * bands + r, (f ^ 8) * bands + r)
+        for f in range(lax.axis_size("frames"))
+        for r in (0, bands - 1)
+    ]
     to_next = route(1, [(r, r) for r in range(bands)])
+    to_next += [((devices - bands) + r, r) for r in range(bands)]
 
     def window(*shape):
         return pltpu.VMEM(shape, jnp.bfloat16)

time: 69.5 us -> 64.1 us (0.922)
  starting transfers between devices: 14.8 us -> 8.84 us
    ppermute x8, starting transfers between devices: 14.8 us -> 8.84 us  [send(): return lax.ppermute(values, ('frames', 'rows'), where)]
  transfers between devices with their start and end apart: 8 -> 8, of which waited for: 3 -> 3; matrix products, arithmetic and copies ran while one was open for 0% -> 0% of each run, Pallas kernels for 11% -> 12%
where the time goes in v7:
time: 64.1 us; the launch traced here: 63.9 us
  blocking collectives  33.5 us (52%)
  Pallas kernels  17.2 us (27%)
  starting transfers between devices  8.84 us (14%)
  waiting for transfers between devices  2.12 us (3%)
  local copies, waits for them, and re-layouts  1.26 us (2%)
  between operations  0.92 us (1%)
    all_to_all x2, blocking collectives, share(): return lax.all_to_all(stats, ('frames', 'rows'), 0, 0, tiled=True)  33.5 us
    pallas_call x8, Pallas kernels, call(): pl.pallas_call(kernel, out_shape=out_shape, in_specs=spaces or [VMEM] * l...  17.2 us
    ppermute x8, starting transfers between devices, send(): return lax.ppermute(values, ('frames', 'rows'), where)  8.84 us
    ppermute x8, waiting for transfers between devices, send(): return lax.ppermute(values, ('frames', 'rows'), where)  2.12 us
  transfers between devices with their start and end apart: 8, of which 3 were waited for; matrix products, arithmetic and copies ran while one was open for 0% of the time, Pallas kernels for 12%

profile of v7, /device:TPU:1, one launch (start us, length us, event | category | flops | bytes accessed | tf_op | source)
XLA Modules:
  0.0 63.9 jit_solution(12560000915424284847)
XLA Ops:
  0.6 0.0 copy-start
  0.6 1.2 %copy-done = bf16[8,4,64,256]{3,2,1,0:T(8,128)(2,1)S(1)} copy-done((bf16[8,4,64,256]{3,2,1,0:T(8,128)(2,1)S(1)}, bf16[8,4,64,256]{3,2,1,0:T(8,128)(2,1)}, u32[]{:S(2)}) %copy-start) | copy-done | bytes 1048600
  1.9 0.0 copy-start.1
  1.9 0.0 copy-start.2
  1.9 0.0 copy-start.4
  1.9 0.0 copy-start.5
  1.9 3.6 %collective-permute-start = (bf16[4,4,64,256]{3,2,1,0:T(8,128)(2,1)S(1)}, bf16[4,4,64,256]{3,2,1,0:T(8,128)(2,1)S(1)}, u32[]{:S(2)}, u32[]{:S(2)}) collective-permute-start(bf16[4,4,64,256]{3,2,1,0:T(8,128)(2,1)S(1)} %past.1), channel_id=1, source_target_pairs={{0,4},{1,5},{2,6},{3,7},{4,8},{5,9},{6,10},{7,11},{8,12},{9,13},{1... | collective-permute-start | bytes 1572872 | tf_op jit(solution)/shard_map/ppermute | solution.py:425
  5.6 0.9 %stats_one.1 = f32[128,128]{1,0:T(8,128)S(1)} custom-call(bf16[8,4,64,256]{3,2,1,0:T(8,128)(2,1)S(1)} %copy-done), custom_call_target="tpu_custom_call" | custom-call | flops 10000000000 | bytes 1000000 | tf_op jit(solution)/shard_map/stats_one/pallas_call | solution.py:442
  6.5 19.2 %all_to_all.23 = f32[128,1,128]{2,1,0:T(1,128)S(1)} all-to-all(f32[128,1,128]{2,1,0:T(1,128)S(1)} %bitcast.17), channel_id=1, replica_groups=mesh['frames'=32,'rows'=4] {'frames','rows'}, dimensions={0} | all-to-all | bytes 131072 | tf_op jit(solution)/shard_map/all_to_all | solution.py:429
  25.7 0.0 collective-permute-done.past_ref
  25.7 0.1 edges.1
  25.7 0.8 %collective-permute-start.1 = (bf16[12,64,256]{2,1,0:T(8,128)(2,1)S(1)}, bf16[12,64,256]{2,1,0:T(8,128)(2,1)S(1)}, u32[]{:S(2)}, u32[]{:S(2)}) collective-permute-start(bf16[12,64,256]{2,1,0:T(8,128)(2,1)S(1)} %get-tuple-element.21), channel_id=1, source_target_pairs={{0,1},{1,0},{2,3},{3,2},{4,5},{5,4},{6,7},{7,6},{8,9},{9,8},{10,11... | collective-permute-start | bytes 1179656 | tf_op jit(solution)/shard_map/ppermute | solution.py:425
  26.6 0.9 %collective-permute-start.2 = (bf16[12,64,256]{2,1,0:T(8,128)(2,1)S(1)}, bf16[12,64,256]{2,1,0:T(8,128)(2,1)S(1)}, u32[]{:S(2)}, u32[]{:S(2)}) collective-permute-start(bf16[12,64,256]{2,1,0:T(8,128)(2,1)S(1)} %get-tuple-element.22), channel_id=1, source_target_pairs={{1,2},{2,1},{5,6},{6,5},{9,10},{10,9},{13,14},{14,13},{17,18},{18,... | collective-permute-start | bytes 1179656 | tf_op jit(solution)/shard_map/ppermute | solution.py:425
  27.5 0.0 copy-done.1
  27.5 0.0 copy-done.2
  27.5 0.0 copy-done.4
  27.5 0.0 copy-done.5
  27.5 5.7 %conv_inner.1 = (bf16[10,2,64,256]{3,2,1,0:T(8,128)(2,1)S(1)}, f32[10,2,64,256]{3,2,1,0:T(8,128)S(1)}, bf16[12,2,64,256]{3,2,1,0:T(8,128)(2,1)S(1)}, f32[8,256]{1,0:T(8,128)S(1)}) custom-call(bf16[8,4,64,256]{3,2,1,0:T(8,128)(2,1)S(1)} %copy-done.1, bf16[4,4,64,256]{3,2,1,0:T(8,128)(2,1)S(1)} %collective-permute-done.past_ref, f32[128,128]{1,0:T(8,128)S(1)} %bitcast.13, ...), custom_call_target="tpu_custom_call" | custom-call | flops 6039797760 | bytes 1000000 | tf_op jit(solution)/shard_map/conv_inner/pallas_call | solution.py:442
  33.2 0.0 collective-permute-done.1.near_ref
  33.2 0.8 %collective-permute-done.2.far_ref = bf16[12,64,256]{2,1,0:T(8,128)(2,1)S(1)} collective-permute-done((bf16[12,64,256]{2,1,0:T(8,128)(2,1)S(1)}, bf16[12,64,256]{2,1,0:T(8,128)(2,1)S(1)}, u32[]{:S(2)}, u32[]{:S(2)}) %collective-permute-start.2) | collective-permute-done | bytes 393248 | tf_op jit(solution)/shard_map/ppermute | solution.py:425
  34.0 0.0 copy-start.3
  34.0 0.0 copy-start.6
  34.0 0.0 copy-start.7
  34.0 0.0 copy-start.8
  34.0 2.6 %conv_outer.1 = (f32[128,128]{1,0:T(8,128)S(1)}, bf16[10,64,256]{2,1,0:T(8,128)(2,1)S(1)}, bf16[10,64,256]{2,1,0:T(8,128)(2,1)S(1)}) custom-call(bf16[12,64,256]{2,1,0:T(8,128)(2,1)S(1)} %collective-permute-done.1.near_ref, bf16[12,64,256]{2,1,0:T(8,128)(2,1)S(1)} %collective-permute-done.2.far_ref, f32[128,128]{1,0:T(8,128)S(1)} %bitcast.14, ...), custom_call_target="tpu_custom_call" | custom-call | flops 2415919104 | bytes 1000000 | tf_op jit(solution)/shard_map/conv_outer/pallas_call | solution.py:442
  36.7 0.5 collective-permute-start.3
  37.1 0.4 collective-permute-start.4
  37.5 14.3 %all_to_all.24 = f32[128,1,128]{2,1,0:T(1,128)S(1)} all-to-all(f32[128,1,128]{2,1,0:T(1,128)S(1)} %bitcast.15), channel_id=1, replica_groups=mesh['frames'=32,'rows'=4] {'frames','rows'}, dimensions={0} | all-to-all | bytes 131072 | tf_op jit(solution)/shard_map/all_to_all | solution.py:429
  51.8 0.0 collective-permute-done.3.near_ref
  51.8 0.0 collective-permute-done.4.far_ref
  51.9 0.0 copy-done.3
  51.9 0.0 copy-done.6
  51.9 0.0 copy-done.7
  51.9 0.0 copy-done.8
  51.9 6.3 %conv_two.1 = (bf16[4,2,8,256]{3,2,1,0:T(8,128)(2,1)S(1)}, bf16[4,2,8,256]{3,2,1,0:T(8,128)(2,1)S(1)}, bf16[4,2,8,256]{3,2,1,0:T(8,128)(2,1)S(1)}, bf16[4,2,8,25...) custom-call(bf16[10,2,64,256]{3,2,1,0:T(8,128)(2,1)S(1)} %get-tuple-element.20.hidden_ref, ...), custom_call_target="tpu_custom_call" | custom-call | flops 4831838208 | bytes 1000000 | tf_op jit(solution)/shard_map/conv_two/pallas_call | solution.py:442
  58.2 0.8 %collective-permute-start.5 = (bf16[4,2,8,256]{3,2,1,0:T(8,128)(2,1)S(1)}, bf16[4,2,8,256]{3,2,1,0:T(8,128)(2,1)S(1)}, u32[]{:S(2)}, u32[]{:S(2)}) collective-permute-start(bf16[4,2,8,256]{3,2,1,0:T(8,128)(2,1)S(1)} %get-tuple-element.30), channel_id=1, source_target_pairs={{0,1},{1,0},{2,3},{3,2},{4,5},{5,4},{6,7},{7,6},{8,9},{9,8},{10,11... | collective-permute-start | bytes 98312 | tf_op jit(solution)/shard_map/ppermute | solution.py:425
  59.0 0.3 collective-permute-start.6
  59.3 1.4 %collective-permute-start.7 = (bf16[4,2,8,256]{3,2,1,0:T(8,128)(2,1)S(1)}, bf16[4,2,8,256]{3,2,1,0:T(8,128)(2,1)S(1)}, u32[]{:S(2)}, u32[]{:S(2)}) collective-permute-start(bf16[4,2,8,256]{3,2,1,0:T(8,128)(2,1)S(1)} %get-tuple-element.32), channel_id=1, source_target_pairs={{0,3},{1,2},{2,1},{3,0},{4,7},{5,6},{6,5},{7,4},{8,11},{9,10},{10,... | collective-permute-start | bytes 98312 | tf_op jit(solution)/shard_map/ppermute | solution.py:425
  60.8 1.0 %high_bands.1 = bf16[7,4,2,32,256]{4,3,2,1,0:T(8,128)(2,1)} custom-call(bf16[7,4,2,32,256]{4,3,2,1,0:T(8,128)(2,1)S(1)} %get-tuple-element.33.held_ref), custom_call_target="tpu_custom_call" | custom-call | flops 1000000000 | bytes 1000000 | tf_op jit(solution)/shard_map/high_bands/pallas_call | solution.py:442
  61.7 0.0 collective-permute-done.5.refs_1_
  61.7 0.1 collective-permute-done.6.refs_2_
  61.8 1.2 %collective-permute-done.7.refs_3_ = bf16[4,2,8,256]{3,2,1,0:T(8,128)(2,1)S(1)} collective-permute-done((bf16[4,2,8,256]{3,2,1,0:T(8,128)(2,1)S(1)}, bf16[4,2,8,256]{3,2,1,0:T(8,128)(2,1)S(1)}, u32[]{:S(2)}, u32[]{:S(2)}) %collective-permute-start.7) | collective-permute-done | bytes 32800 | tf_op jit(solution)/shard_map/ppermute | solution.py:425
  63.1 0.7 %low_rows.1 = bf16[4,8,8,256]{3,2,1,0:T(8,128)(2,1)} custom-call(bf16[4,2,8,256]{3,2,1,0:T(8,128)(2,1)S(1)} %get-tuple-element.29.refs_0_, bf16[4,2,8,256]{3,2,1,0:T(8,128)(2,1)S(1)} %collective-permute-done.5.refs_1_, bf16[4,2,8,256]{3,2,1,0:T(8,128)(2,1)S(1)} %collective-permute-done.6.refs_2_, bf16[4,2,8,256]{3,2,1,0:T(8,128)(2,1)S(1)} %collective-permute-done.7.refs_3_), custom_call_target="tpu_custom_call" | custom-call | tf_op jit(solution)/shard_map/low_rows/pallas_call | solution.py:442
  (1 shorter events, 0.0 us)
Async XLA Ops:
  0.6 1.2 %copy-start = (bf16[8,4,64,256]{3,2,1,0:T(8,128)(2,1)S(1)}, bf16[8,4,64,256]{3,2,1,0:T(8,128)(2,1)}, u32[]{:S(2)}) copy-start(bf16[8,4,64,256]{3,2,1,0:T(8,128)(2,1)} %source_ref.1) | copy-start | bytes 3145732
  1.9 25.6 %copy-start.1 = (bf16[8,4,64,256]{3,2,1,0:T(8,128)(2,1)S(1)}, bf16[8,4,64,256]{3,2,1,0:T(8,128)(2,1)}, u32[]{:S(2)}) copy-start(bf16[8,4,64,256]{3,2,1,0:T(8,128)(2,1)} %source_ref.1) | copy-start | bytes 3145732
  1.9 25.6 %copy-start.2 = (bf16[3,3,3,256,256]{4,3,2,1,0:T(8,128)(2,1)S(1)}, bf16[3,3,3,256,256]{4,3,2,1,0:T(8,128)(2,1)}, u32[]{:S(2)}) copy-start(bf16[3,3,3,256,256]{4,3,2,1,0:T(8,128)(2,1)} %kernel_ref.4) | copy-start | bytes 10616836
  1.9 25.6 %copy-start.4 = (f32[256]{0:T(256)S(1)}, f32[256]{0:T(256)}, u32[]{:S(2)}) copy-start(f32[256]{0:T(256)} %param.10) | copy-start | bytes 3076
  1.9 25.6 %copy-start.5 = (f32[256]{0:T(256)S(1)}, f32[256]{0:T(256)}, u32[]{:S(2)}) copy-start(f32[256]{0:T(256)} %param.11) | copy-start | bytes 3076
  1.9 23.7 %collective-permute-start = (bf16[4,4,64,256]{3,2,1,0:T(8,128)(2,1)S(1)}, bf16[4,4,64,256]{3,2,1,0:T(8,128)(2,1)S(1)}, u32[]{:S(2)}, u32[]{:S(2)}) collective-permute-start(bf16[4,4,64,256]{3,2,1,0:T(8,128)(2,1)S(1)} %past.1), channel_id=1, source_target_pairs={{0,4},{1,5},{2,6},{3,7},{4,8},{5,9},{6,10},{7,11},{8,12},{9,13},{1... | collective-permute-start | bytes 1572872 | tf_op jit(solution)/shard_map/ppermute | solution.py:425
  25.7 7.5 %collective-permute-start.1 = (bf16[12,64,256]{2,1,0:T(8,128)(2,1)S(1)}, bf16[12,64,256]{2,1,0:T(8,128)(2,1)S(1)}, u32[]{:S(2)}, u32[]{:S(2)}) collective-permute-start(bf16[12,64,256]{2,1,0:T(8,128)(2,1)S(1)} %get-tuple-element.21), channel_id=1, source_target_pairs={{0,1},{1,0},{2,3},{3,2},{4,5},{5,4},{6,7},{7,6},{8,9},{9,8},{10,11... | collective-permute-start | bytes 1179656 | tf_op jit(solution)/shard_map/ppermute | solution.py:425
  26.6 7.5 %collective-permute-start.2 = (bf16[12,64,256]{2,1,0:T(8,128)(2,1)S(1)}, bf16[12,64,256]{2,1,0:T(8,128)(2,1)S(1)}, u32[]{:S(2)}, u32[]{:S(2)}) collective-permute-start(bf16[12,64,256]{2,1,0:T(8,128)(2,1)S(1)} %get-tuple-element.22), channel_id=1, source_target_pairs={{1,2},{2,1},{5,6},{6,5},{9,10},{10,9},{13,14},{14,13},{17,18},{18,... | collective-permute-start | bytes 1179656 | tf_op jit(solution)/shard_map/ppermute | solution.py:425
  34.0 17.8 %copy-start.3 = (bf16[3,3,3,256,256]{4,3,2,1,0:T(8,128)(2,1)S(1)}, bf16[3,3,3,256,256]{4,3,2,1,0:T(8,128)(2,1)}, u32[]{:S(2)}) copy-start(bf16[3,3,3,256,256]{4,3,2,1,0:T(8,128)(2,1)} %kernel_ref.5) | copy-start | bytes 10616836
  34.0 17.8 %copy-start.6 = (f32[256]{0:T(256)S(1)}, f32[256]{0:T(256)}, u32[]{:S(2)}) copy-start(f32[256]{0:T(256)} %param.13) | copy-start | bytes 3076
  34.0 17.8 %copy-start.7 = (f32[256]{0:T(256)S(1)}, f32[256]{0:T(256)}, u32[]{:S(2)}) copy-start(f32[256]{0:T(256)} %param.14) | copy-start | bytes 3076
  34.0 17.8 %copy-start.8 = (f32[256]{0:T(256)S(1)}, f32[256]{0:T(256)}, u32[]{:S(2)}) copy-start(f32[256]{0:T(256)} %param.15) | copy-start | bytes 3076
  36.7 15.2 %collective-permute-start.3 = (bf16[10,64,256]{2,1,0:T(8,128)(2,1)S(1)}, bf16[10,64,256]{2,1,0:T(8,128)(2,1)S(1)}, u32[]{:S(2)}, u32[]{:S(2)}) collective-permute-start(bf16[10,64,256]{2,1,0:T(8,128)(2,1)S(1)} %get-tuple-element.26.own_near_ref), channel_id=1, source_target_pairs={{0,1},{1,0},{2,3},{3,2},{4,5},{5,4},{6,7},{7,6},{8,9},{9,8},{10,11... | collective-permute-start | bytes 983048 | tf_op jit(solution)/shard_map/ppermute | solution.py:425
  37.1 14.7 %collective-permute-start.4 = (bf16[10,64,256]{2,1,0:T(8,128)(2,1)S(1)}, bf16[10,64,256]{2,1,0:T(8,128)(2,1)S(1)}, u32[]{:S(2)}, u32[]{:S(2)}) collective-permute-start(bf16[10,64,256]{2,1,0:T(8,128)(2,1)S(1)} %get-tuple-element.27.own_far_ref), channel_id=1, source_target_pairs={{1,2},{2,1},{5,6},{6,5},{9,10},{10,9},{13,14},{14,13},{17,18},{18,... | collective-permute-start | bytes 983048 | tf_op jit(solution)/shard_map/ppermute | solution.py:425
  58.2 3.5 %collective-permute-start.5 = (bf16[4,2,8,256]{3,2,1,0:T(8,128)(2,1)S(1)}, bf16[4,2,8,256]{3,2,1,0:T(8,128)(2,1)S(1)}, u32[]{:S(2)}, u32[]{:S(2)}) collective-permute-start(bf16[4,2,8,256]{3,2,1,0:T(8,128)(2,1)S(1)} %get-tuple-element.30), channel_id=1, source_target_pairs={{0,1},{1,0},{2,3},{3,2},{4,5},{5,4},{6,7},{7,6},{8,9},{9,8},{10,11... | collective-permute-start | bytes 98312 | tf_op jit(solution)/shard_map/ppermute | solution.py:425
  59.0 2.8 %collective-permute-start.6 = (bf16[4,2,8,256]{3,2,1,0:T(8,128)(2,1)S(1)}, bf16[4,2,8,256]{3,2,1,0:T(8,128)(2,1)S(1)}, u32[]{:S(2)}, u32[]{:S(2)}) collective-permute-start(bf16[4,2,8,256]{3,2,1,0:T(8,128)(2,1)S(1)} %get-tuple-element.31), channel_id=1, source_target_pairs={{0,2},{1,3},{2,0},{3,1},{4,6},{5,7},{6,4},{7,5},{8,10},{9,11},{10,... | collective-permute-start | bytes 98312 | tf_op jit(solution)/shard_map/ppermute | solution.py:425
  59.3 3.7 %collective-permute-start.7 = (bf16[4,2,8,256]{3,2,1,0:T(8,128)(2,1)S(1)}, bf16[4,2,8,256]{3,2,1,0:T(8,128)(2,1)S(1)}, u32[]{:S(2)}, u32[]{:S(2)}) collective-permute-start(bf16[4,2,8,256]{3,2,1,0:T(8,128)(2,1)S(1)} %get-tuple-element.32), channel_id=1, source_target_pairs={{0,3},{1,2},{2,1},{3,0},{4,7},{5,6},{6,5},{7,4},{8,11},{9,10},{10,... | collective-permute-start | bytes 98312 | tf_op jit(solution)/shard_map/ppermute | solution.py:425

commit v8 on v7

--- a/solution.py
+++ b/solution.py
@@ -11,7 +11,8 @@
 EPS = 1e-06
 LANES = 128
 LAGS = 4
-STEP = 2
+OUTER_STEP = 2
+INNER_STEPS, SECOND_STEPS = (4, 2, 4), (2, 2, 2, 2)
 LAG_COLS = (1, 0, 2)
 VMEM = pl.BlockSpec(memory_space=pltpu.VMEM)
 HBM = pl.BlockSpec(memory_space=pltpu.HBM)
@@ -41,9 +42,7 @@
     return values.astype(jnp.float32).reshape(-1, 8, values.shape[-1])
 
 
-def put_stats(out_ref, total, squares, centre, count):
-    mean = channel_group_sums(total) / count
-    away = mean - centre
+def put_stats(out_ref, mean, away, squares, count):
     spread = channel_group_sums(squares) - count * (away * away)
     kind = jnp.bitwise_and(lax.broadcasted_iota(jnp.int32, (1, LANES), 1), 7)
     row = jnp.zeros((1, LANES), jnp.float32)
@@ -197,18 +196,15 @@
 def stats_kernel(values_ref, out_ref):
     frames, rows, cols, chans = values_ref.shape
     count = float(frames * rows * cols * (chans // GROUPS))
-    zero = jnp.zeros((8, chans), jnp.float32)
-
-    total = zero
-    for index in range(frames):
-        total = total + jnp.sum(folded(values_ref[index]), axis=0)
-    centre = channel_group_sums(total) / count
-
-    squares = zero
+    total = squares = jnp.zeros((8, chans), jnp.float32)
+    sample = jnp.sum(folded(values_ref[0, 0]), axis=0)
+    centre = channel_group_sums(sample) / (cols * (chans // GROUPS))
     for index in range(frames):
         away = folded(values_ref[index]) - centre
+        total = total + jnp.sum(away, axis=0)
         squares = squares + jnp.sum(away * away, axis=0)
-    put_stats(out_ref, total, squares, centre, count)
+    away = channel_group_sums(total) / count
+    put_stats(out_ref, centre + away, away, squares, count)
 
 
 def group_count(frames, rows, cols, chans):
@@ -222,6 +218,7 @@
     frames, rows, cols, chans = own_ref.shape
     terms = norm_terms(stats_ref, gain_ref, offset_ref, group_count(*own_ref.shape))
     total = jnp.zeros((8, chans), jnp.float32)
+    start, steps = 0, list(INNER_STEPS)
     for frame in range(frames + LAGS):
         body, valid = own_ref.at[frame - LAGS], None
         if frame < LAGS:
@@ -233,24 +230,24 @@
                 wide_ref[frame, index, pair * cols : (pair + 1) * cols] = value.astype(jnp.bfloat16)
             side_ref[frame, pair] = (lines[pair] - lines[pair + 2]).astype(jnp.bfloat16)
             middle_ref[frame, pair] = lines[pair + 1].astype(jnp.bfloat16)
-        if frame < STEP + 1 or (frame - 1) % STEP:
+        if not steps or frame < start + steps[0] + 1:
             continue
-        start = frame - 1 - STEP
+        count = steps.pop(0)
         sums = [None, None]
         sides = [None, None]
         for lag_col in LAG_COLS:
             if start == 0:
                 mix_taps(kernel_ref, mixed_ref, lag_col)
             taps = [[mixed_ref[at, lag, lag_col] for lag in range(3)] for at in range(2)]
-            plus, minus = (product(wide_ref, start, STEP, at, taps[at]) for at in range(2))
+            plus, minus = (product(wide_ref, start, count, at, taps[at]) for at in range(2))
             for at, part in enumerate((plus + minus, plus - minus)):
                 part = shifted(part, cols, lag_col)
                 sums[at] = part if sums[at] is None else sums[at] + part
             for at in range(2):
                 taps = [kernel_ref[lag, 2 - 2 * at, lag_col] for lag in range(3)]
-                part = shifted(product(side_ref, start, STEP, at, taps), cols, lag_col)
+                part = shifted(product(side_ref, start, count, at, taps), cols, lag_col)
                 sides[at] = part if sides[at] is None else sides[at] + part
-        for at in range(STEP):
+        for at in range(count):
             place = start + at
             partial_ref[place, 0] = sums[0][2 * at]
             partial_ref[place, 1] = sums[1][2 * at + 1]
@@ -261,6 +258,7 @@
                 hidden_ref[place, row] = hidden
                 if place >= 2:
                     total = total + jnp.sum(folded(hidden), axis=0)
+        start += count
     sums_ref[...] = total
 
 
@@ -294,16 +292,16 @@
         side_ref[frame, 1] = (middle[1] - lower).astype(jnp.bfloat16)
         if 2 <= frame < count_frames:
             squares = squares + square(hidden_ref[frame])
-        if frame < STEP + 1 or (frame - 1) % STEP:
+        if frame < OUTER_STEP + 1 or (frame - 1) % OUTER_STEP:
             continue
-        start = frame - 1 - STEP
+        start = frame - 1 - OUTER_STEP
         sides = [None, None]
         for lag_col in LAG_COLS:
             for at in range(2):
                 taps = [kernel_ref[lag, 2 * at, lag_col] for lag in range(3)]
-                part = shifted(product(side_ref, start, STEP, at, taps), cols, lag_col)
+                part = shifted(product(side_ref, start, OUTER_STEP, at, taps), cols, lag_col)
                 sides[at] = part if sides[at] is None else sides[at] + part
-        for at in range(STEP):
+        for at in range(OUTER_STEP):
             place = start + at
             edges = [
                 (partial_ref[place, 0] + sides[0][at]).astype(jnp.bfloat16),
@@ -315,7 +313,8 @@
                 for edge in edges:
                     squares = squares + square(edge)
                     sums = sums + jnp.sum(folded(edge), axis=0)
-    put_stats(out_stats_ref, sums, squares, centre, count)
+    mean = channel_group_sums(sums) / count
+    put_stats(out_stats_ref, mean, mean - centre, squares, count)
 
 
 def columns_apart(line, pair_ref):
@@ -340,6 +339,7 @@
     factor = 0.5**1.5
     bands = len(low_refs)
     width = cols // 2 // bands
+    done, steps = [], list(SECOND_STEPS)
     for frame in range(frames + 2):
         near, far = own_near_ref[frame], own_far_ref[frame]
         body = (
@@ -347,40 +347,40 @@
             jnp.where(window.odd, far, near),
         )
         window.put(frame, body, near_ref[frame], far_ref[frame], has_past() if frame < 2 else None)
-        if frame < 3 or frame % 2 == 0:
+        start = len(done)
+        if not steps or frame < start + steps[0] + 1:
             continue
-        start = frame - 3
-        index = start // 2
-        conv = window.conv(start, 2, kernel_ref, mixed_ref, mix=start == 0)
-        summed = [
-            [
-                source_ref[start + at, row].astype(jnp.float32) + conv[at][row] + bias_ref[...]
-                for row in range(rows)
+        done += window.conv(start, steps.pop(0), kernel_ref, mixed_ref, mix=start == 0)
+        for index in range(start // 2, len(done) // 2):
+            summed = [
+                [
+                    source_ref[own, row].astype(jnp.float32) + done[own][row] + bias_ref[...]
+                    for row in range(rows)
+                ]
+                for own in (2 * index, 2 * index + 1)
             ]
-            for at in range(2)
-        ]
-        for time_band in range(2):
-            mixed = [
-                before - after if time_band else before + after
-                for before, after in zip(*summed, strict=True)
-            ]
-            for pair in range(rows // 2):
-                upper, lower = mixed[2 * pair], mixed[2 * pair + 1]
-                for row_band in range(2):
-                    line = (upper - lower if row_band else upper + lower) * factor
-                    slot = ((index * 2 + time_band) * (rows // 2) + pair) * 2 + row_band
-                    even, uneven = columns_apart(line, pair_ref.at[slot % pair_ref.shape[0]])
-                    for col_band in range(2):
-                        value = even - uneven if col_band else even + uneven
-                        value = value.astype(jnp.bfloat16)
-                        band = 4 * time_band + 2 * row_band + col_band
-                        if band:
-                            high_ref[band - 1, index, pair] = value
-                        else:
-                            for target in range(bands):
-                                low_ref[target, index, pair] = value[
-                                    target * width : (target + 1) * width
-                                ]
+            for time_band in range(2):
+                mixed = [
+                    before - after if time_band else before + after
+                    for before, after in zip(*summed, strict=True)
+                ]
+                for pair in range(rows // 2):
+                    upper, lower = mixed[2 * pair], mixed[2 * pair + 1]
+                    for row_band in range(2):
+                        line = (upper - lower if row_band else upper + lower) * factor
+                        slot = ((index * 2 + time_band) * (rows // 2) + pair) * 2 + row_band
+                        even, uneven = columns_apart(line, pair_ref.at[slot % pair_ref.shape[0]])
+                        for col_band in range(2):
+                            value = even - uneven if col_band else even + uneven
+                            value = value.astype(jnp.bfloat16)
+                            band = 4 * time_band + 2 * row_band + col_band
+                            if band:
+                                high_ref[band - 1, index, pair] = value
+                            else:
+                                for target in range(bands):
+                                    low_ref[target, index, pair] = value[
+                                        target * width : (target + 1) * width
+                                    ]
     place = lax.axis_index("rows")
     for index, out_ref in enumerate(low_refs):
         out_ref[...] = low_ref[lax.bitwise_xor(place, index)]

time: 64.1 us -> 64.1 us (level)
  no operation moved by 1% of the time
where the time goes in v8:
time: 64.1 us; the launch traced here: 63.9 us
  blocking collectives  33.5 us (52%)
  Pallas kernels  17.1 us (27%)
  starting transfers between devices  8.99 us (14%)
  waiting for transfers between devices  2.12 us (3%)
  local copies, waits for them, and re-layouts  1.26 us (2%)
  between operations  0.92 us (1%)
    all_to_all x2, blocking collectives, share(): return lax.all_to_all(stats, ('frames', 'rows'), 0, 0, tiled=True)  33.5 us
    pallas_call x8, Pallas kernels, call(): pl.pallas_call(kernel, out_shape=out_shape, in_specs=spaces or [VMEM] * l...  17.1 us
    ppermute x8, starting transfers between devices, send(): return lax.ppermute(values, ('frames', 'rows'), where)  8.99 us
    ppermute x8, waiting for transfers between devices, send(): return lax.ppermute(values, ('frames', 'rows'), where)  2.12 us
  transfers between devices with their start and end apart: 8, of which 3 were waited for; matrix products, arithmetic and copies ran while one was open for 0% of the time, Pallas kernels for 12%

profile of v8, /device:TPU:1, one launch (start us, length us, event | category | flops | bytes accessed | tf_op | source)
XLA Modules:
  0.0 63.9 jit_solution(17938219171915403910)
XLA Ops:
  0.6 0.0 copy-start
  0.6 1.2 %copy-done = bf16[8,4,64,256]{3,2,1,0:T(8,128)(2,1)S(1)} copy-done((bf16[8,4,64,256]{3,2,1,0:T(8,128)(2,1)S(1)}, bf16[8,4,64,256]{3,2,1,0:T(8,128)(2,1)}, u32[]{:S(2)}) %copy-start) | copy-done | bytes 1048600
  1.9 0.0 copy-start.1
  1.9 0.0 copy-start.2
  1.9 0.0 copy-start.4
  1.9 0.0 copy-start.5
  1.9 3.6 %collective-permute-start = (bf16[4,4,64,256]{3,2,1,0:T(8,128)(2,1)S(1)}, bf16[4,4,64,256]{3,2,1,0:T(8,128)(2,1)S(1)}, u32[]{:S(2)}, u32[]{:S(2)}) collective-permute-start(bf16[4,4,64,256]{3,2,1,0:T(8,128)(2,1)S(1)} %past.1), channel_id=1, source_target_pairs={{0,4},{1,5},{2,6},{3,7},{4,8},{5,9},{6,10},{7,11},{8,12},{9,13},{1... | collective-permute-start | bytes 1572872 | tf_op jit(solution)/shard_map/ppermute | solution.py:425
  5.6 0.8 %stats_one.1 = f32[128,128]{1,0:T(8,128)S(1)} custom-call(bf16[8,4,64,256]{3,2,1,0:T(8,128)(2,1)S(1)} %copy-done), custom_call_target="tpu_custom_call" | custom-call | flops 10000000000 | bytes 1000000 | tf_op jit(solution)/shard_map/stats_one/pallas_call | solution.py:442
  6.4 19.2 %all_to_all.23 = f32[128,1,128]{2,1,0:T(1,128)S(1)} all-to-all(f32[128,1,128]{2,1,0:T(1,128)S(1)} %bitcast.17), channel_id=1, replica_groups=mesh['frames'=32,'rows'=4] {'frames','rows'}, dimensions={0} | all-to-all | bytes 131072 | tf_op jit(solution)/shard_map/all_to_all | solution.py:429
  25.6 0.0 collective-permute-done.past_ref
  25.6 0.1 edges.1
  25.6 0.8 %collective-permute-start.1 = (bf16[12,64,256]{2,1,0:T(8,128)(2,1)S(1)}, bf16[12,64,256]{2,1,0:T(8,128)(2,1)S(1)}, u32[]{:S(2)}, u32[]{:S(2)}) collective-permute-start(bf16[12,64,256]{2,1,0:T(8,128)(2,1)S(1)} %get-tuple-element.21), channel_id=1, source_target_pairs={{0,1},{1,0},{2,3},{3,2},{4,5},{5,4},{6,7},{7,6},{8,9},{9,8},{10,11... | collective-permute-start | bytes 1179656 | tf_op jit(solution)/shard_map/ppermute | solution.py:425
  26.5 1.0 %collective-permute-start.2 = (bf16[12,64,256]{2,1,0:T(8,128)(2,1)S(1)}, bf16[12,64,256]{2,1,0:T(8,128)(2,1)S(1)}, u32[]{:S(2)}, u32[]{:S(2)}) collective-permute-start(bf16[12,64,256]{2,1,0:T(8,128)(2,1)S(1)} %get-tuple-element.22), channel_id=1, source_target_pairs={{1,2},{2,1},{5,6},{6,5},{9,10},{10,9},{13,14},{14,13},{17,18},{18,... | collective-permute-start | bytes 1179656 | tf_op jit(solution)/shard_map/ppermute | solution.py:425
  27.5 0.0 copy-done.1
  27.5 0.0 copy-done.2
  27.5 0.0 copy-done.4
  27.5 0.0 copy-done.5
  27.5 5.6 %conv_inner.1 = (bf16[10,2,64,256]{3,2,1,0:T(8,128)(2,1)S(1)}, f32[10,2,64,256]{3,2,1,0:T(8,128)S(1)}, bf16[12,2,64,256]{3,2,1,0:T(8,128)(2,1)S(1)}, f32[8,256]{1,0:T(8,128)S(1)}) custom-call(bf16[8,4,64,256]{3,2,1,0:T(8,128)(2,1)S(1)} %copy-done.1, bf16[4,4,64,256]{3,2,1,0:T(8,128)(2,1)S(1)} %collective-permute-done.past_ref, f32[128,128]{1,0:T(8,128)S(1)} %bitcast.13, ...), custom_call_target="tpu_custom_call" | custom-call | flops 6039797760 | bytes 1000000 | tf_op jit(solution)/shard_map/conv_inner/pallas_call | solution.py:442
  33.1 0.0 collective-permute-done.1.near_ref
  33.1 0.8 %collective-permute-done.2.far_ref = bf16[12,64,256]{2,1,0:T(8,128)(2,1)S(1)} collective-permute-done((bf16[12,64,256]{2,1,0:T(8,128)(2,1)S(1)}, bf16[12,64,256]{2,1,0:T(8,128)(2,1)S(1)}, u32[]{:S(2)}, u32[]{:S(2)}) %collective-permute-start.2) | collective-permute-done | bytes 393248 | tf_op jit(solution)/shard_map/ppermute | solution.py:425
  34.0 0.0 copy-start.3
  34.0 0.0 copy-start.6
  34.0 0.0 copy-start.7
  34.0 0.0 copy-start.8
  34.0 2.6 %conv_outer.1 = (f32[128,128]{1,0:T(8,128)S(1)}, bf16[10,64,256]{2,1,0:T(8,128)(2,1)S(1)}, bf16[10,64,256]{2,1,0:T(8,128)(2,1)S(1)}) custom-call(bf16[12,64,256]{2,1,0:T(8,128)(2,1)S(1)} %collective-permute-done.1.near_ref, bf16[12,64,256]{2,1,0:T(8,128)(2,1)S(1)} %collective-permute-done.2.far_ref, f32[128,128]{1,0:T(8,128)S(1)} %bitcast.14, ...), custom_call_target="tpu_custom_call" | custom-call | flops 2415919104 | bytes 1000000 | tf_op jit(solution)/shard_map/conv_outer/pallas_call | solution.py:442
  36.6 0.5 collective-permute-start.3
  37.1 0.5 collective-permute-start.4
  37.5 14.3 %all_to_all.24 = f32[128,1,128]{2,1,0:T(1,128)S(1)} all-to-all(f32[128,1,128]{2,1,0:T(1,128)S(1)} %bitcast.15), channel_id=1, replica_groups=mesh['frames'=32,'rows'=4] {'frames','rows'}, dimensions={0} | all-to-all | bytes 131072 | tf_op jit(solution)/shard_map/all_to_all | solution.py:429
  51.8 0.0 collective-permute-done.3.near_ref
  51.8 0.0 collective-permute-done.4.far_ref
  51.9 0.0 copy-done.3
  51.9 0.0 copy-done.6
  51.9 0.0 copy-done.7
  51.9 0.0 copy-done.8
  51.9 6.3 %conv_two.1 = (bf16[4,2,8,256]{3,2,1,0:T(8,128)(2,1)S(1)}, bf16[4,2,8,256]{3,2,1,0:T(8,128)(2,1)S(1)}, bf16[4,2,8,256]{3,2,1,0:T(8,128)(2,1)S(1)}, bf16[4,2,8,25...) custom-call(bf16[10,2,64,256]{3,2,1,0:T(8,128)(2,1)S(1)} %get-tuple-element.20.hidden_ref, ...), custom_call_target="tpu_custom_call" | custom-call | flops 4831838208 | bytes 1000000 | tf_op jit(solution)/shard_map/conv_two/pallas_call | solution.py:442
  58.2 0.8 %collective-permute-start.5 = (bf16[4,2,8,256]{3,2,1,0:T(8,128)(2,1)S(1)}, bf16[4,2,8,256]{3,2,1,0:T(8,128)(2,1)S(1)}, u32[]{:S(2)}, u32[]{:S(2)}) collective-permute-start(bf16[4,2,8,256]{3,2,1,0:T(8,128)(2,1)S(1)} %get-tuple-element.30), channel_id=1, source_target_pairs={{0,1},{1,0},{2,3},{3,2},{4,5},{5,4},{6,7},{7,6},{8,9},{9,8},{10,11... | collective-permute-start | bytes 98312 | tf_op jit(solution)/shard_map/ppermute | solution.py:425
  59.0 0.3 collective-permute-start.6
  59.3 1.4 %collective-permute-start.7 = (bf16[4,2,8,256]{3,2,1,0:T(8,128)(2,1)S(1)}, bf16[4,2,8,256]{3,2,1,0:T(8,128)(2,1)S(1)}, u32[]{:S(2)}, u32[]{:S(2)}) collective-permute-start(bf16[4,2,8,256]{3,2,1,0:T(8,128)(2,1)S(1)} %get-tuple-element.32), channel_id=1, source_target_pairs={{0,3},{1,2},{2,1},{3,0},{4,7},{5,6},{6,5},{7,4},{8,11},{9,10},{10,... | collective-permute-start | bytes 98312 | tf_op jit(solution)/shard_map/ppermute | solution.py:425
  60.8 1.0 %high_bands.1 = bf16[7,4,2,32,256]{4,3,2,1,0:T(8,128)(2,1)} custom-call(bf16[7,4,2,32,256]{4,3,2,1,0:T(8,128)(2,1)S(1)} %get-tuple-element.33.held_ref), custom_call_target="tpu_custom_call" | custom-call | flops 1000000000 | bytes 1000000 | tf_op jit(solution)/shard_map/high_bands/pallas_call | solution.py:442
  61.7 0.0 collective-permute-done.5.refs_1_
  61.7 0.1 collective-permute-done.6.refs_2_
  61.8 1.2 %collective-permute-done.7.refs_3_ = bf16[4,2,8,256]{3,2,1,0:T(8,128)(2,1)S(1)} collective-permute-done((bf16[4,2,8,256]{3,2,1,0:T(8,128)(2,1)S(1)}, bf16[4,2,8,256]{3,2,1,0:T(8,128)(2,1)S(1)}, u32[]{:S(2)}, u32[]{:S(2)}) %collective-permute-start.7) | collective-permute-done | bytes 32800 | tf_op jit(solution)/shard_map/ppermute | solution.py:425
  63.1 0.7 %low_rows.1 = bf16[4,8,8,256]{3,2,1,0:T(8,128)(2,1)} custom-call(bf16[4,2,8,256]{3,2,1,0:T(8,128)(2,1)S(1)} %get-tuple-element.29.refs_0_, bf16[4,2,8,256]{3,2,1,0:T(8,128)(2,1)S(1)} %collective-permute-done.5.refs_1_, bf16[4,2,8,256]{3,2,1,0:T(8,128)(2,1)S(1)} %collective-permute-done.6.refs_2_, bf16[4,2,8,256]{3,2,1,0:T(8,128)(2,1)S(1)} %collective-permute-done.7.refs_3_), custom_call_target="tpu_custom_call" | custom-call | tf_op jit(solution)/shard_map/low_rows/pallas_call | solution.py:442
  (1 shorter events, 0.0 us)
Async XLA Ops:
  0.6 1.2 %copy-start = (bf16[8,4,64,256]{3,2,1,0:T(8,128)(2,1)S(1)}, bf16[8,4,64,256]{3,2,1,0:T(8,128)(2,1)}, u32[]{:S(2)}) copy-start(bf16[8,4,64,256]{3,2,1,0:T(8,128)(2,1)} %source_ref.1) | copy-start | bytes 3145732
  1.9 25.6 %copy-start.1 = (bf16[8,4,64,256]{3,2,1,0:T(8,128)(2,1)S(1)}, bf16[8,4,64,256]{3,2,1,0:T(8,128)(2,1)}, u32[]{:S(2)}) copy-start(bf16[8,4,64,256]{3,2,1,0:T(8,128)(2,1)} %source_ref.1) | copy-start | bytes 3145732
  1.9 25.6 %copy-start.2 = (bf16[3,3,3,256,256]{4,3,2,1,0:T(8,128)(2,1)S(1)}, bf16[3,3,3,256,256]{4,3,2,1,0:T(8,128)(2,1)}, u32[]{:S(2)}) copy-start(bf16[3,3,3,256,256]{4,3,2,1,0:T(8,128)(2,1)} %kernel_ref.4) | copy-start | bytes 10616836
  1.9 25.6 %copy-start.4 = (f32[256]{0:T(256)S(1)}, f32[256]{0:T(256)}, u32[]{:S(2)}) copy-start(f32[256]{0:T(256)} %param.10) | copy-start | bytes 3076
  1.9 25.6 %copy-start.5 = (f32[256]{0:T(256)S(1)}, f32[256]{0:T(256)}, u32[]{:S(2)}) copy-start(f32[256]{0:T(256)} %param.11) | copy-start | bytes 3076
  1.9 23.6 %collective-permute-start = (bf16[4,4,64,256]{3,2,1,0:T(8,128)(2,1)S(1)}, bf16[4,4,64,256]{3,2,1,0:T(8,128)(2,1)S(1)}, u32[]{:S(2)}, u32[]{:S(2)}) collective-permute-start(bf16[4,4,64,256]{3,2,1,0:T(8,128)(2,1)S(1)} %past.1), channel_id=1, source_target_pairs={{0,4},{1,5},{2,6},{3,7},{4,8},{5,9},{6,10},{7,11},{8,12},{9,13},{1... | collective-permute-start | bytes 1572872 | tf_op jit(solution)/shard_map/ppermute | solution.py:425
  25.6 7.5 %collective-permute-start.1 = (bf16[12,64,256]{2,1,0:T(8,128)(2,1)S(1)}, bf16[12,64,256]{2,1,0:T(8,128)(2,1)S(1)}, u32[]{:S(2)}, u32[]{:S(2)}) collective-permute-start(bf16[12,64,256]{2,1,0:T(8,128)(2,1)S(1)} %get-tuple-element.21), channel_id=1, source_target_pairs={{0,1},{1,0},{2,3},{3,2},{4,5},{5,4},{6,7},{7,6},{8,9},{9,8},{10,11... | collective-permute-start | bytes 1179656 | tf_op jit(solution)/shard_map/ppermute | solution.py:425
  26.5 7.5 %collective-permute-start.2 = (bf16[12,64,256]{2,1,0:T(8,128)(2,1)S(1)}, bf16[12,64,256]{2,1,0:T(8,128)(2,1)S(1)}, u32[]{:S(2)}, u32[]{:S(2)}) collective-permute-start(bf16[12,64,256]{2,1,0:T(8,128)(2,1)S(1)} %get-tuple-element.22), channel_id=1, source_target_pairs={{1,2},{2,1},{5,6},{6,5},{9,10},{10,9},{13,14},{14,13},{17,18},{18,... | collective-permute-start | bytes 1179656 | tf_op jit(solution)/shard_map/ppermute | solution.py:425
  34.0 17.9 %copy-start.3 = (bf16[3,3,3,256,256]{4,3,2,1,0:T(8,128)(2,1)S(1)}, bf16[3,3,3,256,256]{4,3,2,1,0:T(8,128)(2,1)}, u32[]{:S(2)}) copy-start(bf16[3,3,3,256,256]{4,3,2,1,0:T(8,128)(2,1)} %kernel_ref.5) | copy-start | bytes 10616836
  34.0 17.9 %copy-start.6 = (f32[256]{0:T(256)S(1)}, f32[256]{0:T(256)}, u32[]{:S(2)}) copy-start(f32[256]{0:T(256)} %param.13) | copy-start | bytes 3076
  34.0 17.9 %copy-start.7 = (f32[256]{0:T(256)S(1)}, f32[256]{0:T(256)}, u32[]{:S(2)}) copy-start(f32[256]{0:T(256)} %param.14) | copy-start | bytes 3076
  34.0 17.9 %copy-start.8 = (f32[256]{0:T(256)S(1)}, f32[256]{0:T(256)}, u32[]{:S(2)}) copy-start(f32[256]{0:T(256)} %param.15) | copy-start | bytes 3076
  36.6 15.3 %collective-permute-start.3 = (bf16[10,64,256]{2,1,0:T(8,128)(2,1)S(1)}, bf16[10,64,256]{2,1,0:T(8,128)(2,1)S(1)}, u32[]{:S(2)}, u32[]{:S(2)}) collective-permute-start(bf16[10,64,256]{2,1,0:T(8,128)(2,1)S(1)} %get-tuple-element.26.own_near_ref), channel_id=1, source_target_pairs={{0,1},{1,0},{2,3},{3,2},{4,5},{5,4},{6,7},{7,6},{8,9},{9,8},{10,11... | collective-permute-start | bytes 983048 | tf_op jit(solution)/shard_map/ppermute | solution.py:425
  37.1 14.8 %collective-permute-start.4 = (bf16[10,64,256]{2,1,0:T(8,128)(2,1)S(1)}, bf16[10,64,256]{2,1,0:T(8,128)(2,1)S(1)}, u32[]{:S(2)}, u32[]{:S(2)}) collective-permute-start(bf16[10,64,256]{2,1,0:T(8,128)(2,1)S(1)} %get-tuple-element.27.own_far_ref), channel_id=1, source_target_pairs={{1,2},{2,1},{5,6},{6,5},{9,10},{10,9},{13,14},{14,13},{17,18},{18,... | collective-permute-start | bytes 983048 | tf_op jit(solution)/shard_map/ppermute | solution.py:425
  58.2 3.5 %collective-permute-start.5 = (bf16[4,2,8,256]{3,2,1,0:T(8,128)(2,1)S(1)}, bf16[4,2,8,256]{3,2,1,0:T(8,128)(2,1)S(1)}, u32[]{:S(2)}, u32[]{:S(2)}) collective-permute-start(bf16[4,2,8,256]{3,2,1,0:T(8,128)(2,1)S(1)} %get-tuple-element.30), channel_id=1, source_target_pairs={{0,1},{1,0},{2,3},{3,2},{4,5},{5,4},{6,7},{7,6},{8,9},{9,8},{10,11... | collective-permute-start | bytes 98312 | tf_op jit(solution)/shard_map/ppermute | solution.py:425
  59.0 2.8 %collective-permute-start.6 = (bf16[4,2,8,256]{3,2,1,0:T(8,128)(2,1)S(1)}, bf16[4,2,8,256]{3,2,1,0:T(8,128)(2,1)S(1)}, u32[]{:S(2)}, u32[]{:S(2)}) collective-permute-start(bf16[4,2,8,256]{3,2,1,0:T(8,128)(2,1)S(1)} %get-tuple-element.31), channel_id=1, source_target_pairs={{0,2},{1,3},{2,0},{3,1},{4,6},{5,7},{6,4},{7,5},{8,10},{9,11},{10,... | collective-permute-start | bytes 98312 | tf_op jit(solution)/shard_map/ppermute | solution.py:425
  59.3 3.7 %collective-permute-start.7 = (bf16[4,2,8,256]{3,2,1,0:T(8,128)(2,1)S(1)}, bf16[4,2,8,256]{3,2,1,0:T(8,128)(2,1)S(1)}, u32[]{:S(2)}, u32[]{:S(2)}) collective-permute-start(bf16[4,2,8,256]{3,2,1,0:T(8,128)(2,1)S(1)} %get-tuple-element.32), channel_id=1, source_target_pairs={{0,3},{1,2},{2,1},{3,0},{4,7},{5,6},{6,5},{7,4},{8,11},{9,10},{10,... | collective-permute-start | bytes 98312 | tf_op jit(solution)/shard_map/ppermute | solution.py:425
